TPU v7x, 512 devices: a whole 4x8x8 slice. The times are simulated.
512 devices in a mesh: blk: 16 (over z_hi, x, core), group: 32 (over y, z_lo).
Axes of the slice: x: 4, y: 8, z: 8 (z_hi: 2, z_lo: 4; z = z_hi * 4 + z_lo), core: 2. Of those that a mesh axis runs over, the one named last changes fastest.
Arguments:
- images: bfloat16 [196608, 768], P(('blk', 'group')), may hold values from -8 to 8
- texts: bfloat16 [196608, 768], P(('blk', 'group')), may hold values from -8 to 8
- logit_scale: float32 [1], replicated, may hold values from 5 to 12
- logit_bias: float32 [1], replicated, may hold values from -3 to -1
Outputs:
- image_grad: float32 [196608, 768], P(('blk', 'group'))
- text_grad: float32 [196608, 768], P(('blk', 'group'))
All inputs are finite; a program needn't handle non-finite values.
Results may differ from a plain program's by a relative error of at most 0.0041.
Values may be sent and summed in bfloat16 or wider, within the bound.
No kernel may reach another device: no remote copies, remote signals or barrier semaphores. Data moves between devices by JAX's collectives and lax.ppermute only.
A program may use at most 64 MiB of HBM per device.

v0:
```python
import jax
import jax.numpy as jnp
from jax import lax
from jax.sharding import PartitionSpec as P

STEPS = 4


epsilon = 1e-06


def partner_2(shard, axis, bit):
    return lax.ppermute(shard, axis, [(i, i ^ 1 << bit) for i in range(lax.axis_size(axis))])


def from_behind(shard, axis, by):
    size = lax.axis_size(axis)
    return lax.ppermute(shard, axis, [(i, (i + by) % size) for i in range(size)])


def normalize(values):
    full = values.astype(jnp.float32)
    inverse = lax.rsqrt(jnp.sum(full * full, axis=-1, keepdims=True) + epsilon)
    return (full * inverse, inverse)


def project(grad, unit, inverse):
    return (grad - unit * jnp.sum(unit * grad, axis=-1, keepdims=True)) * inverse


def on_device(images, texts, logit_scale, logit_bias):
    scale_value = logit_scale[0]
    bias_value = logit_bias[0]
    image_unit, image_inv = normalize(images)
    text_unit, text_inv = normalize(texts)
    image_hat = image_unit.astype(jnp.bfloat16)
    text_hat = text_unit.astype(jnp.bfloat16)
    rows = images.shape[0]
    diagonal_mask = jnp.eye(rows, dtype=bool)
    own_signs = jnp.where(diagonal_mask, 1.0, -1.0).astype(jnp.float32)

    def slopes_for(left, right, positive):
        logits = (
            scale_value
            * lax.dot_general(
                left, right, (((1,), (1,)), ((), ())), preferred_element_type=jnp.float32
            )
            + bias_value
        )
        if positive:
            return (scale_value * own_signs * (jax.nn.sigmoid(own_signs * logits) - 1.0)).astype(
                jnp.bfloat16
            )
        return (scale_value * -1.0 * (jax.nn.sigmoid(-logits) - 1.0)).astype(jnp.bfloat16)

    def text_term(slopes):
        return lax.dot_general(
            slopes, image_hat, (((0,), (0,)), ((), ())), preferred_element_type=jnp.float32
        )

    partner = partner_2(text_hat, "group", 0)
    blocks = (text_hat, partner)
    image_sum = jnp.zeros(images.shape, jnp.float32)
    zeros_text = jnp.zeros(texts.shape, jnp.float32)
    pending = (zeros_text, zeros_text)
    for step in range(STEPS):
        if step > 0:
            blocks = from_behind((blocks[0], blocks[1]), "blk", 1)
        own_slopes = slopes_for(image_hat, blocks[0], step == 0)
        partner_slopes = slopes_for(image_hat, blocks[1], False)
        image_sum = image_sum + jnp.dot(own_slopes, blocks[0], preferred_element_type=jnp.float32)
        image_sum = image_sum + jnp.dot(
            partner_slopes, blocks[1], preferred_element_type=jnp.float32
        )
        terms = (text_term(own_slopes), text_term(partner_slopes))
        if step > 0:
            pending = from_behind((pending[0], pending[1]), "blk", 1)
        pending = (pending[0] + terms[0], pending[1] + terms[1])
    pending = from_behind((pending[0], pending[1]), "blk", -(STEPS - 1))
    returned = partner_2(pending[1], "group", 0)
    text_sum = pending[0] + returned
    image_grad = project(image_sum, image_unit, image_inv)
    text_grad = project(text_sum, text_unit, text_inv)
    return (image_grad, text_grad)


def solution(mesh):
    return jax.shard_map(
        on_device,
        mesh=mesh,
        in_specs=(P(("blk", "group"), None), P(("blk", "group"), None), P(), P()),
        out_specs=(P(("blk", "group"), None), P(("blk", "group"), None)),
        check_vma=False,
    )
```

profile of v0, /device:TPU:184, one launch (start us, length us, event | category | flops | bytes accessed | tf_op | source)
XLA Modules:
  0.0 344.5 jit_solution(1360714273979877626)
XLA Ops:
  3.2 4.3 %collective-permute-start = (bf16[384,768]{1,0:T(8,128)(2,1)S(1)}, bf16[384,768]{1,0:T(8,128)(2,1)S(1)}, u32[]{:S(2)}, u32[]{:S(2)}) collective-permute-start(bf16[384,768]{1,0:T(8,128)(2,1)S(1)} %fusion.2), channel_id=1, source_target_pairs={{0,1},{1,0},{2,3},{3,2},{4,5},{5,4},{6,7},{7,6},{8,9},{9,8},{10,11... | collective-permute-start | bytes 1769480 | tf_op jit(solution)/shard_map/ppermute | solution.py:13
  9.0 11.8 %collective-permute-done = bf16[384,768]{1,0:T(8,128)(2,1)S(1)} collective-permute-done((bf16[384,768]{1,0:T(8,128)(2,1)S(1)}, bf16[384,768]{1,0:T(8,128)(2,1)S(1)}, u32[]{:S(2)}, u32[]{:S(2)}) %collective-permute-start) | collective-permute-done | bytes 589856 | tf_op jit(solution)/shard_map/ppermute | solution.py:13
  22.0 1.9 collective-permute-start.11
  23.9 3.5 %collective-permute-start.2 = (bf16[384,768]{1,0:T(8,128)(2,1)S(1)}, bf16[384,768]{1,0:T(8,128)(2,1)S(1)}, u32[]{:S(2)}, u32[]{:S(2)}) collective-permute-start(bf16[384,768]{1,0:T(8,128)(2,1)S(1)} %collective-permute-done), channel_id=1, source_target_pairs={{0,32},{32,64},{64,96},{96,128},{128,160},{160,192},{192,224},{224... | collective-permute-start | bytes 1769480 | tf_op jit(solution)/shard_map/ppermute | solution.py:18
  28.6 1.9 collective-permute-start.7
  30.6 3.5 %collective-permute-start.1 = (bf16[384,768]{1,0:T(8,128)(2,1)S(1)}, bf16[384,768]{1,0:T(8,128)(2,1)S(1)}, u32[]{:S(2)}, u32[]{:S(2)}) collective-permute-start(bf16[384,768]{1,0:T(8,128)(2,1)S(1)} %fusion.2), channel_id=1, source_target_pairs={{0,32},{32,64},{64,96},{96,128},{128,160},{160,192},{192,224},{224... | collective-permute-start | bytes 1769480 | tf_op jit(solution)/shard_map/ppermute | solution.py:18
  34.1 140.0 %collective-permute-done.2 = bf16[384,768]{1,0:T(8,128)(2,1)S(1)} collective-permute-done((bf16[384,768]{1,0:T(8,128)(2,1)S(1)}, bf16[384,768]{1,0:T(8,128)(2,1)S(1)}, u32[]{:S(2)}, u32[]{:S(2)}) %collective-permute-start.2) | collective-permute-done | bytes 589856 | tf_op jit(solution)/shard_map/ppermute | solution.py:18
  177.2 1.9 collective-permute-start.12
  179.6 13.4 %collective-permute-done.1 = bf16[384,768]{1,0:T(8,128)(2,1)S(1)} collective-permute-done((bf16[384,768]{1,0:T(8,128)(2,1)S(1)}, bf16[384,768]{1,0:T(8,128)(2,1)S(1)}, u32[]{:S(2)}, u32[]{:S(2)}) %collective-permute-start.1) | collective-permute-done | bytes 589856 | tf_op jit(solution)/shard_map/ppermute | solution.py:18
  196.1 1.9 collective-permute-start.8
  202.4 9.5 %collective-permute-done.12 = f32[384,768]{1,0:T(8,128)S(1)} collective-permute-done((f32[384,768]{1,0:T(8,128)S(1)}, f32[384,768]{1,0:T(8,128)S(1)}, u32[]{:S(2)}, u32[]{:S(2)}) %collective-permute-start.12) | collective-permute-done | bytes 1179680 | tf_op jit(solution)/shard_map/ppermute | solution.py:18
  212.1 1.9 collective-permute-start.13
  214.5 3.8 %collective-permute-done.3 = bf16[384,768]{1,0:T(8,128)(2,1)S(1)} collective-permute-done((bf16[384,768]{1,0:T(8,128)(2,1)S(1)}, bf16[384,768]{1,0:T(8,128)(2,1)S(1)}, u32[]{:S(2)}, u32[]{:S(2)}) %collective-permute-start.3) | collective-permute-done | bytes 589856 | tf_op jit(solution)/shard_map/ppermute | solution.py:18
  219.5 14.9 %collective-permute-done.8 = f32[384,768]{1,0:T(8,128)S(1)} collective-permute-done((f32[384,768]{1,0:T(8,128)S(1)}, f32[384,768]{1,0:T(8,128)S(1)}, u32[]{:S(2)}, u32[]{:S(2)}) %collective-permute-start.8) | collective-permute-done | bytes 1179680 | tf_op jit(solution)/shard_map/ppermute | solution.py:18
  234.5 1.9 collective-permute-start.9
  236.5 7.7 %collective-permute-done.6 = bf16[384,768]{1,0:T(8,128)(2,1)S(1)} collective-permute-done((bf16[384,768]{1,0:T(8,128)(2,1)S(1)}, bf16[384,768]{1,0:T(8,128)(2,1)S(1)}, u32[]{:S(2)}, u32[]{:S(2)}) %collective-permute-start.6) | collective-permute-done | bytes 589856 | tf_op jit(solution)/shard_map/ppermute | solution.py:18
  245.4 17.2 %collective-permute-done.13 = f32[384,768]{1,0:T(8,128)S(1)} collective-permute-done((f32[384,768]{1,0:T(8,128)S(1)}, f32[384,768]{1,0:T(8,128)S(1)}, u32[]{:S(2)}, u32[]{:S(2)}) %collective-permute-start.13) | collective-permute-done | bytes 1179680 | tf_op jit(solution)/shard_map/ppermute | solution.py:18
  262.7 1.9 collective-permute-start.14
  265.1 2.1 collective-permute-start.5
  268.1 14.3 %collective-permute-done.5 = bf16[384,768]{1,0:T(8,128)(2,1)S(1)} collective-permute-done((bf16[384,768]{1,0:T(8,128)(2,1)S(1)}, bf16[384,768]{1,0:T(8,128)(2,1)S(1)}, u32[]{:S(2)}, u32[]{:S(2)}) %collective-permute-start.5) | collective-permute-done | bytes 589856 | tf_op jit(solution)/shard_map/ppermute | solution.py:18
  285.7 7.2 %collective-permute-done.14 = f32[384,768]{1,0:T(8,128)S(1)} collective-permute-done((f32[384,768]{1,0:T(8,128)S(1)}, f32[384,768]{1,0:T(8,128)S(1)}, u32[]{:S(2)}, u32[]{:S(2)}) %collective-permute-start.14) | collective-permute-done | bytes 1179680 | tf_op jit(solution)/shard_map/ppermute | solution.py:18
  292.9 3.6 %collective-permute-start.15 = (f32[384,768]{1,0:T(8,128)S(1)}, f32[384,768]{1,0:T(8,128)S(1)}, u32[]{:S(2)}, u32[]{:S(2)}) collective-permute-start(f32[384,768]{1,0:T(8,128)S(1)} %collective-permute-done.14), channel_id=1, source_target_pairs={{0,1},{1,0},{2,3},{3,2},{4,5},{5,4},{6,7},{7,6},{8,9},{9,8},{10,11... | collective-permute-start | bytes 3538952 | tf_op jit(solution)/shard_map/ppermute | solution.py:13
  299.3 15.3 %collective-permute-done.10 = f32[384,768]{1,0:T(8,128)S(1)} collective-permute-done((f32[384,768]{1,0:T(8,128)S(1)}, f32[384,768]{1,0:T(8,128)S(1)}, u32[]{:S(2)}, u32[]{:S(2)}) %collective-permute-start.10) | collective-permute-done | bytes 1179680 | tf_op jit(solution)/shard_map/ppermute | solution.py:18
  314.5 28.3 %collective-permute-done.15 = f32[384,768]{1,0:T(8,128)S(1)} collective-permute-done((f32[384,768]{1,0:T(8,128)S(1)}, f32[384,768]{1,0:T(8,128)S(1)}, u32[]{:S(2)}, u32[]{:S(2)}) %collective-permute-start.15) | collective-permute-done | bytes 1179680 | tf_op jit(solution)/shard_map/ppermute | solution.py:13
  (48 shorter events, 28.4 us)
Async XLA Ops:
  0.6 8.2 %copy-start = (bf16[384,768]{1,0:T(8,128)(2,1)S(1)}, bf16[384,768]{1,0:T(8,128)(2,1)}, u32[]{:S(2)}) copy-start(bf16[384,768]{1,0:T(8,128)(2,1)} %param.4) | copy-start | bytes 1769476
  3.2 17.6 %collective-permute-start = (bf16[384,768]{1,0:T(8,128)(2,1)S(1)}, bf16[384,768]{1,0:T(8,128)(2,1)S(1)}, u32[]{:S(2)}, u32[]{:S(2)}) collective-permute-start(bf16[384,768]{1,0:T(8,128)(2,1)S(1)} %fusion.2), channel_id=1, source_target_pairs={{0,1},{1,0},{2,3},{3,2},{4,5},{5,4},{6,7},{7,6},{8,9},{9,8},{10,11... | collective-permute-start | bytes 1769480 | tf_op jit(solution)/shard_map/ppermute | solution.py:13
  22.0 154.6 %collective-permute-start.11 = (f32[384,768]{1,0:T(8,128)S(1)}, f32[384,768]{1,0:T(8,128)S(1)}, u32[]{:S(2)}, u32[]{:S(2)}) collective-permute-start(f32[384,768]{1,0:T(8,128)S(1)} %fusion.79), channel_id=1, source_target_pairs={{0,32},{32,64},{64,96},{96,128},{128,160},{160,192},{192,224},{224... | collective-permute-start | bytes 3538952 | tf_op jit(solution)/shard_map/ppermute | solution.py:18
  23.9 150.2 %collective-permute-start.2 = (bf16[384,768]{1,0:T(8,128)(2,1)S(1)}, bf16[384,768]{1,0:T(8,128)(2,1)S(1)}, u32[]{:S(2)}, u32[]{:S(2)}) collective-permute-start(bf16[384,768]{1,0:T(8,128)(2,1)S(1)} %collective-permute-done), channel_id=1, source_target_pairs={{0,32},{32,64},{64,96},{96,128},{128,160},{160,192},{192,224},{224... | collective-permute-start | bytes 1769480 | tf_op jit(solution)/shard_map/ppermute | solution.py:18
  28.6 166.9 %collective-permute-start.7 = (f32[384,768]{1,0:T(8,128)S(1)}, f32[384,768]{1,0:T(8,128)S(1)}, u32[]{:S(2)}, u32[]{:S(2)}) collective-permute-start(f32[384,768]{1,0:T(8,128)S(1)} %fusion.86), channel_id=1, source_target_pairs={{0,32},{32,64},{64,96},{96,128},{128,160},{160,192},{192,224},{224... | collective-permute-start | bytes 3538952 | tf_op jit(solution)/shard_map/ppermute | solution.py:18
  30.6 162.5 %collective-permute-start.1 = (bf16[384,768]{1,0:T(8,128)(2,1)S(1)}, bf16[384,768]{1,0:T(8,128)(2,1)S(1)}, u32[]{:S(2)}, u32[]{:S(2)}) collective-permute-start(bf16[384,768]{1,0:T(8,128)(2,1)S(1)} %fusion.2), channel_id=1, source_target_pairs={{0,32},{32,64},{64,96},{96,128},{128,160},{160,192},{192,224},{224... | collective-permute-start | bytes 1769480 | tf_op jit(solution)/shard_map/ppermute | solution.py:18
  174.1 25.3 %collective-permute-start.4 = (bf16[384,768]{1,0:T(8,128)(2,1)S(1)}, bf16[384,768]{1,0:T(8,128)(2,1)S(1)}, u32[]{:S(2)}, u32[]{:S(2)}) collective-permute-start(bf16[384,768]{1,0:T(8,128)(2,1)S(1)} %collective-permute-done.2), channel_id=1, source_target_pairs={{0,32},{32,64},{64,96},{96,128},{128,160},{160,192},{192,224},{224... | collective-permute-start | bytes 1769480 | tf_op jit(solution)/shard_map/ppermute | solution.py:18
  177.2 34.8 %collective-permute-start.12 = (f32[384,768]{1,0:T(8,128)S(1)}, f32[384,768]{1,0:T(8,128)S(1)}, u32[]{:S(2)}, u32[]{:S(2)}) collective-permute-start(f32[384,768]{1,0:T(8,128)S(1)} %convolution_add_fusion), channel_id=1, source_target_pairs={{0,32},{32,64},{64,96},{96,128},{128,160},{160,192},{192,224},{224... | collective-permute-start | bytes 3538952 | tf_op jit(solution)/shard_map/ppermute | solution.py:18
  193.0 25.3 %collective-permute-start.3 = (bf16[384,768]{1,0:T(8,128)(2,1)S(1)}, bf16[384,768]{1,0:T(8,128)(2,1)S(1)}, u32[]{:S(2)}, u32[]{:S(2)}) collective-permute-start(bf16[384,768]{1,0:T(8,128)(2,1)S(1)} %collective-permute-done.1), channel_id=1, source_target_pairs={{0,32},{32,64},{64,96},{96,128},{128,160},{160,192},{192,224},{224... | collective-permute-start | bytes 1769480 | tf_op jit(solution)/shard_map/ppermute | solution.py:18
  196.1 38.3 %collective-permute-start.8 = (f32[384,768]{1,0:T(8,128)S(1)}, f32[384,768]{1,0:T(8,128)S(1)}, u32[]{:S(2)}, u32[]{:S(2)}) collective-permute-start(f32[384,768]{1,0:T(8,128)S(1)} %convolution_add_fusion.1), channel_id=1, source_target_pairs={{0,32},{32,64},{64,96},{96,128},{128,160},{160,192},{192,224},{224... | collective-permute-start | bytes 3538952 | tf_op jit(solution)/shard_map/ppermute | solution.py:18
  199.3 44.9 %collective-permute-start.6 = (bf16[384,768]{1,0:T(8,128)(2,1)S(1)}, bf16[384,768]{1,0:T(8,128)(2,1)S(1)}, u32[]{:S(2)}, u32[]{:S(2)}) collective-permute-start(bf16[384,768]{1,0:T(8,128)(2,1)S(1)} %collective-permute-done.4), channel_id=1, source_target_pairs={{0,32},{32,64},{64,96},{96,128},{128,160},{160,192},{192,224},{224... | collective-permute-start | bytes 1769480 | tf_op jit(solution)/shard_map/ppermute | solution.py:18
  212.1 50.4 %collective-permute-start.13 = (f32[384,768]{1,0:T(8,128)S(1)}, f32[384,768]{1,0:T(8,128)S(1)}, u32[]{:S(2)}, u32[]{:S(2)}) collective-permute-start(f32[384,768]{1,0:T(8,128)S(1)} %add.154), channel_id=1, source_target_pairs={{0,32},{32,64},{64,96},{96,128},{128,160},{160,192},{192,224},{224... | collective-permute-start | bytes 3538952 | tf_op jit(solution)/shard_map/ppermute | solution.py:18
  234.5 49.1 %collective-permute-start.9 = (f32[384,768]{1,0:T(8,128)S(1)}, f32[384,768]{1,0:T(8,128)S(1)}, u32[]{:S(2)}, u32[]{:S(2)}) collective-permute-start(f32[384,768]{1,0:T(8,128)S(1)} %add.151), channel_id=1, source_target_pairs={{0,32},{32,64},{64,96},{96,128},{128,160},{160,192},{192,224},{224... | collective-permute-start | bytes 3538952 | tf_op jit(solution)/shard_map/ppermute | solution.py:18
  262.7 30.2 %collective-permute-start.14 = (f32[384,768]{1,0:T(8,128)S(1)}, f32[384,768]{1,0:T(8,128)S(1)}, u32[]{:S(2)}, u32[]{:S(2)}) collective-permute-start(f32[384,768]{1,0:T(8,128)S(1)} %add.155), channel_id=1, source_target_pairs={{0,416},{32,448},{64,480},{96,0},{128,32},{160,64},{192,96},{224,1... | collective-permute-start | bytes 3538952 | tf_op jit(solution)/shard_map/ppermute | solution.py:18
  265.1 17.3 %collective-permute-start.5 = (bf16[384,768]{1,0:T(8,128)(2,1)S(1)}, bf16[384,768]{1,0:T(8,128)(2,1)S(1)}, u32[]{:S(2)}, u32[]{:S(2)}) collective-permute-start(bf16[384,768]{1,0:T(8,128)(2,1)S(1)} %collective-permute-done.3), channel_id=1, source_target_pairs={{0,32},{32,64},{64,96},{96,128},{128,160},{160,192},{192,224},{224... | collective-permute-start | bytes 1769480 | tf_op jit(solution)/shard_map/ppermute | solution.py:18
  283.8 30.8 %collective-permute-start.10 = (f32[384,768]{1,0:T(8,128)S(1)}, f32[384,768]{1,0:T(8,128)S(1)}, u32[]{:S(2)}, u32[]{:S(2)}) collective-permute-start(f32[384,768]{1,0:T(8,128)S(1)} %add.152), channel_id=1, source_target_pairs={{0,416},{32,448},{64,480},{96,0},{128,32},{160,64},{192,96},{224,1... | collective-permute-start | bytes 3538952 | tf_op jit(solution)/shard_map/ppermute | solution.py:18
  292.9 49.9 %collective-permute-start.15 = (f32[384,768]{1,0:T(8,128)S(1)}, f32[384,768]{1,0:T(8,128)S(1)}, u32[]{:S(2)}, u32[]{:S(2)}) collective-permute-start(f32[384,768]{1,0:T(8,128)S(1)} %collective-permute-done.14), channel_id=1, source_target_pairs={{0,1},{1,0},{2,3},{3,2},{4,5},{5,4},{6,7},{7,6},{8,9},{9,8},{10,11... | collective-permute-start | bytes 3538952 | tf_op jit(solution)/shard_map/ppermute | solution.py:13
  298.0 44.8 %copy-start.1 = (bf16[384,768]{1,0:T(8,128)(2,1)S(1)}, bf16[384,768]{1,0:T(8,128)(2,1)}, u32[]{:S(2)}) copy-start(bf16[384,768]{1,0:T(8,128)(2,1)} %param.5) | copy-start | bytes 1769476
where the time goes:
time: 345 us; the launch traced here: 344 us
  waiting for transfers between devices  285 us (83%)
  starting transfers between devices  38.1 us (11%)
  matrix products  13.2 us (4%)
  other arithmetic  6.25 us (2%)
    ppermute x14, waiting for transfers between devices, from_behind(): lax.ppermute(shard, axis, [(i, (i + by) % size) for i in range(size)])  245 us
    ppermute x2, waiting for transfers between devices, partner_2(): lax.ppermute(shard, axis, [(i, i ^ 1 << bit) for i in range(lax.axis_size...  40.1 us
    ppermute x14, starting transfers between devices, from_behind(): lax.ppermute(shard, axis, [(i, (i + by) % size) for i in range(size)])  30.2 us
    ppermute x2, starting transfers between devices, partner_2(): lax.ppermute(shard, axis, [(i, i ^ 1 << bit) for i in range(lax.axis_size...  7.87 us
  transfers between devices with their start and end apart: 16, of which 13 were waited for; matrix products, arithmetic and copies ran while one was open for 4% of the time, Pallas kernels for 0%

commit v1 on v0

v1 whole, which is shorter than its diff:
```python
import functools

import jax
import jax.numpy as jnp
from jax import lax
from jax.experimental import pallas as pl
from jax.experimental.pallas import tpu as pltpu
from jax.sharding import PartitionSpec as P

AXES = ("blk", "group")
EPSILON = 1e-06
VMEM_LIMIT = 48 * 1024 * 1024

VMEM = pl.BlockSpec(memory_space=pltpu.VMEM)
SMEM = pl.BlockSpec(memory_space=pltpu.SMEM)
PARAMS = pltpu.CompilerParams(vmem_limit_bytes=VMEM_LIMIT)


def shift_pairs(size, by):
    return [(b, (b + by) % size) for b in range(size)]


def core_pairs(size):
    return [(b, b ^ 1) for b in range(size)]


def odd_pairs(size, by):
    return [(b, (b + by) % size if b % 2 else b) for b in range(size)]


def partner_pairs(size):
    return [(g, g ^ 1) for g in range(size)]


def normalize(values):
    full = values.astype(jnp.float32)
    inverse = lax.rsqrt(jnp.sum(full * full, axis=-1, keepdims=True) + EPSILON)
    return full * inverse, inverse


def hat(values):
    return normalize(values)[0].astype(jnp.bfloat16)


def dot(left, right, left_dim, right_dim):
    return lax.dot_general(
        left, right, (((left_dim,), (right_dim,)), ((), ())), preferred_element_type=jnp.float32
    )


def slopes_of(image_hat, text_hat, scale, bias, same=None):
    chance = jax.nn.sigmoid(scale * dot(image_hat, text_hat, 1, 1) + bias)
    if same is not None:
        chance = chance - same
    return (scale * chance).astype(jnp.bfloat16)


def own_kernel(scale_ref, bias_ref, text_ref, image_ref, partner_ref, own_ref, other_ref, text_grad_ref):
    scale, bias = scale_ref[0], bias_ref[0]
    text_hat = hat(text_ref[...])
    rows = text_hat.shape[0]
    same = (
        lax.broadcasted_iota(jnp.int32, (rows, rows), 0)
        == lax.broadcasted_iota(jnp.int32, (rows, rows), 1)
    ).astype(jnp.float32)
    image_hat = hat(image_ref[...])
    slopes = slopes_of(image_hat, text_hat, scale, bias, same)
    own_ref[...] = dot(slopes, text_hat, 1, 0)
    text_grad_ref[...] = dot(slopes, image_hat, 0, 0)
    image_hat = hat(partner_ref[...])
    slopes = slopes_of(image_hat, text_hat, scale, bias)
    other_ref[...] = dot(slopes, text_hat, 1, 0)
    text_grad_ref[...] += dot(slopes, image_hat, 0, 0)


def rest_kernel(
    scale_ref, bias_ref, near_ref, far_ref, i0, i1, i2, i3, own_ref, other_ref,
    own_out, other_out, cross_out, near_grad_out, far_grad_out, images, grads, text_sum,
):
    scale, bias = scale_ref[0], bias_ref[0]
    for slot, ref in enumerate((i0, i1, i2, i3)):
        images[slot] = hat(ref[...])
    grads[0] = own_ref[...]
    grads[1] = other_ref[...]
    grads[2] = jnp.zeros_like(own_ref)
    grads[3] = jnp.zeros_like(own_ref)

    def against(text_ref, first, out_ref):
        text_hat = hat(text_ref[...])
        text_sum[...] = jnp.zeros_like(text_sum)

        def step(slot, carry):
            image_hat = images[slot]
            slopes = slopes_of(image_hat, text_hat, scale, bias)
            grads[slot] += dot(slopes, text_hat, 1, 0)
            text_sum[...] += dot(slopes, image_hat, 0, 0)
            return carry

        lax.fori_loop(first, 4, step, 0)
        out_ref[...] = text_sum[...].astype(out_ref.dtype)

    against(near_ref, 0, near_grad_out)
    against(far_ref, 2, far_grad_out)
    own_out[...] = grads[0]
    other_out[...] = grads[1]
    cross_out[0] = grads[2].astype(cross_out.dtype)
    cross_out[1] = grads[3].astype(cross_out.dtype)


def final_kernel(count, *refs):
    raw_ref, sum_ref = refs[0], refs[1]
    total = sum_ref[...]
    for ref in refs[2 : 2 + count]:
        total = total + ref[...].astype(jnp.float32)
    unit, inverse = normalize(raw_ref[...])
    out_ref = refs[-1]
    out_ref[...] = (total - unit * jnp.sum(unit * total, axis=-1, keepdims=True)) * inverse


def finish(raw, total, *received):
    rows, width = raw.shape
    block = pl.BlockSpec((rows // 3, width), lambda i: (i, 0))
    return pl.pallas_call(
        functools.partial(final_kernel, len(received)),
        grid=(3,),
        in_specs=[block] * (2 + len(received)),
        out_specs=block,
        out_shape=jax.ShapeDtypeStruct(raw.shape, jnp.float32),
        compiler_params=PARAMS,
    )(raw, total, *received)


def on_device(images, texts, logit_scale, logit_bias):
    n_blk = lax.axis_size("blk")
    n_group = lax.axis_size("group")
    rows, width = images.shape
    full = jax.ShapeDtypeStruct((rows, width), jnp.float32)
    half = jax.ShapeDtypeStruct((rows, width), jnp.bfloat16)
    pair = jax.ShapeDtypeStruct((2, rows, width), jnp.bfloat16)

    def along_blk(values, pairs):
        return lax.ppermute(values, "blk", pairs)

    def to_partner(values):
        return lax.ppermute(values, "group", partner_pairs(n_group))

    near = along_blk(texts, shift_pairs(n_blk, 2))
    far = along_blk(texts, odd_pairs(n_blk, 4))
    partner = to_partner(images)
    other = along_blk(images, core_pairs(n_blk))
    other_partner = along_blk(partner, core_pairs(n_blk))

    own_grad, partner_grad, text_grad = pl.pallas_call(
        own_kernel,
        in_specs=[SMEM, SMEM, VMEM, VMEM, VMEM],
        out_specs=[VMEM] * 3,
        out_shape=[full] * 3,
        compiler_params=PARAMS,
    )(logit_scale, logit_bias, texts, images, partner)

    own_grad, partner_grad, cross, near_grad, far_grad = pl.pallas_call(
        rest_kernel,
        in_specs=[SMEM, SMEM] + [VMEM] * 8,
        out_specs=[VMEM] * 5,
        out_shape=[full, full, pair, half, half],
        scratch_shapes=[
            pltpu.VMEM((4, rows, width), jnp.bfloat16),
            pltpu.VMEM((4, rows, width), jnp.float32),
            pltpu.VMEM((rows, width), jnp.float32),
        ],
        compiler_params=PARAMS,
    )(
        logit_scale, logit_bias, near, far, images, partner, other, other_partner,
        own_grad, partner_grad,
    )

    near_back = along_blk(near_grad, shift_pairs(n_blk, -2))
    far_back = along_blk(far_grad, odd_pairs(n_blk, -4))
    cross = along_blk(cross, core_pairs(n_blk))
    partner_total = (partner_grad + cross[1].astype(jnp.float32)).astype(jnp.bfloat16)
    partner_back = to_partner(partner_total)
    image_grad = finish(images, own_grad, cross[0], partner_back)
    text_grad = finish(texts, text_grad, near_back, far_back)
    return image_grad, text_grad


def solution(mesh):
    return jax.shard_map(
        on_device,
        mesh=mesh,
        in_specs=(P(AXES, None), P(AXES, None), P(), P()),
        out_specs=(P(AXES, None), P(AXES, None)),
        check_vma=False,
    )
```

time: 345 us -> 130 us (0.38)
  the two profiles are of different devices: /device:TPU:184 before, /device:TPU:1 now
where the time goes in v1:
time: 130 us; the launch traced here: 129 us
  waiting for transfers between devices  74.8 us (58%)
  starting transfers between devices  28.8 us (22%)
  Pallas kernels  18.1 us (14%)
  local copies, waits for them, and re-layouts  4.18 us (3%)
  between operations  2.05 us (2%)
  other arithmetic  1.38 us (1%)
    ppermute x7, waiting for transfers between devices, along_blk(): return lax.ppermute(values, 'blk', pairs)  69.8 us
    ppermute x7, starting transfers between devices, along_blk(): return lax.ppermute(values, 'blk', pairs)  22.1 us
    pallas_call x1, Pallas kernels, on_device(): pl.pallas_call(rest_kernel, in_specs=[SMEM, SMEM] + [VMEM] * 8, out_specs...  11.8 us
    ppermute x2, starting transfers between devices, to_partner(): return lax.ppermute(values, 'group', partner_pairs(n_group))  6.75 us
    ppermute x2, waiting for transfers between devices, to_partner(): return lax.ppermute(values, 'group', partner_pairs(n_group))  4.99 us
    unnamed x10, local copies, waits for them, and re-layouts  4.14 us
    pallas_call x2, Pallas kernels, finish(): pl.pallas_call(functools.partial(final_kernel, len(received)), grid=(3,),...  3.85 us
  transfers between devices with their start and end apart: 9, of which 5 were waited for; matrix products, arithmetic and copies ran while one was open for 1% of the time, Pallas kernels for 3%

profile of v1, /device:TPU:1, one launch (start us, length us, event | category | flops | bytes accessed | tf_op | source)
XLA Modules:
  0.0 129.3 jit_solution(17606755916221726317)
XLA Ops:
  0.6 4.8 %collective-permute-start.2 = (bf16[384,768]{1,0:T(8,128)(2,1)}, bf16[384,768]{1,0:T(8,128)(2,1)S(1)}, u32[]{:S(2)}, u32[]{:S(2)}) collective-permute-start(bf16[384,768]{1,0:T(8,128)(2,1)} %refs_0_.2), channel_id=1, source_target_pairs={{0,1},{1,0},{2,3},{3,2},{4,5},{5,4},{6,7},{7,6},{8,9},{9,8},{10,11... | collective-permute-start | bytes 1769480 | tf_op jit(solution)/shard_map/ppermute | solution.py:145
  5.5 4.7 %collective-permute-start.1 = (bf16[384,768]{1,0:T(8,128)(2,1)}, bf16[384,768]{1,0:T(8,128)(2,1)S(1)}, u32[]{:S(2)}, u32[]{:S(2)}) collective-permute-start(bf16[384,768]{1,0:T(8,128)(2,1)} %refs_0_.3), channel_id=1, source_target_pairs={{0,0},{32,160},{64,64},{96,224},{128,128},{160,288},{192,192},{224... | collective-permute-start | bytes 1769480 | tf_op jit(solution)/shard_map/ppermute | solution.py:142
  10.1 2.2 %collective-permute-start = (bf16[384,768]{1,0:T(8,128)(2,1)}, bf16[384,768]{1,0:T(8,128)(2,1)S(1)}, u32[]{:S(2)}, u32[]{:S(2)}) collective-permute-start(bf16[384,768]{1,0:T(8,128)(2,1)} %refs_0_.3), channel_id=1, source_target_pairs={{0,64},{32,96},{64,128},{96,160},{128,192},{160,224},{192,256},{22... | collective-permute-start | bytes 1769480 | tf_op jit(solution)/shard_map/ppermute | solution.py:142
  12.4 2.6 %collective-permute-start.3 = (bf16[384,768]{1,0:T(8,128)(2,1)}, bf16[384,768]{1,0:T(8,128)(2,1)S(1)}, u32[]{:S(2)}, u32[]{:S(2)}) collective-permute-start(bf16[384,768]{1,0:T(8,128)(2,1)} %refs_0_.2), channel_id=1, source_target_pairs={{0,32},{32,0},{64,96},{96,64},{128,160},{160,128},{192,224},{224,1... | collective-permute-start | bytes 1769480 | tf_op jit(solution)/shard_map/ppermute | solution.py:142
  15.0 6.8 %collective-permute-start.4 = (bf16[384,768]{1,0:T(8,128)(2,1)S(1)}, bf16[384,768]{1,0:T(8,128)(2,1)S(1)}, u32[]{:S(2)}, u32[]{:S(2)}) collective-permute-start(bf16[384,768]{1,0:T(8,128)(2,1)S(1)} %collective-permute-done.2.partner_ref.i1), channel_id=1, source_target_pairs={{0,32},{32,0},{64,96},{96,64},{128,160},{160,128},{192,224},{224,1... | collective-permute-start | bytes 1769480 | tf_op jit(solution)/shard_map/ppermute | solution.py:142
  23.2 1.1 copy-done
  24.2 1.1 copy-done.2
  25.3 2.4 %shard_map.59 = (f32[384,768]{1,0:T(8,128)S(1)}, f32[384,768]{1,0:T(8,128)S(1)}, f32[384,768]{1,0:T(8,128)S(1)}) custom-call(f32[1]{0:T(128)S(6)} %copy.6.scale_ref, f32[1]{0:T(128)S(6)} %copy.7.bias_ref, bf16[384,768]{1,0:T(8,128)(2,1)S(1)} %copy-done.2, bf16[384,768]{1,0:T(8,128)(2,1)S(1)} %copy-done, ...), custom_call_target="tpu_custom_call" | custom-call | tf_op jit(solution)/shard_map/pallas_call | solution.py:153
  27.7 0.0 copy-start.3
  27.7 1.0 copy-done.3
  28.7 1.0 copy-done.4
  29.7 13.5 %collective-permute-done.1.far_ref = bf16[384,768]{1,0:T(8,128)(2,1)S(1)} collective-permute-done((bf16[384,768]{1,0:T(8,128)(2,1)}, bf16[384,768]{1,0:T(8,128)(2,1)S(1)}, u32[]{:S(2)}, u32[]{:S(2)}) %collective-permute-start.1) | collective-permute-done | bytes 589856 | tf_op jit(solution)/shard_map/ppermute | solution.py:142
  43.2 10.0 %collective-permute-done.near_ref = bf16[384,768]{1,0:T(8,128)(2,1)S(1)} collective-permute-done((bf16[384,768]{1,0:T(8,128)(2,1)}, bf16[384,768]{1,0:T(8,128)(2,1)S(1)}, u32[]{:S(2)}, u32[]{:S(2)}) %collective-permute-start) | collective-permute-done | bytes 589856 | tf_op jit(solution)/shard_map/ppermute | solution.py:142
  53.2 11.8 %shard_map.60 = (f32[384,768]{1,0:T(8,128)S(1)}, f32[384,768]{1,0:T(8,128)}, bf16[2,384,768]{2,1,0:T(8,128)(2,1)}, bf16[384,768]{1,0:T(8,128)(2,1)S(1)}, bf16[384,768]{1,0:T(8,128)(2,1)S(1)}) custom-call(f32[1]{0:T(128)S(6)} %copy.6.scale_ref, f32[1]{0:T(128)S(6)} %copy.7.bias_ref, bf16[384,768]{1,0:T(8,128)(2,1)S(1)} %collective-permute-done.near_ref, ...), custom_call_target="tpu_custom_call" | custom-call | tf_op jit(solution)/shard_map/pallas_call | solution.py:161
  65.0 1.9 %collective-permute-start.5 = (bf16[2,384,768]{2,1,0:T(8,128)(2,1)}, bf16[2,384,768]{2,1,0:T(8,128)(2,1)S(1)}, u32[]{:S(2)}, u32[]{:S(2)}) collective-permute-start(bf16[2,384,768]{2,1,0:T(8,128)(2,1)} %get-tuple-element.13), channel_id=1, source_target_pairs={{0,32},{32,0},{64,96},{96,64},{128,160},{160,128},{192,224},{224,1... | collective-permute-start | bytes 3538952 | tf_op jit(solution)/shard_map/ppermute | solution.py:142
  67.0 1.9 %collective-permute-start.7 = (bf16[384,768]{1,0:T(8,128)(2,1)S(1)}, bf16[384,768]{1,0:T(8,128)(2,1)S(1)}, u32[]{:S(2)}, u32[]{:S(2)}) collective-permute-start(bf16[384,768]{1,0:T(8,128)(2,1)S(1)} %get-tuple-element.16), channel_id=1, source_target_pairs={{0,448},{32,480},{64,0},{96,32},{128,64},{160,96},{192,128},{224,1... | collective-permute-start | bytes 1769480 | tf_op jit(solution)/shard_map/ppermute | solution.py:142
  68.9 1.9 %collective-permute-start.8 = (bf16[384,768]{1,0:T(8,128)(2,1)S(1)}, bf16[384,768]{1,0:T(8,128)(2,1)S(1)}, u32[]{:S(2)}, u32[]{:S(2)}) collective-permute-start(bf16[384,768]{1,0:T(8,128)(2,1)S(1)} %get-tuple-element.17), channel_id=1, source_target_pairs={{0,0},{32,416},{64,64},{96,480},{128,128},{160,32},{192,192},{224,... | collective-permute-start | bytes 1769480 | tf_op jit(solution)/shard_map/ppermute | solution.py:142
  70.8 1.4 %fusion = bf16[384,768]{1,0:T(8,128)(2,1)S(1)} fusion(f32[384,768]{1,0:T(8,128)} %get-tuple-element.14, bf16[2,384,768]{2,1,0:T(8,128)(2,1)S(1)} %collective-permute-done.5), kind=kLoop, calls=%fused_computation.1 | loop fusion | flops 884736 | bytes 2359296 | tf_op jit(solution)/shard_map/convert_element_type | solution.py:180
  72.2 1.9 %collective-permute-start.6 = (bf16[384,768]{1,0:T(8,128)(2,1)S(1)}, bf16[384,768]{1,0:T(8,128)(2,1)S(1)}, u32[]{:S(2)}, u32[]{:S(2)}) collective-permute-start(bf16[384,768]{1,0:T(8,128)(2,1)S(1)} %fusion), channel_id=1, source_target_pairs={{0,1},{1,0},{2,3},{3,2},{4,5},{5,4},{6,7},{7,6},{8,9},{9,8},{10,11... | collective-permute-start | bytes 1769480 | tf_op jit(solution)/shard_map/ppermute | solution.py:145
  74.1 13.0 %collective-permute-done.7.refs_2_ = bf16[384,768]{1,0:T(8,128)(2,1)S(1)} collective-permute-done((bf16[384,768]{1,0:T(8,128)(2,1)S(1)}, bf16[384,768]{1,0:T(8,128)(2,1)S(1)}, u32[]{:S(2)}, u32[]{:S(2)}) %collective-permute-start.7) | collective-permute-done | bytes 589856 | tf_op jit(solution)/shard_map/ppermute | solution.py:142
  87.2 33.3 %collective-permute-done.8.refs_3_ = bf16[384,768]{1,0:T(8,128)(2,1)S(1)} collective-permute-done((bf16[384,768]{1,0:T(8,128)(2,1)S(1)}, bf16[384,768]{1,0:T(8,128)(2,1)S(1)}, u32[]{:S(2)}, u32[]{:S(2)}) %collective-permute-start.8) | collective-permute-done | bytes 589856 | tf_op jit(solution)/shard_map/ppermute | solution.py:142
  120.4 1.9 %shard_map.62 = f32[384,768]{1,0:T(8,128)} custom-call(bf16[384,768]{1,0:T(8,128)(2,1)S(1)} %copy-done.2, f32[384,768]{1,0:T(8,128)S(1)} %get-tuple-element.15.refs_1_, bf16[384,768]{1,0:T(8,128)(2,1)S(1)} %collective-permute-done.7.refs_2_, bf16[384,768]{1,0:T(8,128)(2,1)S(1)} %collective-permute-done.8.refs_3_), custom_call_target="tpu_custom_call" | custom-call | tf_op jit(solution)/shard_map/pallas_call | solution.py:123
  122.4 5.0 %collective-permute-done.6.refs_3_ = bf16[384,768]{1,0:T(8,128)(2,1)S(1)} collective-permute-done((bf16[384,768]{1,0:T(8,128)(2,1)S(1)}, bf16[384,768]{1,0:T(8,128)(2,1)S(1)}, u32[]{:S(2)}, u32[]{:S(2)}) %collective-permute-start.6) | collective-permute-done | bytes 589856 | tf_op jit(solution)/shard_map/ppermute | solution.py:145
  127.4 1.9 %shard_map.61 = f32[384,768]{1,0:T(8,128)} custom-call(bf16[384,768]{1,0:T(8,128)(2,1)S(1)} %copy-done.1, f32[384,768]{1,0:T(8,128)S(1)} %get-tuple-element.12.refs_1_, bf16[384,768]{1,0:T(8,128)(2,1)S(1)} %slice_bitcast_fusion.1.refs_2_, bf16[384,768]{1,0:T(8,128)(2,1)S(1)} %collective-permute-done.6.refs_3_), custom_call_target="tpu_custom_call" | custom-call | tf_op jit(solution)/shard_map/pallas_call | solution.py:123
  (10 shorter events, 0.1 us)
Async XLA Ops:
  0.6 14.4 %collective-permute-start.2 = (bf16[384,768]{1,0:T(8,128)(2,1)}, bf16[384,768]{1,0:T(8,128)(2,1)S(1)}, u32[]{:S(2)}, u32[]{:S(2)}) collective-permute-start(bf16[384,768]{1,0:T(8,128)(2,1)} %refs_0_.2), channel_id=1, source_target_pairs={{0,1},{1,0},{2,3},{3,2},{4,5},{5,4},{6,7},{7,6},{8,9},{9,8},{10,11... | collective-permute-start | bytes 1769480 | tf_op jit(solution)/shard_map/ppermute | solution.py:145
  5.5 37.7 %collective-permute-start.1 = (bf16[384,768]{1,0:T(8,128)(2,1)}, bf16[384,768]{1,0:T(8,128)(2,1)S(1)}, u32[]{:S(2)}, u32[]{:S(2)}) collective-permute-start(bf16[384,768]{1,0:T(8,128)(2,1)} %refs_0_.3), channel_id=1, source_target_pairs={{0,0},{32,160},{64,64},{96,224},{128,128},{160,288},{192,192},{224... | collective-permute-start | bytes 1769480 | tf_op jit(solution)/shard_map/ppermute | solution.py:142
  10.1 43.1 %collective-permute-start = (bf16[384,768]{1,0:T(8,128)(2,1)}, bf16[384,768]{1,0:T(8,128)(2,1)S(1)}, u32[]{:S(2)}, u32[]{:S(2)}) collective-permute-start(bf16[384,768]{1,0:T(8,128)(2,1)} %refs_0_.3), channel_id=1, source_target_pairs={{0,64},{32,96},{64,128},{96,160},{128,192},{160,224},{192,256},{22... | collective-permute-start | bytes 1769480 | tf_op jit(solution)/shard_map/ppermute | solution.py:142
  12.4 40.8 %collective-permute-start.3 = (bf16[384,768]{1,0:T(8,128)(2,1)}, bf16[384,768]{1,0:T(8,128)(2,1)S(1)}, u32[]{:S(2)}, u32[]{:S(2)}) collective-permute-start(bf16[384,768]{1,0:T(8,128)(2,1)} %refs_0_.2), channel_id=1, source_target_pairs={{0,32},{32,0},{64,96},{96,64},{128,160},{160,128},{192,224},{224,1... | collective-permute-start | bytes 1769480 | tf_op jit(solution)/shard_map/ppermute | solution.py:142
  15.0 38.2 %collective-permute-start.4 = (bf16[384,768]{1,0:T(8,128)(2,1)S(1)}, bf16[384,768]{1,0:T(8,128)(2,1)S(1)}, u32[]{:S(2)}, u32[]{:S(2)}) collective-permute-start(bf16[384,768]{1,0:T(8,128)(2,1)S(1)} %collective-permute-done.2.partner_ref.i1), channel_id=1, source_target_pairs={{0,32},{32,0},{64,96},{96,64},{128,160},{160,128},{192,224},{224,1... | collective-permute-start | bytes 1769480 | tf_op jit(solution)/shard_map/ppermute | solution.py:142
  23.1 1.1 copy-start
  24.2 1.1 copy-start.2
  25.3 27.9 %copy-start.1 = (bf16[384,768]{1,0:T(8,128)(2,1)S(1)}, bf16[384,768]{1,0:T(8,128)(2,1)}, u32[]{:S(2)}) copy-start(bf16[384,768]{1,0:T(8,128)(2,1)} %refs_0_.2) | copy-start | bytes 1769476
  27.7 1.0 copy-start.3
  28.7 1.0 copy-start.4
  65.0 5.8 %collective-permute-start.5 = (bf16[2,384,768]{2,1,0:T(8,128)(2,1)}, bf16[2,384,768]{2,1,0:T(8,128)(2,1)S(1)}, u32[]{:S(2)}, u32[]{:S(2)}) collective-permute-start(bf16[2,384,768]{2,1,0:T(8,128)(2,1)} %get-tuple-element.13), channel_id=1, source_target_pairs={{0,32},{32,0},{64,96},{96,64},{128,160},{160,128},{192,224},{224,1... | collective-permute-start | bytes 3538952 | tf_op jit(solution)/shard_map/ppermute | solution.py:142
  67.0 20.2 %collective-permute-start.7 = (bf16[384,768]{1,0:T(8,128)(2,1)S(1)}, bf16[384,768]{1,0:T(8,128)(2,1)S(1)}, u32[]{:S(2)}, u32[]{:S(2)}) collective-permute-start(bf16[384,768]{1,0:T(8,128)(2,1)S(1)} %get-tuple-element.16), channel_id=1, source_target_pairs={{0,448},{32,480},{64,0},{96,32},{128,64},{160,96},{192,128},{224,1... | collective-permute-start | bytes 1769480 | tf_op jit(solution)/shard_map/ppermute | solution.py:142
  68.9 51.5 %collective-permute-start.8 = (bf16[384,768]{1,0:T(8,128)(2,1)S(1)}, bf16[384,768]{1,0:T(8,128)(2,1)S(1)}, u32[]{:S(2)}, u32[]{:S(2)}) collective-permute-start(bf16[384,768]{1,0:T(8,128)(2,1)S(1)} %get-tuple-element.17), channel_id=1, source_target_pairs={{0,0},{32,416},{64,64},{96,480},{128,128},{160,32},{192,192},{224,... | collective-permute-start | bytes 1769480 | tf_op jit(solution)/shard_map/ppermute | solution.py:142
  72.2 55.2 %collective-permute-start.6 = (bf16[384,768]{1,0:T(8,128)(2,1)S(1)}, bf16[384,768]{1,0:T(8,128)(2,1)S(1)}, u32[]{:S(2)}, u32[]{:S(2)}) collective-permute-start(bf16[384,768]{1,0:T(8,128)(2,1)S(1)} %fusion), channel_id=1, source_target_pairs={{0,1},{1,0},{2,3},{3,2},{4,5},{5,4},{6,7},{7,6},{8,9},{9,8},{10,11... | collective-permute-start | bytes 1769480 | tf_op jit(solution)/shard_map/ppermute | solution.py:145

commit v2 on v1

v2 whole, which is shorter than its diff:
```python
import functools

import jax
import jax.numpy as jnp
from jax import lax
from jax.experimental import pallas as pl
from jax.experimental.pallas import tpu as pltpu
from jax.sharding import PartitionSpec as P

AXES = ("blk", "group")
EPSILON = 1e-06
CHIPS = 4
CHUNKS = 2

SMEM = pl.BlockSpec(memory_space=pltpu.SMEM)
WHOLE = pl.BlockSpec(memory_space=pltpu.VMEM)


def params(mib):
    return pltpu.CompilerParams(vmem_limit_bytes=mib * 1024 * 1024)


def near_to(b, g, size):
    to = (b + 2) % size
    return to, g ^ (to // (2 * CHIPS) != b // (2 * CHIPS))


def far_to(b, g, size):
    if b % 2 == 0:
        return b, g
    to = (b + 4) % size
    return to, g ^ (to // (2 * CHIPS) != b // (2 * CHIPS))


def other_core(b, g, size):
    return b ^ 1, g


def partner(b, g, size):
    return b, g ^ 1


def move(values, where, inverse=False):
    n_blk, n_group = lax.axis_size("blk"), lax.axis_size("group")
    pairs = []
    for b in range(n_blk):
        for g in range(n_group):
            to_b, to_g = where(b, g, n_blk)
            pair = (b * n_group + g, to_b * n_group + to_g)
            pairs.append(pair[::-1] if inverse else pair)
    return lax.ppermute(values, AXES, sorted(pairs))


def normalize(values):
    full = values.astype(jnp.float32)
    inverse = lax.rsqrt(jnp.sum(full * full, axis=-1, keepdims=True) + EPSILON)
    return full * inverse, inverse


def hat(values):
    return normalize(values)[0].astype(jnp.bfloat16)


def dot(left, right, left_dim, right_dim):
    return lax.dot_general(
        left, right, (((left_dim,), (right_dim,)), ((), ())), preferred_element_type=jnp.float32
    )


def slopes_of(text_hat, image_hat, scale, bias, same=None):
    chance = jax.nn.sigmoid(scale * dot(text_hat, image_hat, 1, 1) + bias)
    if same is not None:
        chance = chance - same
    return (scale * chance).astype(jnp.bfloat16)


def own_kernel(scale_ref, bias_ref, text_ref, image_ref, partner_ref, text_grad_ref, slopes_ref, hat_ref):
    scale, bias = scale_ref[0], bias_ref[0]
    text_hat = hat(text_ref[...])
    rows = text_hat.shape[0]
    same = (
        lax.broadcasted_iota(jnp.int32, (rows, rows), 0)
        == lax.broadcasted_iota(jnp.int32, (rows, rows), 1)
    ).astype(jnp.float32)
    image_hat = hat(image_ref[...])
    slopes = slopes_of(text_hat, image_hat, scale, bias, same)
    slopes_ref[0] = slopes
    total = dot(slopes, image_hat, 1, 0)
    image_hat = hat(partner_ref[...])
    slopes = slopes_of(text_hat, image_hat, scale, bias)
    slopes_ref[1] = slopes
    text_grad_ref[...] = total + dot(slopes, image_hat, 1, 0)
    hat_ref[...] = text_hat


def hats_kernel(*refs):
    for slot, ref in enumerate(refs[:-1]):
        refs[-1][slot] = hat(ref[...])


def text_kernel(scale_ref, bias_ref, text_ref, images_ref, text_grad_ref, slopes_ref, hat_ref):
    count, rows, width = images_ref.shape
    text_hat = hat(text_ref[...])
    images = images_ref[...].reshape(count * rows, width)
    slopes = slopes_of(text_hat, images, scale_ref[0], bias_ref[0])
    text_grad_ref[...] = dot(slopes, images, 1, 0).astype(text_grad_ref.dtype)
    for slot in range(count):
        slopes_ref[slot] = slopes[:, slot * rows : (slot + 1) * rows]
    hat_ref[...] = text_hat


def image_kernel(count, *refs):
    total = None
    for slopes_ref, hat_ref in zip(refs[:count], refs[count : 2 * count]):
        term = dot(slopes_ref[0], hat_ref[...], 0, 0)
        total = term if total is None else total + term
    for ref in refs[2 * count : -1]:
        total = total + ref[...].astype(jnp.float32)
    refs[-1][...] = total.astype(refs[-1].dtype)


def final_kernel(parts, *refs):
    raw_ref, out_ref = refs[0], refs[-1]
    total = refs[1][...]
    at = 2
    for count in parts:
        pieces = [ref[...] for ref in refs[at : at + count]]
        at += count
        piece = pieces[0] if count == 1 else jnp.concatenate(pieces, axis=0)
        total = total + piece.astype(jnp.float32)
    unit, inverse = normalize(raw_ref[...])
    out_ref[...] = (total - unit * jnp.sum(unit * total, axis=-1, keepdims=True)) * inverse


def finish(raw, total, *received):
    flat = [piece for pieces in received for piece in pieces]
    return pl.pallas_call(
        functools.partial(final_kernel, [len(pieces) for pieces in received]),
        in_specs=[WHOLE] * (2 + len(flat)),
        out_specs=WHOLE,
        out_shape=jax.ShapeDtypeStruct(raw.shape, jnp.float32),
        compiler_params=params(12),
    )(raw, total, *flat)


def on_device(images, texts, logit_scale, logit_bias):
    rows, width = images.shape
    part = rows // CHUNKS
    bf16 = functools.partial(jax.ShapeDtypeStruct, dtype=jnp.bfloat16)
    full = jax.ShapeDtypeStruct((rows, width), jnp.float32)

    near = [move(texts[i * part : (i + 1) * part], near_to) for i in range(CHUNKS)]
    far = move(texts, far_to)
    partner_images = move(images, partner)
    other_images = move(images, other_core)
    positive = logit_scale[0] > 0

    def swap_cores(values):
        return move(values, other_core)

    other_partner = lax.cond(positive, swap_cores, swap_cores, partner_images)

    text_grad, own_slopes, own_hat = pl.pallas_call(
        own_kernel,
        in_specs=[SMEM, SMEM] + [WHOLE] * 3,
        out_specs=[WHOLE] * 3,
        out_shape=[full, bf16((2, rows, rows)), bf16((rows, width))],
        compiler_params=params(16),
    )(logit_scale, logit_bias, texts, images, partner_images)

    all_hats = pl.pallas_call(
        hats_kernel,
        in_specs=[WHOLE] * 4,
        out_specs=WHOLE,
        out_shape=bf16((4, rows, width)),
        compiler_params=params(12),
    )(images, partner_images, other_images, other_partner)

    def against(text, count):
        size = text.shape[0]
        return pl.pallas_call(
            text_kernel,
            grid=(1,),
            in_specs=[
                SMEM,
                SMEM,
                pl.BlockSpec((size, width), lambda i: (0, 0)),
                pl.BlockSpec((count, rows, width), lambda i: (4 // count - 1, 0, 0)),
            ],
            out_specs=[
                pl.BlockSpec((size, width), lambda i: (0, 0)),
                pl.BlockSpec((count, size, rows), lambda i: (0, 0, 0)),
                pl.BlockSpec((size, width), lambda i: (0, 0)),
            ],
            out_shape=[bf16((size, width)), bf16((count, size, rows)), bf16((size, width))],
            compiler_params=params(20),
        )(logit_scale, logit_bias, text, all_hats)

    far_grad, far_slopes, far_hat = against(far, 2)
    far_back = move(far_grad, far_to, True)
    terms = [against(text, 4) for text in near]
    near_back = [move(grad, near_to, True) for grad, _, _ in terms]

    def image_sum(sources, dtype, *more):
        slopes = [s for s, _, _ in sources]
        hats = [h for _, h, _ in sources]
        slots = [slot for _, _, slot in sources]
        return pl.pallas_call(
            functools.partial(image_kernel, len(sources)),
            grid=(1,),
            in_specs=[
                pl.BlockSpec((1,) + s.shape[1:], lambda i, slot=slot: (slot, 0, 0))
                for s, slot in zip(slopes, slots)
            ]
            + [pl.BlockSpec(a.shape, lambda i: (0, 0)) for a in hats + list(more)],
            out_specs=pl.BlockSpec((rows, width), lambda i: (0, 0)),
            out_shape=jax.ShapeDtypeStruct((rows, width), dtype),
            compiler_params=params(20),
        )(*slopes, *hats, *more)

    def near_terms(slot):
        return [(s, h, slot) for _, s, h in terms]

    cross_partner = image_sum(near_terms(3) + [(far_slopes, far_hat, 1)], jnp.bfloat16)
    cross_own = image_sum(near_terms(2) + [(far_slopes, far_hat, 0)], jnp.bfloat16)

    def exchange(cross_partner, cross_own, near_slopes, near_hats, own_slopes, own_hat):
        cross_partner = move(cross_partner, other_core)
        cross_own = move(cross_own, other_core)
        sources = [(s, h, 1) for s, h in zip(near_slopes + [own_slopes], near_hats + [own_hat])]
        from_partner = move(image_sum(sources, jnp.bfloat16, cross_partner), partner)
        return cross_own, from_partner

    cross_own, from_partner = lax.cond(
        positive,
        exchange,
        exchange,
        cross_partner,
        cross_own,
        [s for _, s, _ in terms],
        [h for _, _, h in terms],
        own_slopes,
        own_hat,
    )
    own_grad = image_sum(near_terms(0) + [(own_slopes, own_hat, 0)], jnp.float32)

    image_grad = finish(images, own_grad, [cross_own], [from_partner])
    text_grad = finish(texts, text_grad, near_back, [far_back])
    return image_grad, text_grad


def solution(mesh):
    return jax.shard_map(
        on_device,
        mesh=mesh,
        in_specs=(P(AXES, None), P(AXES, None), P(), P()),
        out_specs=(P(AXES, None), P(AXES, None)),
        check_vma=False,
    )
```

time: 130 us -> 106 us (0.82)
  waiting for transfers between devices: 74.8 us -> 22.3 us
  starting transfers between devices: 28.8 us -> 60.1 us
  local copies, waits for them, and re-layouts: 4.18 us -> 1.52 us
  other arithmetic: 1.38 us -> 0 us
    ppermute x9 -> x12, waiting for transfers between devices: 74.8 us -> 22.3 us  [move(): return lax.ppermute(values, AXES, sorted(pairs))]
    ppermute x9 -> x12, starting transfers between devices: 28.8 us -> 60.1 us  [move(): return lax.ppermute(values, AXES, sorted(pairs))]
    unnamed x10 -> x8, local copies, waits for them, and re-layouts: 4.14 us -> 0.42 us
    convert_element_type x1 -> x0, other arithmetic: 1.38 us -> none  [on_device(): (partner_grad + cross[1].astype(jnp.float32)).astype(jnp.bfloat16)]
    pallas_call x4 -> x11, Pallas kernels: 18.1 us -> 19 us  [the longest x3 6.58 us: against(): pl.pallas_call(text_kernel, grid=(1,), in_specs=[SMEM, SMEM, pl.BlockSpec...]
  transfers between devices with their start and end apart: 9 -> 12, of which waited for: 5 -> 2; matrix products, arithmetic and copies ran while one was open for 1% -> 1% of each run, Pallas kernels for 3% -> 15%
where the time goes in v2:
time: 106 us; the launch traced here: 105 us
  starting transfers between devices  60.1 us (57%)
  waiting for transfers between devices  22.3 us (21%)
  Pallas kernels  19 us (18%)
  between operations  2.1 us (2%)
  local copies, waits for them, and re-layouts  1.52 us (1%)
    ppermute x12, starting transfers between devices, move(): return lax.ppermute(values, AXES, sorted(pairs))  60.1 us
    ppermute x12, waiting for transfers between devices, move(): return lax.ppermute(values, AXES, sorted(pairs))  22.3 us
    pallas_call x3, Pallas kernels, against(): pl.pallas_call(text_kernel, grid=(1,), in_specs=[SMEM, SMEM, pl.BlockSpec...  6.58 us
    pallas_call x2, Pallas kernels, finish(): pl.pallas_call(functools.partial(final_kernel, [len(pieces) for pieces in...  5.54 us
    pallas_call x4, Pallas kernels, image_sum(): pl.pallas_call(functools.partial(image_kernel, len(sources)), grid=(1,),...  3.24 us
  transfers between devices with their start and end apart: 12, of which 2 were waited for; matrix products, arithmetic and copies ran while one was open for 1% of the time, Pallas kernels for 15%

profile of v2, /device:TPU:1, one launch (start us, length us, event | category | flops | bytes accessed | tf_op | source)
XLA Modules:
  0.0 105.1 jit_solution(6391825484351315278)
XLA Ops:
  0.6 5.0 %collective-permute-start.9 = (bf16[384,768]{1,0:T(8,128)(2,1)}, bf16[384,768]{1,0:T(8,128)(2,1)S(1)}, u32[]{:S(2)}, u32[]{:S(2)}) collective-permute-start(bf16[384,768]{1,0:T(8,128)(2,1)} %refs_0_.4), channel_id=1, source_target_pairs={{0,1},{1,0},{2,3},{3,2},{4,5},{5,4},{6,7},{7,6},{8,9},{9,8},{10,11... | collective-permute-start | bytes 1769480 | tf_op jit(solution)/shard_map/ppermute | solution.py:51
  5.6 5.9 %collective-permute-start.10 = (bf16[384,768]{1,0:T(8,128)(2,1)}, bf16[384,768]{1,0:T(8,128)(2,1)S(1)}, u32[]{:S(2)}, u32[]{:S(2)}) collective-permute-start(bf16[384,768]{1,0:T(8,128)(2,1)} %refs_0_.4), channel_id=1, source_target_pairs={{0,32},{1,33},{2,34},{3,35},{4,36},{5,37},{6,38},{7,39},{8,40},{9,... | collective-permute-start | bytes 1769480 | tf_op jit(solution)/shard_map/ppermute | solution.py:51
  11.5 1.9 %collective-permute-start.12 = (bf16[384,768]{1,0:T(8,128)(2,1)}, bf16[384,768]{1,0:T(8,128)(2,1)S(1)}, u32[]{:S(2)}, u32[]{:S(2)}) collective-permute-start(bf16[384,768]{1,0:T(8,128)(2,1)} %refs_0_.5), channel_id=1, source_target_pairs={{0,0},{1,1},{2,2},{3,3},{4,4},{5,5},{6,6},{7,7},{8,8},{9,9},{10,10... | collective-permute-start | bytes 1769480 | tf_op jit(solution)/shard_map/ppermute | solution.py:51
  13.4 1.1 %fusion = (bf16[192,768]{1,0:T(8,128)(2,1)S(1)}, bf16[192,768]{1,0:T(8,128)(2,1)S(1)}) fusion(bf16[384,768]{1,0:T(8,128)(2,1)} %refs_0_.5), kind=kLoop, calls=%fused_computation | loop fusion | bytes 1179648 | tf_op jit(solution)/shard_map/slice | solution.py:152
  14.5 1.9 %collective-permute-start.11 = (bf16[192,768]{1,0:T(8,128)(2,1)S(1)}, bf16[192,768]{1,0:T(8,128)(2,1)S(1)}, u32[]{:S(2)}, u32[]{:S(2)}) collective-permute-start(bf16[192,768]{1,0:T(8,128)(2,1)S(1)} %get-tuple-element.83), channel_id=1, source_target_pairs={{0,64},{1,65},{2,66},{3,67},{4,68},{5,69},{6,70},{7,71},{8,72},{9,... | collective-permute-start | bytes 884744 | tf_op jit(solution)/shard_map/ppermute | solution.py:51
  16.5 8.1 %collective-permute-start.8 = (bf16[192,768]{1,0:T(8,128)(2,1)S(1)}, bf16[192,768]{1,0:T(8,128)(2,1)S(1)}, u32[]{:S(2)}, u32[]{:S(2)}) collective-permute-start(bf16[192,768]{1,0:T(8,128)(2,1)S(1)} %get-tuple-element.84), channel_id=1, source_target_pairs={{0,64},{1,65},{2,66},{3,67},{4,68},{5,69},{6,70},{7,71},{8,72},{9,... | collective-permute-start | bytes 884744 | tf_op jit(solution)/shard_map/ppermute | solution.py:51
  25.9 4.0 %conditional.2 = (bf16[384,768]{1,0:T(8,128)(2,1)}) conditional(s32[]{:T(128)} %bitcast, bf16[384,768]{1,0:T(8,128)(2,1)S(1)} %collective-permute-done.9.refs_1_.partner_ref, bf16[384,768]{1,0:T(8,128)(2,1)S(1)} %collective-permute-done.9.refs_1_.partner_ref), branch_computations={%region_0.0_spmd, %region_1.0_spmd} | conditional | bytes 2359344 | solution.py:161
  25.9 1.9 %collective-permute-start.1 = (bf16[384,768]{1,0:T(8,128)(2,1)S(1)}, bf16[384,768]{1,0:T(8,128)(2,1)}, u32[]{:S(2)}, u32[]{:S(2)}) collective-permute-start(bf16[384,768]{1,0:T(8,128)(2,1)S(1)} %param.1), channel_id=1, source_target_pairs={{0,32},{1,33},{2,34},{3,35},{4,36},{5,37},{6,38},{7,39},{8,40},{9,... | collective-permute-start | bytes 1769480 | tf_op jit(solution)/shard_map/cond/branch_1_fun/ppermute | solution.py:51
  27.9 2.1 %collective-permute-done.1 = bf16[384,768]{1,0:T(8,128)(2,1)} collective-permute-done((bf16[384,768]{1,0:T(8,128)(2,1)S(1)}, bf16[384,768]{1,0:T(8,128)(2,1)}, u32[]{:S(2)}, u32[]{:S(2)}) %collective-permute-start.1) | collective-permute-done | bytes 589856 | tf_op jit(solution)/shard_map/cond/branch_1_fun/ppermute | solution.py:51
  30.0 1.8 %shard_map.59.images_ref = bf16[4,384,768]{2,1,0:T(8,128)(2,1)S(1)} custom-call(bf16[384,768]{1,0:T(8,128)(2,1)S(1)} %copy-done, bf16[384,768]{1,0:T(8,128)(2,1)S(1)} %collective-permute-done.9.refs_1_.partner_ref, bf16[384,768]{1,0:T(8,128)(2,1)S(1)} %collective-permute-done.10.refs_2_, bf16[384,768]{1,0:T(8,128)(2,1)} %get-tuple-element.89.refs_3_), custom_call_target="tpu_custom_call" | custom-call | tf_op jit(solution)/shard_map/pallas_call | solution.py:171
  31.8 2.2 %shard_map.64 = (bf16[384,768]{1,0:T(8,128)(2,1)}, bf16[2,384,384]{2,1,0:T(8,128)(2,1)S(1)}, bf16[384,768]{1,0:T(8,128)(2,1)S(1)}) custom-call(f32[1]{0:T(128)S(6)} %copy.12.scale_ref, f32[1]{0:T(128)S(6)} %copy.13.bias_ref, bf16[384,768]{1,0:T(8,128)(2,1)S(1)} %collective-permute-done.12.text_ref, bf16[4,384,768]{2,1,0:T(8,128)(2,1)S(1)} %shard_map.59.images_ref), custom_call_target="tpu_custom_call" | custom-call | tf_op jit(solution)/shard_map/pallas_call | solution.py:181
  34.0 10.7 %collective-permute-start.15 = (bf16[384,768]{1,0:T(8,128)(2,1)}, bf16[384,768]{1,0:T(8,128)(2,1)}, u32[]{:S(2)}, u32[]{:S(2)}) collective-permute-start(bf16[384,768]{1,0:T(8,128)(2,1)} %get-tuple-element.82), channel_id=1, source_target_pairs={{0,0},{1,1},{2,2},{3,3},{4,4},{5,5},{6,6},{7,7},{8,8},{9,9},{10,10... | collective-permute-start | bytes 1769480 | tf_op jit(solution)/shard_map/ppermute | solution.py:51
  44.7 2.2 %shard_map.61 = (bf16[192,768]{1,0:T(8,128)(2,1)}, bf16[4,192,384]{2,1,0:T(8,128)(2,1)S(1)}, bf16[192,768]{1,0:T(8,128)(2,1)S(1)}) custom-call(f32[1]{0:T(128)S(6)} %copy.12.scale_ref, f32[1]{0:T(128)S(6)} %copy.13.bias_ref, bf16[192,768]{1,0:T(8,128)(2,1)S(1)} %collective-permute-done.11.text_ref, bf16[4,384,768]{2,1,0:T(8,128)(2,1)S(1)} %shard_map.59.images_ref), custom_call_target="tpu_custom_call" | custom-call | tf_op jit(solution)/shard_map/pallas_call | solution.py:181
  46.9 16.5 %collective-permute-start.14 = (bf16[192,768]{1,0:T(8,128)(2,1)}, bf16[192,768]{1,0:T(8,128)(2,1)}, u32[]{:S(2)}, u32[]{:S(2)}) collective-permute-start(bf16[192,768]{1,0:T(8,128)(2,1)} %get-tuple-element.81), channel_id=1, source_target_pairs={{0,449},{1,448},{2,451},{3,450},{4,453},{5,452},{6,455},{7,454},{8... | collective-permute-start | bytes 884744 | tf_op jit(solution)/shard_map/ppermute | solution.py:51
  63.4 2.2 %shard_map.60 = (bf16[192,768]{1,0:T(8,128)(2,1)}, bf16[4,192,384]{2,1,0:T(8,128)(2,1)S(1)}, bf16[192,768]{1,0:T(8,128)(2,1)S(1)}) custom-call(f32[1]{0:T(128)S(6)} %copy.12.scale_ref, f32[1]{0:T(128)S(6)} %copy.13.bias_ref, bf16[192,768]{1,0:T(8,128)(2,1)S(1)} %collective-permute-done.8.text_ref, bf16[4,384,768]{2,1,0:T(8,128)(2,1)S(1)} %shard_map.59.images_ref), custom_call_target="tpu_custom_call" | custom-call | tf_op jit(solution)/shard_map/pallas_call | solution.py:181
  65.6 1.9 %collective-permute-start.13 = (bf16[192,768]{1,0:T(8,128)(2,1)}, bf16[192,768]{1,0:T(8,128)(2,1)}, u32[]{:S(2)}, u32[]{:S(2)}) collective-permute-start(bf16[192,768]{1,0:T(8,128)(2,1)} %get-tuple-element.80), channel_id=1, source_target_pairs={{0,449},{1,448},{2,451},{3,450},{4,453},{5,452},{6,455},{7,454},{8... | collective-permute-start | bytes 884744 | tf_op jit(solution)/shard_map/ppermute | solution.py:51
  69.6 1.9 %shard_map.62 = (f32[384,768]{1,0:T(8,128)S(1)}, bf16[2,384,384]{2,1,0:T(8,128)(2,1)S(1)}, bf16[384,768]{1,0:T(8,128)(2,1)S(1)}) custom-call(f32[1]{0:T(128)S(6)} %copy.12.scale_ref, f32[1]{0:T(128)S(6)} %copy.13.bias_ref, bf16[384,768]{1,0:T(8,128)(2,1)S(1)} %copy-done.1, bf16[384,768]{1,0:T(8,128)(2,1)S(1)} %copy-done, bf16[384,768]{1,0:T(8,128)(2,1)S(1)} %copy-done.3), custom_call_target="tpu_custom_call" | custom-call | tf_op jit(solution)/shard_map/pallas_call | solution.py:163
  72.3 27.3 %conditional.3 = (bf16[384,768]{1,0:T(8,128)(2,1)}, bf16[384,768]{1,0:T(8,128)(2,1)}) conditional(s32[]{:T(128)} %bitcast, (bf16[384,768]{1,0:T(8,128)(2,1)S(1)}, bf16[384,768]{1,0:T(8,128)(2,1)S(1)}, bf16[4,192,384]{2,1,0:T(8,128)(2,1)S(1)}, bf16[4,192,384]{2,1,0:T(8,128)(2,1)S(1)}, bf16[2,384,384]{2,1,0:T(8,128)(2,1)S(1)}, ...), branch_computations={%region_2.0_spmd, %region_3.0_spmd} | conditional | bytes 7078024 | solution.py:234
  72.3 1.9 %collective-permute-start.6 = (bf16[384,768]{1,0:T(8,128)(2,1)S(1)}, bf16[384,768]{1,0:T(8,128)(2,1)S(1)}, u32[]{:S(2)}, u32[]{:S(2)}) collective-permute-start(bf16[384,768]{1,0:T(8,128)(2,1)S(1)} %get-tuple-element.52), channel_id=1, source_target_pairs={{0,32},{1,33},{2,34},{3,35},{4,36},{5,37},{6,38},{7,39},{8,40},{9,... | collective-permute-start | bytes 1769480 | tf_op jit(solution)/shard_map/cond/branch_1_fun/ppermute | solution.py:51
  74.2 2.4 %collective-permute-start.5 = (bf16[384,768]{1,0:T(8,128)(2,1)S(1)}, bf16[384,768]{1,0:T(8,128)(2,1)}, u32[]{:S(2)}, u32[]{:S(2)}) collective-permute-start(bf16[384,768]{1,0:T(8,128)(2,1)S(1)} %get-tuple-element.45), channel_id=1, source_target_pairs={{0,32},{1,33},{2,34},{3,35},{4,36},{5,37},{6,38},{7,39},{8,40},{9,... | collective-permute-start | bytes 1769480 | tf_op jit(solution)/shard_map/cond/branch_1_fun/ppermute | solution.py:51
  77.5 1.9 %collective-permute-start.7 = (bf16[384,768]{1,0:T(8,128)(2,1)S(1)}, bf16[384,768]{1,0:T(8,128)(2,1)}, u32[]{:S(2)}, u32[]{:S(2)}) collective-permute-start(bf16[384,768]{1,0:T(8,128)(2,1)S(1)} %branch_1_fun.1), channel_id=1, source_target_pairs={{0,1},{1,0},{2,3},{3,2},{4,5},{5,4},{6,7},{7,6},{8,9},{9,8},{10,11... | collective-permute-start | bytes 1769480 | tf_op jit(solution)/shard_map/cond/branch_1_fun/ppermute | solution.py:51
  79.4 20.2 %collective-permute-done.7 = bf16[384,768]{1,0:T(8,128)(2,1)} collective-permute-done((bf16[384,768]{1,0:T(8,128)(2,1)S(1)}, bf16[384,768]{1,0:T(8,128)(2,1)}, u32[]{:S(2)}, u32[]{:S(2)}) %collective-permute-start.7) | collective-permute-done | bytes 589856 | tf_op jit(solution)/shard_map/cond/branch_1_fun/ppermute | solution.py:51
  99.6 2.8 %shard_map.67 = f32[384,768]{1,0:T(8,128)} custom-call(bf16[384,768]{1,0:T(8,128)(2,1)S(1)} %copy-done, f32[384,768]{1,0:T(8,128)S(1)} %shard_map.63.refs_1_, bf16[384,768]{1,0:T(8,128)(2,1)} %get-tuple-element.77.refs_2_, bf16[384,768]{1,0:T(8,128)(2,1)} %get-tuple-element.78.refs_3_), custom_call_target="tpu_custom_call" | custom-call | tf_op jit(solution)/shard_map/pallas_call | solution.py:137
  102.4 2.8 %shard_map.68 = f32[384,768]{1,0:T(8,128)} custom-call(bf16[384,768]{1,0:T(8,128)(2,1)S(1)} %copy-done.1, f32[384,768]{1,0:T(8,128)S(1)} %get-tuple-element.79.refs_1_, bf16[192,768]{1,0:T(8,128)(2,1)} %collective-permute-done.13.refs_2_, bf16[192,768]{1,0:T(8,128)(2,1)} %collective-permute-done.14.refs_3_, bf16[384,768]{1,0:T(8,128)(2,1)} %collective-permute-done.15.refs_4_), custom_call_target="tpu_custom_call" | custom-call | tf_op jit(solution)/shard_map/pallas_call | solution.py:137
  (22 shorter events, 3.7 us)
Async XLA Ops:
  0.6 29.4 %copy-start = (bf16[384,768]{1,0:T(8,128)(2,1)S(1)}, bf16[384,768]{1,0:T(8,128)(2,1)}, u32[]{:S(2)}) copy-start(bf16[384,768]{1,0:T(8,128)(2,1)} %refs_0_.4) | copy-start | bytes 1769476
  0.6 25.3 %collective-permute-start.9 = (bf16[384,768]{1,0:T(8,128)(2,1)}, bf16[384,768]{1,0:T(8,128)(2,1)S(1)}, u32[]{:S(2)}, u32[]{:S(2)}) collective-permute-start(bf16[384,768]{1,0:T(8,128)(2,1)} %refs_0_.4), channel_id=1, source_target_pairs={{0,1},{1,0},{2,3},{3,2},{4,5},{5,4},{6,7},{7,6},{8,9},{9,8},{10,11... | collective-permute-start | bytes 1769480 | tf_op jit(solution)/shard_map/ppermute | solution.py:51
  5.6 24.4 %collective-permute-start.10 = (bf16[384,768]{1,0:T(8,128)(2,1)}, bf16[384,768]{1,0:T(8,128)(2,1)S(1)}, u32[]{:S(2)}, u32[]{:S(2)}) collective-permute-start(bf16[384,768]{1,0:T(8,128)(2,1)} %refs_0_.4), channel_id=1, source_target_pairs={{0,32},{1,33},{2,34},{3,35},{4,36},{5,37},{6,38},{7,39},{8,40},{9,... | collective-permute-start | bytes 1769480 | tf_op jit(solution)/shard_map/ppermute | solution.py:51
  11.5 20.3 %collective-permute-start.12 = (bf16[384,768]{1,0:T(8,128)(2,1)}, bf16[384,768]{1,0:T(8,128)(2,1)S(1)}, u32[]{:S(2)}, u32[]{:S(2)}) collective-permute-start(bf16[384,768]{1,0:T(8,128)(2,1)} %refs_0_.5), channel_id=1, source_target_pairs={{0,0},{1,1},{2,2},{3,3},{4,4},{5,5},{6,6},{7,7},{8,8},{9,9},{10,10... | collective-permute-start | bytes 1769480 | tf_op jit(solution)/shard_map/ppermute | solution.py:51
  14.5 30.2 %collective-permute-start.11 = (bf16[192,768]{1,0:T(8,128)(2,1)S(1)}, bf16[192,768]{1,0:T(8,128)(2,1)S(1)}, u32[]{:S(2)}, u32[]{:S(2)}) collective-permute-start(bf16[192,768]{1,0:T(8,128)(2,1)S(1)} %get-tuple-element.83), channel_id=1, source_target_pairs={{0,64},{1,65},{2,66},{3,67},{4,68},{5,69},{6,70},{7,71},{8,72},{9,... | collective-permute-start | bytes 884744 | tf_op jit(solution)/shard_map/ppermute | solution.py:51
  16.5 46.9 %collective-permute-start.8 = (bf16[192,768]{1,0:T(8,128)(2,1)S(1)}, bf16[192,768]{1,0:T(8,128)(2,1)S(1)}, u32[]{:S(2)}, u32[]{:S(2)}) collective-permute-start(bf16[192,768]{1,0:T(8,128)(2,1)S(1)} %get-tuple-element.84), channel_id=1, source_target_pairs={{0,64},{1,65},{2,66},{3,67},{4,68},{5,69},{6,70},{7,71},{8,72},{9,... | collective-permute-start | bytes 884744 | tf_op jit(solution)/shard_map/ppermute | solution.py:51
  25.9 5.9 %copy-start.2 = (bf16[384,768]{1,0:T(8,128)(2,1)}, bf16[384,768]{1,0:T(8,128)(2,1)S(1)}, u32[]{:S(2)}) copy-start(bf16[384,768]{1,0:T(8,128)(2,1)S(1)} %collective-permute-done.9.refs_1_.partner_ref) | copy-start | bytes 1769476
  25.9 4.0 %collective-permute-start.1 = (bf16[384,768]{1,0:T(8,128)(2,1)S(1)}, bf16[384,768]{1,0:T(8,128)(2,1)}, u32[]{:S(2)}, u32[]{:S(2)}) collective-permute-start(bf16[384,768]{1,0:T(8,128)(2,1)S(1)} %param.1), channel_id=1, source_target_pairs={{0,32},{1,33},{2,34},{3,35},{4,36},{5,37},{6,38},{7,39},{8,40},{9,... | collective-permute-start | bytes 1769480 | tf_op jit(solution)/shard_map/cond/branch_1_fun/ppermute | solution.py:51
  34.0 68.4 %collective-permute-start.15 = (bf16[384,768]{1,0:T(8,128)(2,1)}, bf16[384,768]{1,0:T(8,128)(2,1)}, u32[]{:S(2)}, u32[]{:S(2)}) collective-permute-start(bf16[384,768]{1,0:T(8,128)(2,1)} %get-tuple-element.82), channel_id=1, source_target_pairs={{0,0},{1,1},{2,2},{3,3},{4,4},{5,5},{6,6},{7,7},{8,8},{9,9},{10,10... | collective-permute-start | bytes 1769480 | tf_op jit(solution)/shard_map/ppermute | solution.py:51
  46.9 55.4 %collective-permute-start.14 = (bf16[192,768]{1,0:T(8,128)(2,1)}, bf16[192,768]{1,0:T(8,128)(2,1)}, u32[]{:S(2)}, u32[]{:S(2)}) collective-permute-start(bf16[192,768]{1,0:T(8,128)(2,1)} %get-tuple-element.81), channel_id=1, source_target_pairs={{0,449},{1,448},{2,451},{3,450},{4,453},{5,452},{6,455},{7,454},{8... | collective-permute-start | bytes 884744 | tf_op jit(solution)/shard_map/ppermute | solution.py:51
  65.6 36.7 %collective-permute-start.13 = (bf16[192,768]{1,0:T(8,128)(2,1)}, bf16[192,768]{1,0:T(8,128)(2,1)}, u32[]{:S(2)}, u32[]{:S(2)}) collective-permute-start(bf16[192,768]{1,0:T(8,128)(2,1)} %get-tuple-element.80), channel_id=1, source_target_pairs={{0,449},{1,448},{2,451},{3,450},{4,453},{5,452},{6,455},{7,454},{8... | collective-permute-start | bytes 884744 | tf_op jit(solution)/shard_map/ppermute | solution.py:51
  68.4 1.1 %copy-start.1 = (bf16[384,768]{1,0:T(8,128)(2,1)S(1)}, bf16[384,768]{1,0:T(8,128)(2,1)}, u32[]{:S(2)}) copy-start(bf16[384,768]{1,0:T(8,128)(2,1)} %refs_0_.5) | copy-start | bytes 1769476
  68.4 1.2 %copy-start.3 = (bf16[384,768]{1,0:T(8,128)(2,1)S(1)}, bf16[384,768]{1,0:T(8,128)(2,1)}, u32[]{:S(2)}) copy-start(bf16[384,768]{1,0:T(8,128)(2,1)} %copy-done.2) | copy-start | bytes 1769476
  72.3 4.3 %collective-permute-start.6 = (bf16[384,768]{1,0:T(8,128)(2,1)S(1)}, bf16[384,768]{1,0:T(8,128)(2,1)S(1)}, u32[]{:S(2)}, u32[]{:S(2)}) collective-permute-start(bf16[384,768]{1,0:T(8,128)(2,1)S(1)} %get-tuple-element.52), channel_id=1, source_target_pairs={{0,32},{1,33},{2,34},{3,35},{4,36},{5,37},{6,38},{7,39},{8,40},{9,... | collective-permute-start | bytes 1769480 | tf_op jit(solution)/shard_map/cond/branch_1_fun/ppermute | solution.py:51
  74.2 5.2 %collective-permute-start.5 = (bf16[384,768]{1,0:T(8,128)(2,1)S(1)}, bf16[384,768]{1,0:T(8,128)(2,1)}, u32[]{:S(2)}, u32[]{:S(2)}) collective-permute-start(bf16[384,768]{1,0:T(8,128)(2,1)S(1)} %get-tuple-element.45), channel_id=1, source_target_pairs={{0,32},{1,33},{2,34},{3,35},{4,36},{5,37},{6,38},{7,39},{8,40},{9,... | collective-permute-start | bytes 1769480 | tf_op jit(solution)/shard_map/cond/branch_1_fun/ppermute | solution.py:51
  77.5 22.1 %collective-permute-start.7 = (bf16[384,768]{1,0:T(8,128)(2,1)S(1)}, bf16[384,768]{1,0:T(8,128)(2,1)}, u32[]{:S(2)}, u32[]{:S(2)}) collective-permute-start(bf16[384,768]{1,0:T(8,128)(2,1)S(1)} %branch_1_fun.1), channel_id=1, source_target_pairs={{0,1},{1,0},{2,3},{3,2},{4,5},{5,4},{6,7},{7,6},{8,9},{9,8},{10,11... | collective-permute-start | bytes 1769480 | tf_op jit(solution)/shard_map/cond/branch_1_fun/ppermute | solution.py:51

commit v3 on v0

v3 whole, which is shorter than its diff:
```python
import functools

import jax
import jax.numpy as jnp
from jax import lax
from jax.experimental import pallas as pl
from jax.experimental.pallas import tpu as pltpu
from jax.sharding import PartitionSpec as P

AXES = ("blk", "group")
EPSILON = 1e-06
CHIPS = 4

SMEM = pl.BlockSpec(memory_space=pltpu.SMEM)
WHOLE = pl.BlockSpec(memory_space=pltpu.VMEM)


def params(mib):
    return pltpu.CompilerParams(vmem_limit_bytes=mib * 1024 * 1024)


def near_to(b, g, size):
    to = (b + 2) % size
    return to, g ^ (to // (2 * CHIPS) != b // (2 * CHIPS))


def crossed(b, to):
    return to // (2 * CHIPS) != b // (2 * CHIPS)


def guest_to(b, g, size):
    if b % 2 == 1:
        return None
    to = (b - 1) % size
    return to, g ^ crossed(b, to)


def guest_partner_to(b, g, size):
    if b % 2 == 1:
        return None
    to = (b - 1) % size
    return to, g ^ 1 ^ crossed(b, to)


def far_to(b, g, size):
    return ((b + 3) % size, g ^ 1) if b % 2 == 1 and b // 2 % CHIPS == CHIPS - 2 else None


def inside(where):
    def to(b, g, size):
        end = where(b, g, size)
        return end if b % 2 == 0 and b // 2 % CHIPS > 0 else None

    return to


def other_core(b, g, size):
    return b ^ 1, g


def partner(b, g, size):
    return b, g ^ 1


def move(values, where, inverse=False):
    n_blk, n_group = lax.axis_size("blk"), lax.axis_size("group")
    pairs = []
    for b in range(n_blk):
        for g in range(n_group):
            to = where(b, g, n_blk)
            if to is not None:
                pair = (b * n_group + g, to[0] * n_group + to[1])
                pairs.append(pair[::-1] if inverse else pair)
    return lax.ppermute(values, AXES, sorted(pairs))


def normalize(values):
    full = values.astype(jnp.float32)
    inverse = lax.rsqrt(jnp.sum(full * full, axis=-1, keepdims=True) + EPSILON)
    return full * inverse, inverse


def hat(values):
    return normalize(values)[0].astype(jnp.bfloat16)


def dot(left, right, left_dim, right_dim):
    return lax.dot_general(
        left, right, (((left_dim,), (right_dim,)), ((), ())), preferred_element_type=jnp.float32
    )


def slopes_of(text_hat, image_hat, scale, bias, same=None):
    chance = jax.nn.sigmoid(scale * dot(text_hat, image_hat, 1, 1) + bias)
    if same is not None:
        chance = chance - same
    return (scale * chance).astype(jnp.bfloat16)


def rows_of(ref):
    count, rows, width = ref.shape
    return ref[...].reshape(count * rows, width)


def is_odd(role):
    return role[0] == 1


def takes_far(role):
    return jnp.logical_and(role[0] == 0, role[1] == 0)


def hats_kernel(image_ref, partner_ref, hats_ref):
    hats_ref[0] = hat(image_ref[...])
    hats_ref[1] = hat(partner_ref[...])


def own_kernel(
    role, scale_ref, bias_ref, text_ref, mine_ref, text_sum_ref, mine_sum_ref, partner_sum_ref,
):
    scale, bias = scale_ref[0], bias_ref[0]
    rows, width = text_ref.shape
    text_hat = hat(text_ref[...])
    same = (
        lax.broadcasted_iota(jnp.int32, (rows, 2 * rows), 0)
        == lax.broadcasted_iota(jnp.int32, (rows, 2 * rows), 1)
    ).astype(jnp.float32)
    images = rows_of(mine_ref)
    slopes = slopes_of(text_hat, images, scale, bias, same)
    text_sum_ref[...] = dot(slopes, images, 1, 0)
    mine_sum_ref[...] = dot(slopes[:, :rows], text_hat, 0, 0)
    partner_sum_ref[...] = dot(slopes[:, rows:], text_hat, 0, 0)


def near_kernel(
    role, scale_ref, bias_ref, text_ref, mine_ref, theirs_ref, guest_ref, guest_partner_ref, far_ref,
    grad_ref, slopes_ref, hat_ref, guest_slopes_ref, back_partner_ref, far_slopes_ref, far_hat_ref,
    images_ref,
):
    scale, bias = scale_ref[0], bias_ref[0]
    rows, width = text_ref.shape
    hat_ref[...] = hat(text_ref[...])
    for slot in range(2):
        images_ref[slot] = mine_ref[slot]
        images_ref[2 + slot] = theirs_ref[slot]

    @pl.when(role[0] == 0)
    def _():
        images = images_ref[:4].reshape(4 * rows, width)
        slopes = slopes_of(hat_ref[...], images, scale, bias)
        slopes_ref[...] = slopes
        grad_ref[...] = dot(slopes, images, 1, 0).astype(grad_ref.dtype)

    @pl.when(role[0] == 1)
    def _():
        images_ref[4] = hat(guest_ref[...])
        images_ref[5] = hat(guest_partner_ref[...])
        images = rows_of(images_ref)
        near_hat = hat_ref[...]
        slopes = slopes_of(near_hat, images, scale, bias)
        grad_ref[...] = dot(slopes, images, 1, 0).astype(grad_ref.dtype)
        slopes_ref[...] = slopes[:, : 4 * rows]
        guest_slopes_ref[...] = slopes[:, 4 * rows : 5 * rows]
        back_partner_ref[...] = dot(slopes[:, 5 * rows :], near_hat, 0, 0).astype(back_partner_ref.dtype)

    @pl.when(takes_far(role))
    def _():
        text_hat = hat(far_ref[...])
        far_hat_ref[...] = text_hat
        far_slopes_ref[...] = slopes_of(text_hat, rows_of(mine_ref), scale, bias)


def theirs_kernel(
    role, scale_ref, bias_ref, slopes_ref, hat_ref, text_ref, theirs_ref, text_sum_ref, guest_slopes_ref,
    cross_ref, text_sum_out, back_ref,
):
    rows, width = text_ref.shape
    near_hat = hat_ref[...]

    @pl.when(role[0] == 0)
    def _():
        text_hat = hat(text_ref[...])
        images = rows_of(theirs_ref)
        own = slopes_of(text_hat, images, scale_ref[0], bias_ref[0])
        text_sum_out[...] = text_sum_ref[...] + dot(own, images, 1, 0)
        for slot in range(2):
            at = slice((2 + slot) * rows, (3 + slot) * rows)
            total = dot(slopes_ref[:, at], hat_ref[...], 0, 0)
            total = total + dot(own[:, slot * rows : (slot + 1) * rows], text_hat, 0, 0)
            cross_ref[slot] = total.astype(cross_ref.dtype)

    @pl.when(role[0] == 1)
    def _():
        text_sum_out[...] = text_sum_ref[...]
        for slot in range(2):
            at = slice((2 + slot) * rows, (3 + slot) * rows)
            cross_ref[slot] = dot(slopes_ref[:, at], hat_ref[...], 0, 0).astype(cross_ref.dtype)
        back_ref[...] = dot(guest_slopes_ref[...], hat_ref[...], 0, 0).astype(back_ref.dtype)


def partner_kernel(role, slopes_ref, hat_ref, far_slopes_ref, far_hat_ref, sum_ref, cross_ref, back_ref, out_ref, total):
    rows = hat_ref.shape[0]
    even = 1.0 - is_odd(role).astype(jnp.float32)
    total[...] = (
        dot(slopes_ref[:, rows : 2 * rows], hat_ref[...], 0, 0)
        + sum_ref[...]
        + cross_ref[0].astype(jnp.float32)
        + even * back_ref[...].astype(jnp.float32)
    )

    @pl.when(takes_far(role))
    def _():
        total[...] += dot(far_slopes_ref[:, rows:], far_hat_ref[...], 0, 0)

    out_ref[...] = total[...].astype(out_ref.dtype)


def mine_kernel(role, slopes_ref, hat_ref, far_slopes_ref, far_hat_ref, sum_ref, cross_ref, out_ref, total):
    rows = hat_ref.shape[0]
    out_ref[...] = (
        dot(slopes_ref[:, :rows], hat_ref[...], 0, 0) + sum_ref[...] + cross_ref[0].astype(jnp.float32)
    )

    @pl.when(takes_far(role))
    def _():
        out_ref[...] += dot(far_slopes_ref[:, :rows], far_hat_ref[...], 0, 0)


def project(raw, total):
    unit, inverse = normalize(raw)
    return (total - unit * jnp.sum(unit * total, axis=-1, keepdims=True)) * inverse


def text_final_kernel(role, texts, text_sum, near_back, role_out, out_ref):
    role_out[0] = role[0]
    out_ref[...] = project(texts[...], text_sum[...] + near_back[...].astype(jnp.float32))


def image_final_kernel(role, images, image_sum, from_partner, back, out_ref):
    even = 1.0 - is_odd(role).astype(jnp.float32)
    total = image_sum[...] + from_partner[...].astype(jnp.float32) + even * back[...].astype(jnp.float32)
    out_ref[...] = project(images[...], total)


def call(kernel, out_shape, *operands, mib=16, scalars=3, scalar_outs=0, scratch=()):
    outs = out_shape if isinstance(out_shape, list) else [out_shape]
    out_specs = [SMEM] * scalar_outs + [WHOLE] * (len(outs) - scalar_outs)
    return pl.pallas_call(
        kernel,
        in_specs=[SMEM] * scalars + [WHOLE] * (len(operands) - scalars),
        out_specs=out_specs if isinstance(out_shape, list) else out_specs[0],
        out_shape=out_shape,
        scratch_shapes=list(scratch),
        compiler_params=params(mib),
    )(*operands)


def on_device(images, texts, logit_scale, logit_bias):
    rows, width = images.shape
    bf16 = functools.partial(jax.ShapeDtypeStruct, dtype=jnp.bfloat16)
    full = jax.ShapeDtypeStruct((rows, width), jnp.float32)
    half = bf16((rows, width))
    half_pair = bf16((2, rows, width))

    index = lax.axis_index("blk")
    role = jnp.stack([index % 2, index // 2 % CHIPS]).astype(jnp.int32)
    scalars = (role, logit_scale, logit_bias)
    positive = logit_scale[0] > 0

    def together(body, *operands):
        return lax.cond(positive, body, body, *operands)

    partner_images = move(images, partner)
    near = move(texts, near_to)
    guest = move(images, guest_to)
    guest_partner = move(images, guest_partner_to)
    far = move(texts, far_to)
    mine = call(hats_kernel, half_pair, images, partner_images, scalars=0)
    theirs = together(lambda values: move(values, other_core), mine)
    text_sum, mine_sum, partner_sum = call(own_kernel, [full, full, full], *scalars, texts, mine)
    near_grad, slopes, near_hat, guest_slopes, back_partner, far_slopes, far_hat = call(
        near_kernel,
        [half, bf16((rows, 4 * rows)), half, bf16((rows, rows)), half, bf16((rows, 2 * rows)), half],
        *scalars, near, mine, theirs, guest, guest_partner, far,
        scratch=[pltpu.VMEM((6, rows, width), jnp.bfloat16)],
        mib=24,
    )
    near_back = move(near_grad, near_to, True)
    back_partner = move(back_partner, inside(guest_to), True)
    cross, text_sum, back = call(
        theirs_kernel,
        [half_pair, full, half],
        *scalars, slopes, near_hat, texts, theirs, text_sum, guest_slopes,
    )

    def sum_with_cross(kernel, slot, dtype, *operands):
        specs = []
        for operand in operands:
            if operand.shape == (2,):
                specs.append(SMEM)
            elif operand.ndim == 3:
                specs.append(pl.BlockSpec((1, rows, width), lambda i: (slot, 0, 0)))
            else:
                specs.append(pl.BlockSpec(operand.shape, lambda i: (0, 0)))
        return pl.pallas_call(
            kernel,
            grid=(1,),
            in_specs=specs,
            out_specs=pl.BlockSpec((rows, width), lambda i: (0, 0)),
            out_shape=jax.ShapeDtypeStruct((rows, width), dtype),
            scratch_shapes=[pltpu.VMEM((rows, width), jnp.float32)],
            compiler_params=params(20),
        )(*operands)

    def across(cross, role, slopes, near_hat, far_slopes, far_hat, partner_sum, back_partner):
        cross = move(cross, other_core)
        return cross, sum_with_cross(
            partner_kernel, 1, jnp.bfloat16,
            role, slopes, near_hat, far_slopes, far_hat, partner_sum, cross, back_partner,
        )

    cross, for_partner = together(
        across, cross, role, slopes, near_hat, far_slopes, far_hat, partner_sum, back_partner
    )
    from_partner = move(for_partner, partner)
    back = together(lambda values: move(values, inside(guest_to), True), back)
    image_sum = sum_with_cross(
        mine_kernel, 0, jnp.float32, role, slopes, near_hat, far_slopes, far_hat, mine_sum, cross
    )
    role, text_grad = call(
        text_final_kernel,
        [jax.ShapeDtypeStruct((2,), jnp.int32), full],
        role, texts, text_sum, near_back,
        scalars=1, scalar_outs=1,
    )
    image_grad = call(image_final_kernel, full, role, images, image_sum, from_partner, back, scalars=1)
    return image_grad, text_grad


def solution(mesh):
    return jax.shard_map(
        on_device,
        mesh=mesh,
        in_specs=(P(AXES, None), P(AXES, None), P(), P()),
        out_specs=(P(AXES, None), P(AXES, None)),
        check_vma=False,
    )
```

time: 345 us -> 99.2 us (0.29)
  the two profiles are of different devices: /device:TPU:184 before, /device:TPU:1 now
where the time goes in v3:
time: 99.2 us; the launch traced here: 98.6 us
  starting transfers between devices  50 us (50%)
  Pallas kernels  22.5 us (23%)
  waiting for transfers between devices  21.5 us (22%)
  between operations  2.14 us (2%)
  local copies, waits for them, and re-layouts  2.1 us (2%)
    ppermute x11, starting transfers between devices, move(): return lax.ppermute(values, AXES, sorted(pairs))  50 us
    ppermute x11, waiting for transfers between devices, move(): return lax.ppermute(values, AXES, sorted(pairs))  21.5 us
    pallas_call x6, Pallas kernels, call(): pl.pallas_call(kernel, in_specs=[SMEM] * scalars + [WHOLE] * (len(operand...  17.6 us
    pallas_call x2, Pallas kernels, sum_with_cross(): pl.pallas_call(kernel, grid=(1,), in_specs=specs, out_specs=pl.BlockSpec(...  4.96 us
    unnamed x18, local copies, waits for them, and re-layouts  2.1 us
  transfers between devices with their start and end apart: 11, of which 5 were waited for; matrix products, arithmetic and copies ran while one was open for 0% of the time, Pallas kernels for 14%

profile of v3, /device:TPU:1, one launch (start us, length us, event | category | flops | bytes accessed | tf_op | source)
XLA Modules:
  0.0 98.6 jit_solution(18050429226736677509)
XLA Ops:
  0.6 4.8 %collective-permute-start.7 = (bf16[384,768]{1,0:T(8,128)(2,1)}, bf16[384,768]{1,0:T(8,128)(2,1)S(1)}, u32[]{:S(2)}, u32[]{:S(2)}) collective-permute-start(bf16[384,768]{1,0:T(8,128)(2,1)} %images.1), channel_id=1, source_target_pairs={{0,1},{1,0},{2,3},{3,2},{4,5},{5,4},{6,7},{7,6},{8,9},{9,8},{10,11... | collective-permute-start | bytes 1769480 | tf_op jit(solution)/shard_map/ppermute | solution.py:74
  5.5 1.3 %collective-permute-start.8 = (bf16[384,768]{1,0:T(8,128)(2,1)}, bf16[384,768]{1,0:T(8,128)(2,1)S(1)}, u32[]{:S(2)}, u32[]{:S(2)}) collective-permute-start(bf16[384,768]{1,0:T(8,128)(2,1)} %images.1), channel_id=1, source_target_pairs={{0,481},{1,480},{2,483},{3,482},{4,485},{5,484},{6,487},{7,486},{8... | collective-permute-start | bytes 1769480 | tf_op jit(solution)/shard_map/ppermute | solution.py:74
  8.8 3.1 %collective-permute-start.6 = (bf16[384,768]{1,0:T(8,128)(2,1)}, bf16[384,768]{1,0:T(8,128)(2,1)S(1)}, u32[]{:S(2)}, u32[]{:S(2)}) collective-permute-start(bf16[384,768]{1,0:T(8,128)(2,1)} %texts.1), channel_id=1, source_target_pairs={{0,64},{1,65},{2,66},{3,67},{4,68},{5,69},{6,70},{7,71},{8,72},{9,... | collective-permute-start | bytes 1769480 | tf_op jit(solution)/shard_map/ppermute | solution.py:74
  13.3 1.4 %collective-permute-done.7.partner_ref = bf16[384,768]{1,0:T(8,128)(2,1)S(1)} collective-permute-done((bf16[384,768]{1,0:T(8,128)(2,1)}, bf16[384,768]{1,0:T(8,128)(2,1)S(1)}, u32[]{:S(2)}, u32[]{:S(2)}) %collective-permute-start.7) | collective-permute-done | bytes 589856 | tf_op jit(solution)/shard_map/ppermute | solution.py:74
  17.1 13.6 %conditional.3 = (bf16[2,384,768]{2,1,0:T(8,128)(2,1)}) conditional(s32[]{:T(128)} %bitcast.2, bf16[2,384,768]{2,1,0:T(8,128)(2,1)S(1)} %shard_map.59.mine_ref, bf16[2,384,768]{2,1,0:T(8,128)(2,1)S(1)} %shard_map.59.mine_ref), branch_computations={%region_0.1_spmd, %region_1.2_spmd} | conditional | bytes 4718640 | solution.py:271
  17.1 11.0 %collective-permute-start.1 = (bf16[2,384,768]{2,1,0:T(8,128)(2,1)S(1)}, bf16[2,384,768]{2,1,0:T(8,128)(2,1)}, u32[]{:S(2)}, u32[]{:S(2)}) collective-permute-start(bf16[2,384,768]{2,1,0:T(8,128)(2,1)S(1)} %param.1), channel_id=1, source_target_pairs={{0,32},{1,33},{2,34},{3,35},{4,36},{5,37},{6,38},{7,39},{8,40},{9,... | collective-permute-start | bytes 3538952 | tf_op jit(solution)/shard_map/cond/branch_1_fun/ppermute | solution.py:74
  28.1 2.6 %collective-permute-done.1 = bf16[2,384,768]{2,1,0:T(8,128)(2,1)} collective-permute-done((bf16[2,384,768]{2,1,0:T(8,128)(2,1)S(1)}, bf16[2,384,768]{2,1,0:T(8,128)(2,1)}, u32[]{:S(2)}, u32[]{:S(2)}) %collective-permute-start.1) | collective-permute-done | bytes 1179680 | tf_op jit(solution)/shard_map/cond/branch_1_fun/ppermute | solution.py:74
  30.7 6.2 %shard_map.60 = (bf16[384,768]{1,0:T(8,128)(2,1)}, bf16[384,1536]{1,0:T(8,128)(2,1)S(1)}, bf16[384,768]{1,0:T(8,128)(2,1)S(1)}, bf16[384,384]{1,0:T(8,128)(2,1)S...) custom-call(s32[2]{0:T(128)S(1)} %pad_add_fusion.role, ...), custom_call_target="tpu_custom_call" | custom-call | tf_op jit(solution)/shard_map/pallas_call | solution.py:248
  37.0 2.0 %collective-permute-start.12 = (bf16[384,768]{1,0:T(8,128)(2,1)S(1)}, bf16[384,768]{1,0:T(8,128)(2,1)S(1)}, u32[]{:S(2)}, u32[]{:S(2)}) collective-permute-start(bf16[384,768]{1,0:T(8,128)(2,1)S(1)} %get-tuple-element.89), channel_id=1, source_target_pairs={{32,64},{33,65},{34,66},{35,67},{36,68},{37,69},{38,70},{39,71},{4... | collective-permute-start | bytes 1769480 | tf_op jit(solution)/shard_map/ppermute | solution.py:74
  39.0 2.5 %shard_map.61 = (f32[384,768]{1,0:T(8,128)S(1)}, f32[384,768]{1,0:T(8,128)S(1)}, f32[384,768]{1,0:T(8,128)S(1)}) custom-call(s32[2]{0:T(128)S(1)} %pad_add_fusion.role, f32[1]{0:T(128)S(6)} %copy.14.scale_ref, f32[1]{0:T(128)S(6)} %copy.15.bias_ref, bf16[384,768]{1,0:T(8,128)(2,1)S(1)} %copy-done, bf16[2,384,768]{2,1,0:T(8,128)(2,1)S(1)} %copy-done.5), custom_call_target="tpu_custom_call" | custom-call | tf_op jit(solution)/shard_map/pallas_call | solution.py:248
  41.5 19.8 %collective-permute-start.11 = (bf16[384,768]{1,0:T(8,128)(2,1)}, bf16[384,768]{1,0:T(8,128)(2,1)}, u32[]{:S(2)}, u32[]{:S(2)}) collective-permute-start(bf16[384,768]{1,0:T(8,128)(2,1)} %get-tuple-element.82), channel_id=1, source_target_pairs={{0,449},{1,448},{2,451},{3,450},{4,453},{5,452},{6,455},{7,454},{8... | collective-permute-start | bytes 1769480 | tf_op jit(solution)/shard_map/ppermute | solution.py:74
  61.3 3.3 %shard_map.62 = (bf16[2,384,768]{2,1,0:T(8,128)(2,1)S(1)}, f32[384,768]{1,0:T(8,128)S(1)}, bf16[384,768]{1,0:T(8,128)(2,1)}) custom-call(s32[2]{0:T(128)S(1)} %pad_add_fusion.role, f32[1]{0:T(128)S(6)} %copy.14.scale_ref, f32[1]{0:T(128)S(6)} %copy.15.bias_ref, bf16[384,1536]{1,0:T(8,128)(2,1)S(1)} %get-tuple-element.77.slopes_ref, ...), custom_call_target="tpu_custom_call" | custom-call | tf_op jit(solution)/shard_map/pallas_call | solution.py:248
  64.6 7.6 %conditional.4 = (bf16[2,384,768]{2,1,0:T(8,128)(2,1)}, bf16[384,768]{1,0:T(8,128)(2,1)}) conditional(s32[]{:T(128)} %bitcast.2, (bf16[2,384,768]{2,1,0:T(8,128)(2,1)S(1)}, s32[2]{0:T(128)S(1)}, bf16[384,1536]{1,0:T(8,128)(2,1)S(1)}, bf16[384,768]{1,0:T(8,128)(2,1)S(1)}, bf16[384,768]{1,0:T(8,128)(2,1)S(1)}, ...), branch_computations={%region_2.3_spmd, %region_3.4_spmd} | conditional | bytes 4718648 | solution.py:271
  64.8 1.9 %collective-permute-start.3 = (bf16[2,384,768]{2,1,0:T(8,128)(2,1)S(1)}, bf16[2,384,768]{2,1,0:T(8,128)(2,1)}, u32[]{:S(2)}, u32[]{:S(2)}) collective-permute-start(bf16[2,384,768]{2,1,0:T(8,128)(2,1)S(1)} %get-tuple-element.50), channel_id=1, source_target_pairs={{0,32},{1,33},{2,34},{3,35},{4,36},{5,37},{6,38},{7,39},{8,40},{9,... | collective-permute-start | bytes 3538952 | tf_op jit(solution)/shard_map/cond/branch_1_fun/ppermute | solution.py:74
  66.8 2.9 %collective-permute-done.3.cross_ref = bf16[2,384,768]{2,1,0:T(8,128)(2,1)} collective-permute-done((bf16[2,384,768]{2,1,0:T(8,128)(2,1)S(1)}, bf16[2,384,768]{2,1,0:T(8,128)(2,1)}, u32[]{:S(2)}, u32[]{:S(2)}) %collective-permute-start.3) | collective-permute-done | bytes 1179680 | tf_op jit(solution)/shard_map/cond/branch_1_fun/ppermute | solution.py:74
  69.7 2.5 %branch_1_fun.1 = bf16[384,768]{1,0:T(8,128)(2,1)} custom-call(s32[2]{0:T(128)S(1)} %get-tuple-element.51.role, bf16[384,1536]{1,0:T(8,128)(2,1)S(1)} %get-tuple-element.52.slopes_ref, bf16[384,768]{1,0:T(8,128)(2,1)S(1)} %get-tuple-element.53.hat_ref, bf16[384,768]{1,0:T(8,128)(2,1)S(1)} %get-tuple-element.54.far_slopes_ref, ...), custom_call_target="tpu_custom_call" | custom-call | tf_op jit(solution)/shard_map/cond/branch_1_fun/pallas_call | solution.py:305
  72.2 1.9 %collective-permute-start.13 = (bf16[384,768]{1,0:T(8,128)(2,1)}, bf16[384,768]{1,0:T(8,128)(2,1)S(1)}, u32[]{:S(2)}, u32[]{:S(2)}) collective-permute-start(bf16[384,768]{1,0:T(8,128)(2,1)} %get-tuple-element.91), channel_id=1, source_target_pairs={{0,1},{1,0},{2,3},{3,2},{4,5},{5,4},{6,7},{7,6},{8,9},{9,8},{10,11... | collective-permute-start | bytes 1769480 | tf_op jit(solution)/shard_map/ppermute | solution.py:74
  74.1 8.4 %conditional.5 = (bf16[384,768]{1,0:T(8,128)(2,1)}) conditional(s32[]{:T(128)} %bitcast.2, bf16[384,768]{1,0:T(8,128)(2,1)} %get-tuple-element.92, bf16[384,768]{1,0:T(8,128)(2,1)} %get-tuple-element.92), branch_computations={%region_4.5_spmd, %region_5.6_spmd} | conditional | bytes 2359344 | solution.py:271
  74.1 2.1 %collective-permute-start.5 = (bf16[384,768]{1,0:T(8,128)(2,1)}, bf16[384,768]{1,0:T(8,128)(2,1)}, u32[]{:S(2)}, u32[]{:S(2)}) collective-permute-start(bf16[384,768]{1,0:T(8,128)(2,1)} %param.5), channel_id=1, source_target_pairs={{32,64},{33,65},{34,66},{35,67},{36,68},{37,69},{38,70},{39,71},{4... | collective-permute-start | bytes 1769480 | tf_op jit(solution)/shard_map/cond/branch_1_fun/ppermute | solution.py:74
  76.3 6.3 %collective-permute-done.5 = bf16[384,768]{1,0:T(8,128)(2,1)} collective-permute-done((bf16[384,768]{1,0:T(8,128)(2,1)}, bf16[384,768]{1,0:T(8,128)(2,1)}, u32[]{:S(2)}, u32[]{:S(2)}) %collective-permute-start.5) | collective-permute-done | bytes 589856 | tf_op jit(solution)/shard_map/cond/branch_1_fun/ppermute | solution.py:74
  82.6 2.5 %shard_map.64.image_sum = f32[384,768]{1,0:T(8,128)S(1)} custom-call(s32[2]{0:T(128)S(1)} %pad_add_fusion.role, bf16[384,1536]{1,0:T(8,128)(2,1)} %copy-done.3, bf16[384,768]{1,0:T(8,128)(2,1)} %copy-done.6, bf16[384,768]{1,0:T(8,128)(2,1)} %copy-done.7, bf16[384,768]{1,0:T(8,128)(2,1)} %copy-done.8, f32[384,768]{1,0:T(8,128)S(1)} %get-tuple-element.86.sum_ref, ...), custom_call_target="tpu_custom_call" | custom-call | tf_op jit(solution)/shard_map/pallas_call | solution.py:305
  85.1 2.6 %shard_map.63 = (s32[2]{0:T(128)S(1)}, f32[384,768]{1,0:T(8,128)}) custom-call(s32[2]{0:T(128)S(1)} %pad_add_fusion.role, bf16[384,768]{1,0:T(8,128)(2,1)S(1)} %copy-done, f32[384,768]{1,0:T(8,128)S(1)} %get-tuple-element.81.text_sum, bf16[384,768]{1,0:T(8,128)(2,1)} %collective-permute-done.11.near_back), custom_call_target="tpu_custom_call" | custom-call | tf_op jit(solution)/shard_map/pallas_call | solution.py:248
  87.7 8.3 %collective-permute-done.13.from_partner = bf16[384,768]{1,0:T(8,128)(2,1)S(1)} collective-permute-done((bf16[384,768]{1,0:T(8,128)(2,1)}, bf16[384,768]{1,0:T(8,128)(2,1)S(1)}, u32[]{:S(2)}, u32[]{:S(2)}) %collective-permute-start.13) | collective-permute-done | bytes 589856 | tf_op jit(solution)/shard_map/ppermute | solution.py:74
  96.0 2.6 %shard_map.65 = f32[384,768]{1,0:T(8,128)} custom-call(s32[2]{0:T(128)S(1)} %get-tuple-element.83.role, bf16[384,768]{1,0:T(8,128)(2,1)S(1)} %copy-done.2, f32[384,768]{1,0:T(8,128)S(1)} %shard_map.64.image_sum, bf16[384,768]{1,0:T(8,128)(2,1)S(1)} %collective-permute-done.13.from_partner, bf16[384,768]{1,0:T(8,128)(2,1)} %get-tuple-element.99.back), custom_call_target="tpu_custom_call" | custom-call | tf_op jit(solution)/shard_map/pallas_call | solution.py:248
  (28 shorter events, 4.5 us)
Async XLA Ops:
  0.6 14.1 %collective-permute-start.7 = (bf16[384,768]{1,0:T(8,128)(2,1)}, bf16[384,768]{1,0:T(8,128)(2,1)S(1)}, u32[]{:S(2)}, u32[]{:S(2)}) collective-permute-start(bf16[384,768]{1,0:T(8,128)(2,1)} %images.1), channel_id=1, source_target_pairs={{0,1},{1,0},{2,3},{3,2},{4,5},{5,4},{6,7},{7,6},{8,9},{9,8},{10,11... | collective-permute-start | bytes 1769480 | tf_op jit(solution)/shard_map/ppermute | solution.py:74
  5.5 25.3 %collective-permute-start.8 = (bf16[384,768]{1,0:T(8,128)(2,1)}, bf16[384,768]{1,0:T(8,128)(2,1)S(1)}, u32[]{:S(2)}, u32[]{:S(2)}) collective-permute-start(bf16[384,768]{1,0:T(8,128)(2,1)} %images.1), channel_id=1, source_target_pairs={{0,481},{1,480},{2,483},{3,482},{4,485},{5,484},{6,487},{7,486},{8... | collective-permute-start | bytes 1769480 | tf_op jit(solution)/shard_map/ppermute | solution.py:74
  6.8 24.0 %collective-permute-start.9 = (bf16[384,768]{1,0:T(8,128)(2,1)}, bf16[384,768]{1,0:T(8,128)(2,1)S(1)}, u32[]{:S(2)}, u32[]{:S(2)}) collective-permute-start(bf16[384,768]{1,0:T(8,128)(2,1)} %images.1), channel_id=1, source_target_pairs={{0,480},{1,481},{2,482},{3,483},{4,484},{5,485},{6,486},{7,487},{8... | collective-permute-start | bytes 1769480 | tf_op jit(solution)/shard_map/ppermute | solution.py:74
  8.1 22.7 %collective-permute-start.10 = (bf16[384,768]{1,0:T(8,128)(2,1)}, bf16[384,768]{1,0:T(8,128)(2,1)S(1)}, u32[]{:S(2)}, u32[]{:S(2)}) collective-permute-start(bf16[384,768]{1,0:T(8,128)(2,1)} %texts.1), channel_id=1, source_target_pairs={{160,257},{161,256},{162,259},{163,258},{164,261},{165,260},{166,2... | collective-permute-start | bytes 1769480 | tf_op jit(solution)/shard_map/ppermute | solution.py:74
  8.8 22.0 %collective-permute-start.6 = (bf16[384,768]{1,0:T(8,128)(2,1)}, bf16[384,768]{1,0:T(8,128)(2,1)S(1)}, u32[]{:S(2)}, u32[]{:S(2)}) collective-permute-start(bf16[384,768]{1,0:T(8,128)(2,1)} %texts.1), channel_id=1, source_target_pairs={{0,64},{1,65},{2,66},{3,67},{4,68},{5,69},{6,70},{7,71},{8,72},{9,... | collective-permute-start | bytes 1769480 | tf_op jit(solution)/shard_map/ppermute | solution.py:74
  14.7 1.1 %copy-start.1 = (bf16[384,768]{1,0:T(8,128)(2,1)S(1)}, bf16[384,768]{1,0:T(8,128)(2,1)}, u32[]{:S(2)}) copy-start(bf16[384,768]{1,0:T(8,128)(2,1)} %images.1) | copy-start | bytes 1769476
  16.1 1.0 %copy-start.4 = (bf16[2,384,768]{2,1,0:T(8,128)(2,1)}, bf16[2,384,768]{2,1,0:T(8,128)(2,1)S(1)}, u32[]{:S(2)}) copy-start(bf16[2,384,768]{2,1,0:T(8,128)(2,1)S(1)} %shard_map.59.mine_ref) | copy-start | bytes 3538948
  17.1 13.6 %collective-permute-start.1 = (bf16[2,384,768]{2,1,0:T(8,128)(2,1)S(1)}, bf16[2,384,768]{2,1,0:T(8,128)(2,1)}, u32[]{:S(2)}, u32[]{:S(2)}) collective-permute-start(bf16[2,384,768]{2,1,0:T(8,128)(2,1)S(1)} %param.1), channel_id=1, source_target_pairs={{0,32},{1,33},{2,34},{3,35},{4,36},{5,37},{6,38},{7,39},{8,40},{9,... | collective-permute-start | bytes 3538952 | tf_op jit(solution)/shard_map/cond/branch_1_fun/ppermute | solution.py:74
  30.7 8.3 %copy-start = (bf16[384,768]{1,0:T(8,128)(2,1)S(1)}, bf16[384,768]{1,0:T(8,128)(2,1)}, u32[]{:S(2)}) copy-start(bf16[384,768]{1,0:T(8,128)(2,1)} %texts.1) | copy-start | bytes 1769476
  30.7 8.3 %copy-start.5 = (bf16[2,384,768]{2,1,0:T(8,128)(2,1)S(1)}, bf16[2,384,768]{2,1,0:T(8,128)(2,1)}, u32[]{:S(2)}) copy-start(bf16[2,384,768]{2,1,0:T(8,128)(2,1)} %copy-done.4) | copy-start | bytes 3538948
  37.0 27.6 %copy-start.3 = (bf16[384,1536]{1,0:T(8,128)(2,1)}, bf16[384,1536]{1,0:T(8,128)(2,1)S(1)}, u32[]{:S(2)}) copy-start(bf16[384,1536]{1,0:T(8,128)(2,1)S(1)} %get-tuple-element.77.slopes_ref) | copy-start | bytes 3538948
  37.0 27.6 %copy-start.6 = (bf16[384,768]{1,0:T(8,128)(2,1)}, bf16[384,768]{1,0:T(8,128)(2,1)S(1)}, u32[]{:S(2)}) copy-start(bf16[384,768]{1,0:T(8,128)(2,1)S(1)} %get-tuple-element.78.hat_ref) | copy-start | bytes 1769476
  37.0 27.6 %copy-start.7 = (bf16[384,768]{1,0:T(8,128)(2,1)}, bf16[384,768]{1,0:T(8,128)(2,1)S(1)}, u32[]{:S(2)}) copy-start(bf16[384,768]{1,0:T(8,128)(2,1)S(1)} %get-tuple-element.84.far_slopes_ref) | copy-start | bytes 1769476
  37.0 27.6 %copy-start.8 = (bf16[384,768]{1,0:T(8,128)(2,1)}, bf16[384,768]{1,0:T(8,128)(2,1)S(1)}, u32[]{:S(2)}) copy-start(bf16[384,768]{1,0:T(8,128)(2,1)S(1)} %get-tuple-element.85.far_hat_ref) | copy-start | bytes 1769476
  37.0 27.6 %collective-permute-start.12 = (bf16[384,768]{1,0:T(8,128)(2,1)S(1)}, bf16[384,768]{1,0:T(8,128)(2,1)S(1)}, u32[]{:S(2)}, u32[]{:S(2)}) collective-permute-start(bf16[384,768]{1,0:T(8,128)(2,1)S(1)} %get-tuple-element.89), channel_id=1, source_target_pairs={{32,64},{33,65},{34,66},{35,67},{36,68},{37,69},{38,70},{39,71},{4... | collective-permute-start | bytes 1769480 | tf_op jit(solution)/shard_map/ppermute | solution.py:74
  41.5 43.6 %collective-permute-start.11 = (bf16[384,768]{1,0:T(8,128)(2,1)}, bf16[384,768]{1,0:T(8,128)(2,1)}, u32[]{:S(2)}, u32[]{:S(2)}) collective-permute-start(bf16[384,768]{1,0:T(8,128)(2,1)} %get-tuple-element.82), channel_id=1, source_target_pairs={{0,449},{1,448},{2,451},{3,450},{4,453},{5,452},{6,455},{7,454},{8... | collective-permute-start | bytes 1769480 | tf_op jit(solution)/shard_map/ppermute | solution.py:74
  64.8 4.9 %collective-permute-start.3 = (bf16[2,384,768]{2,1,0:T(8,128)(2,1)S(1)}, bf16[2,384,768]{2,1,0:T(8,128)(2,1)}, u32[]{:S(2)}, u32[]{:S(2)}) collective-permute-start(bf16[2,384,768]{2,1,0:T(8,128)(2,1)S(1)} %get-tuple-element.50), channel_id=1, source_target_pairs={{0,32},{1,33},{2,34},{3,35},{4,36},{5,37},{6,38},{7,39},{8,40},{9,... | collective-permute-start | bytes 3538952 | tf_op jit(solution)/shard_map/cond/branch_1_fun/ppermute | solution.py:74
  72.2 23.8 %collective-permute-start.13 = (bf16[384,768]{1,0:T(8,128)(2,1)}, bf16[384,768]{1,0:T(8,128)(2,1)S(1)}, u32[]{:S(2)}, u32[]{:S(2)}) collective-permute-start(bf16[384,768]{1,0:T(8,128)(2,1)} %get-tuple-element.91), channel_id=1, source_target_pairs={{0,1},{1,0},{2,3},{3,2},{4,5},{5,4},{6,7},{7,6},{8,9},{9,8},{10,11... | collective-permute-start | bytes 1769480 | tf_op jit(solution)/shard_map/ppermute | solution.py:74
  74.1 8.4 %collective-permute-start.5 = (bf16[384,768]{1,0:T(8,128)(2,1)}, bf16[384,768]{1,0:T(8,128)(2,1)}, u32[]{:S(2)}, u32[]{:S(2)}) collective-permute-start(bf16[384,768]{1,0:T(8,128)(2,1)} %param.5), channel_id=1, source_target_pairs={{32,64},{33,65},{34,66},{35,67},{36,68},{37,69},{38,70},{39,71},{4... | collective-permute-start | bytes 1769480 | tf_op jit(solution)/shard_map/cond/branch_1_fun/ppermute | solution.py:74
  85.0 11.0 %copy-start.2 = (bf16[384,768]{1,0:T(8,128)(2,1)S(1)}, bf16[384,768]{1,0:T(8,128)(2,1)}, u32[]{:S(2)}) copy-start(bf16[384,768]{1,0:T(8,128)(2,1)} %images.1) | copy-start | bytes 1769476

commit v4 on v3

v4 whole, which is shorter than its diff:
```python
import functools

import jax
import jax.numpy as jnp
from jax import lax
from jax.experimental import pallas as pl
from jax.experimental.pallas import tpu as pltpu
from jax.sharding import PartitionSpec as P

AXES = ("blk", "group")
EPSILON = 1e-06
CHIPS = 4

SMEM = pl.BlockSpec(memory_space=pltpu.SMEM)
WHOLE = pl.BlockSpec(memory_space=pltpu.VMEM)


def params(mib):
    return pltpu.CompilerParams(vmem_limit_bytes=mib * 1024 * 1024)


def near_to(b, g, size):
    to = (b + 2) % size
    return to, g ^ (to // (2 * CHIPS) != b // (2 * CHIPS))


def guest_to(b, g, size):
    if b % 2 == 1:
        return None
    return (b - 1 if b // 2 % CHIPS > 0 else b + 2), g


def guest_partner_to(b, g, size):
    return (guest_to(b, g, size)[0], g ^ 1) if b % 2 == 0 else None


def far_to(b, g, size):
    return ((b + 5) % size, g ^ 1) if b % 2 == 1 and b // 2 % CHIPS == CHIPS - 2 else None


def other_core(b, g, size):
    return b ^ 1, g


def partner(b, g, size):
    return b, g ^ 1


def move(values, where, inverse=False):
    n_blk, n_group = lax.axis_size("blk"), lax.axis_size("group")
    pairs = []
    for b in range(n_blk):
        for g in range(n_group):
            to = where(b, g, n_blk)
            if to is not None:
                pair = (b * n_group + g, to[0] * n_group + to[1])
                pairs.append(pair[::-1] if inverse else pair)
    return lax.ppermute(values, AXES, sorted(pairs))


def normalize(values):
    full = values.astype(jnp.float32)
    inverse = lax.rsqrt(jnp.sum(full * full, axis=-1, keepdims=True) + EPSILON)
    return full * inverse, inverse


def hat(values):
    return normalize(values)[0].astype(jnp.bfloat16)


def dot(left, right, left_dim, right_dim):
    return lax.dot_general(
        left, right, (((left_dim,), (right_dim,)), ((), ())), preferred_element_type=jnp.float32
    )


def slopes_of(text_hat, image_hat, scale, bias, same=None):
    half = 0.5 * scale
    slopes = half * jnp.tanh(half * dot(text_hat, image_hat, 1, 1) + 0.5 * bias) + half
    if same is not None:
        slopes = slopes - scale * same
    return slopes.astype(jnp.bfloat16)


def rows_of(ref):
    count, rows, width = ref.shape
    return ref[...].reshape(count * rows, width)


def is_odd(role):
    return role[0] == 1


def has_guests(role):
    return jnp.logical_and(role[0] == 1, role[1] < CHIPS - 1)


def takes_far(role):
    return jnp.logical_and(role[0] == 0, role[1] == 1)


def pass_on(role, role_out):
    role_out[0] = role[0]
    role_out[1] = role[1]


def hats_kernel(image_ref, partner_ref, hats_ref):
    hats_ref[0] = hat(image_ref[...])
    hats_ref[1] = hat(partner_ref[...])


def near_kernel(
    role, scale_ref, bias_ref, text_ref, mine_ref, theirs_ref, guest_ref, guest_partner_ref, far_ref,
    role_out, grad_ref, hat_ref, mine_slopes_ref, theirs_slopes_ref, back_ref, back_partner_ref, far_grad_ref,
    total, guests_ref,
):
    pass_on(role, role_out)
    scale, bias = scale_ref[0], bias_ref[0]
    rows, width = hat_ref.shape
    near_hat = hat(text_ref[...])
    hat_ref[...] = near_hat
    mine, theirs = rows_of(mine_ref), rows_of(theirs_ref)
    mine_slopes = slopes_of(near_hat, mine, scale, bias)
    mine_slopes_ref[...] = mine_slopes
    theirs_slopes = slopes_of(near_hat, theirs, scale, bias)
    theirs_slopes_ref[...] = theirs_slopes
    total[...] = dot(mine_slopes, mine, 1, 0) + dot(theirs_slopes, theirs, 1, 0)

    def visits(text_hat):
        guests_ref[0] = hat(guest_ref[...])
        guests_ref[1] = hat(guest_partner_ref[...])
        guests = rows_of(guests_ref)
        slopes = slopes_of(text_hat, guests, scale, bias)
        back_ref[...] = dot(slopes[:, :rows], text_hat, 0, 0).astype(back_ref.dtype)
        back_partner_ref[...] = dot(slopes[:, rows:], text_hat, 0, 0).astype(back_partner_ref.dtype)
        return slopes, guests

    @pl.when(has_guests(role))
    def _():
        slopes, guests = visits(hat_ref[...])
        total[...] += dot(slopes, guests, 1, 0)

    @pl.when(takes_far(role))
    def _():
        slopes, guests = visits(hat(far_ref[...]))
        far_grad_ref[...] = dot(slopes, guests, 1, 0).astype(far_grad_ref.dtype)

    grad_ref[...] = total[...].astype(grad_ref.dtype)


def own_kernel(
    role, scale_ref, bias_ref, text_ref, mine_ref, theirs_ref, hat_ref,
    mine_slopes_ref, theirs_slopes_ref,
    text_sum_ref, mine_sum_ref, partner_sum_ref, cross_ref,
):
    scale, bias = scale_ref[0], bias_ref[0]
    rows, width = text_ref.shape
    near_hat = hat_ref[...]
    text_hat = hat(text_ref[...])
    same = (
        lax.broadcasted_iota(jnp.int32, (rows, 2 * rows), 0)
        == lax.broadcasted_iota(jnp.int32, (rows, 2 * rows), 1)
    ).astype(jnp.float32)
    images = rows_of(mine_ref)
    slopes = slopes_of(text_hat, images, scale, bias, same)
    text_sum_ref[...] = dot(slopes, images, 1, 0)
    for slot, out_ref in enumerate((mine_sum_ref, partner_sum_ref)):
        at = slice(slot * rows, (slot + 1) * rows)
        out_ref[...] = dot(slopes[:, at], text_hat, 0, 0) + dot(mine_slopes_ref[:, at], near_hat, 0, 0)

    @pl.when(role[0] == 0)
    def _():
        text_hat = hat(text_ref[...])
        images = rows_of(theirs_ref)
        own = slopes_of(text_hat, images, scale, bias)
        text_sum_ref[...] += dot(own, images, 1, 0)
        for slot in range(2):
            at = slice(slot * rows, (slot + 1) * rows)
            total = dot(theirs_slopes_ref[:, at], hat_ref[...], 0, 0) + dot(own[:, at], text_hat, 0, 0)
            cross_ref[slot] = total.astype(cross_ref.dtype)

    @pl.when(role[0] == 1)
    def _():
        for slot in range(2):
            at = slice(slot * rows, (slot + 1) * rows)
            cross_ref[slot] = dot(theirs_slopes_ref[:, at], hat_ref[...], 0, 0).astype(cross_ref.dtype)


def partner_kernel(role, sum_ref, cross_ref, back_ref, out_ref):
    even = 1.0 - is_odd(role).astype(jnp.float32)
    total = sum_ref[...] + cross_ref[0].astype(jnp.float32) + even * back_ref[...].astype(jnp.float32)
    out_ref[...] = total.astype(out_ref.dtype)


def project(raw, total):
    unit, inverse = normalize(raw)
    return (total - unit * jnp.sum(unit * total, axis=-1, keepdims=True)) * inverse


def text_final_kernel(role, texts, text_sum, near_back, far_back, role_out, out_ref):
    pass_on(role, role_out)
    total = text_sum[...] + near_back[...].astype(jnp.float32) + far_back[...].astype(jnp.float32)
    out_ref[...] = project(texts[...], total)


def image_final_kernel(role, images, image_sum, from_partner, out_ref):
    total = image_sum[...] + from_partner[...].astype(jnp.float32)
    out_ref[...] = project(images[...], total)


def call(kernel, out_shape, *operands, mib=16, scalars=3, scalar_outs=0, scratch=()):
    outs = out_shape if isinstance(out_shape, list) else [out_shape]
    out_specs = [SMEM] * scalar_outs + [WHOLE] * (len(outs) - scalar_outs)
    return pl.pallas_call(
        kernel,
        in_specs=[SMEM] * scalars + [WHOLE] * (len(operands) - scalars),
        out_specs=out_specs if isinstance(out_shape, list) else out_specs[0],
        out_shape=out_shape,
        scratch_shapes=list(scratch),
        compiler_params=params(mib),
    )(*operands)


def on_device(images, texts, logit_scale, logit_bias):
    rows, width = images.shape
    bf16 = functools.partial(jax.ShapeDtypeStruct, dtype=jnp.bfloat16)
    full = jax.ShapeDtypeStruct((rows, width), jnp.float32)
    half = bf16((rows, width))
    half_pair = bf16((2, rows, width))

    index = lax.axis_index("blk")
    role = jnp.stack([index % 2, index // 2 % CHIPS]).astype(jnp.int32)
    scalars = (role, logit_scale, logit_bias)
    positive = logit_scale[0] > 0

    def together(body, *operands):
        return lax.cond(positive, body, body, *operands)

    partner_images = move(images, partner)
    near = move(texts, near_to)
    guest = move(images, guest_to)
    guest_partner = move(images, guest_partner_to)
    far = move(texts, far_to)
    mine = call(hats_kernel, half_pair, images, partner_images, scalars=0)
    theirs = together(lambda values: move(values, other_core), mine)
    role_type = jax.ShapeDtypeStruct((2,), jnp.int32)
    scalars = (role, logit_scale, logit_bias)
    slopes_pair = bf16((rows, 2 * rows))
    role, near_grad, near_hat, mine_slopes, theirs_slopes, back, back_partner, far_grad = call(
        near_kernel,
        [role_type, half, half, slopes_pair, slopes_pair, half, half, half],
        *scalars, near, mine, theirs, guest, guest_partner, far,
        scratch=[pltpu.VMEM((rows, width), jnp.float32), pltpu.VMEM((2, rows, width), jnp.bfloat16)],
        mib=24,
        scalar_outs=1,
    )
    scalars = (role, logit_scale, logit_bias)
    near_back = move(near_grad, near_to, True)
    far_back = move(far_grad, far_to, True)
    back_partner = move(back_partner, guest_to, True)
    back = move(back, guest_to, True)
    text_sum, mine_sum, partner_sum, cross = call(
        own_kernel,
        [full, full, full, half_pair],
        *scalars, texts, mine, theirs, near_hat, mine_slopes, theirs_slopes,
        mib=24,
    )

    def sum_with_cross(kernel, slot, dtype, *operands):
        specs = []
        for operand in operands:
            if operand.shape == (2,):
                specs.append(SMEM)
            elif operand.ndim == 3:
                specs.append(pl.BlockSpec((1, rows, width), lambda i: (slot, 0, 0)))
            else:
                specs.append(pl.BlockSpec(operand.shape, lambda i: (0, 0)))
        return pl.pallas_call(
            kernel,
            grid=(1,),
            in_specs=specs,
            out_specs=pl.BlockSpec((rows, width), lambda i: (0, 0)),
            out_shape=jax.ShapeDtypeStruct((rows, width), dtype),
            compiler_params=params(16),
        )(*operands)

    def across(cross, role, partner_sum, back_partner):
        cross = move(cross, other_core)
        return cross, sum_with_cross(partner_kernel, 1, jnp.bfloat16, role, partner_sum, cross, back_partner)

    cross, for_partner = together(across, cross, role, partner_sum, back_partner)
    from_partner = move(for_partner, partner)
    image_sum = sum_with_cross(partner_kernel, 0, jnp.float32, role, mine_sum, cross, back)
    role, text_grad = call(
        text_final_kernel,
        [jax.ShapeDtypeStruct((2,), jnp.int32), full],
        role, texts, text_sum, near_back, far_back,
        scalars=1, scalar_outs=1,
    )
    image_grad = call(image_final_kernel, full, role, images, image_sum, from_partner, scalars=1)
    return image_grad, text_grad


def solution(mesh):
    return jax.shard_map(
        on_device,
        mesh=mesh,
        in_specs=(P(AXES, None), P(AXES, None), P(), P()),
        out_specs=(P(AXES, None), P(AXES, None)),
        check_vma=False,
    )
```

time: 99.2 us -> 97.7 us (0.985)
  Pallas kernels: 22.5 us -> 21.4 us
  local copies, waits for them, and re-layouts: 2.1 us -> 1.07 us
  waiting for transfers between devices: 21.5 us -> 22.5 us
    pallas_call x2, Pallas kernels: 4.96 us -> 2.67 us  [sum_with_cross(): pl.pallas_call(kernel, grid=(1,), in_specs=specs, out_specs=pl.BlockSpec(...]
    pallas_call x6 -> x5, Pallas kernels: 17.6 us -> 18.7 us  [call(): pl.pallas_call(kernel, in_specs=[SMEM] * scalars + [WHOLE] * (len(operand...]
    unnamed x18 -> x6, local copies, waits for them, and re-layouts: 2.1 us -> 1.07 us
    ppermute x11 -> x12, waiting for transfers between devices: 21.5 us -> 22.5 us  [move(): return lax.ppermute(values, AXES, sorted(pairs))]
    ppermute x11 -> x12, starting transfers between devices: 50 us -> 50 us  [move(): return lax.ppermute(values, AXES, sorted(pairs))]
  transfers between devices with their start and end apart: 11 -> 12, of which waited for: 5 -> 5; matrix products, arithmetic and copies ran while one was open for 0% -> 0% of each run, Pallas kernels for 14% -> 12%
where the time goes in v4:
time: 97.7 us; the launch traced here: 97.1 us
  starting transfers between devices  50 us (51%)
  waiting for transfers between devices  22.5 us (23%)
  Pallas kernels  21.4 us (22%)
  between operations  2.12 us (2%)
  local copies, waits for them, and re-layouts  1.07 us (1%)
    ppermute x12, starting transfers between devices, move(): return lax.ppermute(values, AXES, sorted(pairs))  50 us
    ppermute x12, waiting for transfers between devices, move(): return lax.ppermute(values, AXES, sorted(pairs))  22.5 us
    pallas_call x5, Pallas kernels, call(): pl.pallas_call(kernel, in_specs=[SMEM] * scalars + [WHOLE] * (len(operand...  18.7 us
    pallas_call x2, Pallas kernels, sum_with_cross(): pl.pallas_call(kernel, grid=(1,), in_specs=specs, out_specs=pl.BlockSpec(...  2.67 us
  transfers between devices with their start and end apart: 12, of which 5 were waited for; matrix products, arithmetic and copies ran while one was open for 0% of the time, Pallas kernels for 12%

profile of v4, /device:TPU:1, one launch (start us, length us, event | category | flops | bytes accessed | tf_op | source)
XLA Modules:
  0.0 97.1 jit_solution(3737599699750066551)
XLA Ops:
  0.6 4.8 %collective-permute-start.5 = (bf16[384,768]{1,0:T(8,128)(2,1)}, bf16[384,768]{1,0:T(8,128)(2,1)S(1)}, u32[]{:S(2)}, u32[]{:S(2)}) collective-permute-start(bf16[384,768]{1,0:T(8,128)(2,1)} %images.1), channel_id=1, source_target_pairs={{0,1},{1,0},{2,3},{3,2},{4,5},{5,4},{6,7},{7,6},{8,9},{9,8},{10,11... | collective-permute-start | bytes 1769480 | tf_op jit(solution)/shard_map/ppermute | solution.py:58
  6.2 3.1 %collective-permute-start.4 = (bf16[384,768]{1,0:T(8,128)(2,1)}, bf16[384,768]{1,0:T(8,128)(2,1)S(1)}, u32[]{:S(2)}, u32[]{:S(2)}) collective-permute-start(bf16[384,768]{1,0:T(8,128)(2,1)} %texts.1), channel_id=1, source_target_pairs={{0,64},{1,65},{2,66},{3,67},{4,68},{5,69},{6,70},{7,71},{8,72},{9,... | collective-permute-start | bytes 1769480 | tf_op jit(solution)/shard_map/ppermute | solution.py:58
  9.3 1.3 %collective-permute-start.6 = (bf16[384,768]{1,0:T(8,128)(2,1)}, bf16[384,768]{1,0:T(8,128)(2,1)S(1)}, u32[]{:S(2)}, u32[]{:S(2)}) collective-permute-start(bf16[384,768]{1,0:T(8,128)(2,1)} %images.1), channel_id=1, source_target_pairs={{0,64},{1,65},{2,66},{3,67},{4,68},{5,69},{6,70},{7,71},{8,72},{9,... | collective-permute-start | bytes 1769480 | tf_op jit(solution)/shard_map/ppermute | solution.py:58
  13.3 1.4 %collective-permute-done.5.partner_ref = bf16[384,768]{1,0:T(8,128)(2,1)S(1)} collective-permute-done((bf16[384,768]{1,0:T(8,128)(2,1)}, bf16[384,768]{1,0:T(8,128)(2,1)S(1)}, u32[]{:S(2)}, u32[]{:S(2)}) %collective-permute-start.5) | collective-permute-done | bytes 589856 | tf_op jit(solution)/shard_map/ppermute | solution.py:58
  15.8 1.4 %shard_map.59.mine_ref = bf16[2,384,768]{2,1,0:T(8,128)(2,1)} custom-call(bf16[384,768]{1,0:T(8,128)(2,1)S(1)} %copy-done.1, bf16[384,768]{1,0:T(8,128)(2,1)S(1)} %collective-permute-done.5.partner_ref), custom_call_target="tpu_custom_call" | custom-call | tf_op jit(solution)/shard_map/pallas_call | solution.py:214
  17.1 10.0 %conditional.2 = (bf16[2,384,768]{2,1,0:T(8,128)(2,1)}) conditional(s32[]{:T(128)} %bitcast.2, bf16[2,384,768]{2,1,0:T(8,128)(2,1)} %shard_map.59.mine_ref, bf16[2,384,768]{2,1,0:T(8,128)(2,1)} %shard_map.59.mine_ref), branch_computations={%region_0.1_spmd, %region_1.2_spmd} | conditional | bytes 4718640 | solution.py:237
  17.1 7.2 %collective-permute-start.1 = (bf16[2,384,768]{2,1,0:T(8,128)(2,1)}, bf16[2,384,768]{2,1,0:T(8,128)(2,1)}, u32[]{:S(2)}, u32[]{:S(2)}) collective-permute-start(bf16[2,384,768]{2,1,0:T(8,128)(2,1)} %param.1), channel_id=1, source_target_pairs={{0,32},{1,33},{2,34},{3,35},{4,36},{5,37},{6,38},{7,39},{8,40},{9,... | collective-permute-start | bytes 3538952 | tf_op jit(solution)/shard_map/cond/branch_1_fun/ppermute | solution.py:58
  24.3 2.8 %collective-permute-done.1 = bf16[2,384,768]{2,1,0:T(8,128)(2,1)} collective-permute-done((bf16[2,384,768]{2,1,0:T(8,128)(2,1)}, bf16[2,384,768]{2,1,0:T(8,128)(2,1)}, u32[]{:S(2)}, u32[]{:S(2)}) %collective-permute-start.1) | collective-permute-done | bytes 1179680 | tf_op jit(solution)/shard_map/cond/branch_1_fun/ppermute | solution.py:58
  27.1 2.7 %collective-permute-done.4.text_ref = bf16[384,768]{1,0:T(8,128)(2,1)S(1)} collective-permute-done((bf16[384,768]{1,0:T(8,128)(2,1)}, bf16[384,768]{1,0:T(8,128)(2,1)S(1)}, u32[]{:S(2)}, u32[]{:S(2)}) %collective-permute-start.4) | collective-permute-done | bytes 589856 | tf_op jit(solution)/shard_map/ppermute | solution.py:58
  29.8 7.4 %shard_map.60 = (s32[2]{0:T(128)S(1)}, bf16[384,768]{1,0:T(8,128)(2,1)}, bf16[384,768]{1,0:T(8,128)(2,1)S(1)}, bf16[384,768]{1,0:T(8,128)(2,1)S(1)}, bf16[384,76...) custom-call(s32[2]{0:T(128)S(1)} %pad_add_fusion.role, ...), custom_call_target="tpu_custom_call" | custom-call | tf_op jit(solution)/shard_map/pallas_call | solution.py:214
  37.2 10.0 %collective-permute-start.11 = (bf16[384,768]{1,0:T(8,128)(2,1)S(1)}, bf16[384,768]{1,0:T(8,128)(2,1)S(1)}, u32[]{:S(2)}, u32[]{:S(2)}) collective-permute-start(bf16[384,768]{1,0:T(8,128)(2,1)S(1)} %get-tuple-element.58), channel_id=1, source_target_pairs={{32,64},{33,65},{34,66},{35,67},{36,68},{37,69},{38,70},{39,71},{4... | collective-permute-start | bytes 1769480 | tf_op jit(solution)/shard_map/ppermute | solution.py:58
  47.2 3.4 %collective-permute-start.9 = (bf16[384,768]{1,0:T(8,128)(2,1)}, bf16[384,768]{1,0:T(8,128)(2,1)}, u32[]{:S(2)}, u32[]{:S(2)}) collective-permute-start(bf16[384,768]{1,0:T(8,128)(2,1)} %get-tuple-element.52), channel_id=1, source_target_pairs={{0,449},{1,448},{2,451},{3,450},{4,453},{5,452},{6,455},{7,454},{8... | collective-permute-start | bytes 1769480 | tf_op jit(solution)/shard_map/ppermute | solution.py:58
  50.6 1.5 %collective-permute-start.10 = (bf16[384,768]{1,0:T(8,128)(2,1)}, bf16[384,768]{1,0:T(8,128)(2,1)}, u32[]{:S(2)}, u32[]{:S(2)}) collective-permute-start(bf16[384,768]{1,0:T(8,128)(2,1)} %get-tuple-element.53), channel_id=1, source_target_pairs={{64,417},{65,416},{66,419},{67,418},{68,421},{69,420},{70,423},{71... | collective-permute-start | bytes 1769480 | tf_op jit(solution)/shard_map/ppermute | solution.py:58
  52.1 10.3 %collective-permute-start.12 = (bf16[384,768]{1,0:T(8,128)(2,1)}, bf16[384,768]{1,0:T(8,128)(2,1)S(1)}, u32[]{:S(2)}, u32[]{:S(2)}) collective-permute-start(bf16[384,768]{1,0:T(8,128)(2,1)} %get-tuple-element.60), channel_id=1, source_target_pairs={{32,64},{33,65},{34,66},{35,67},{36,68},{37,69},{38,70},{39,71},{4... | collective-permute-start | bytes 1769480 | tf_op jit(solution)/shard_map/ppermute | solution.py:58
  62.4 5.2 %shard_map.61 = (f32[384,768]{1,0:T(8,128)S(1)}, f32[384,768]{1,0:T(8,128)S(1)}, f32[384,768]{1,0:T(8,128)S(1)}, bf16[2,384,768]{2,1,0:T(8,128)(2,1)S(1)}) custom-call(s32[2]{0:T(128)S(1)} %get-tuple-element.47.role, f32[1]{0:T(128)S(6)} %copy.12.scale_ref, f32[1]{0:T(128)S(6)} %copy.13.bias_ref, bf16[384,768]{1,0:T(8,128)(2,1)S(1)} %copy-done, ...), custom_call_target="tpu_custom_call" | custom-call | tf_op jit(solution)/shard_map/pallas_call | solution.py:214
  67.6 6.2 %conditional.3 = (bf16[2,384,768]{2,1,0:T(8,128)(2,1)}, bf16[384,768]{1,0:T(8,128)(2,1)S(1)}) conditional(s32[]{:T(128)} %bitcast.2, (bf16[2,384,768]{2,1,0:T(8,128)(2,1)S(1)}, s32[2]{0:T(128)S(1)}, f32[384,768]{1,0:T(8,128)S(1)}, bf16[384,768]{1,0:T(8,128)(2,1)S(1)}) %tuple.22, (bf16[2,384,768]{2,1,0:T(8,128)(2,1)S(1)}, s32[2]{0:T(128)S(1)}, ...), branch_computations={%region_2.3_spmd, %region_3.4_spmd} | conditional | bytes 4718648 | solution.py:237
  67.6 1.9 %collective-permute-start.3 = (bf16[2,384,768]{2,1,0:T(8,128)(2,1)S(1)}, bf16[2,384,768]{2,1,0:T(8,128)(2,1)}, u32[]{:S(2)}, u32[]{:S(2)}) collective-permute-start(bf16[2,384,768]{2,1,0:T(8,128)(2,1)S(1)} %get-tuple-element.25), channel_id=1, source_target_pairs={{0,32},{1,33},{2,34},{3,35},{4,36},{5,37},{6,38},{7,39},{8,40},{9,... | collective-permute-start | bytes 3538952 | tf_op jit(solution)/shard_map/cond/branch_1_fun/ppermute | solution.py:58
  69.5 2.9 %collective-permute-done.3.cross_ref = bf16[2,384,768]{2,1,0:T(8,128)(2,1)} collective-permute-done((bf16[2,384,768]{2,1,0:T(8,128)(2,1)S(1)}, bf16[2,384,768]{2,1,0:T(8,128)(2,1)}, u32[]{:S(2)}, u32[]{:S(2)}) %collective-permute-start.3) | collective-permute-done | bytes 1179680 | tf_op jit(solution)/shard_map/cond/branch_1_fun/ppermute | solution.py:58
  72.5 1.3 %branch_1_fun.1 = bf16[384,768]{1,0:T(8,128)(2,1)S(1)} custom-call(s32[2]{0:T(128)S(1)} %get-tuple-element.26.role, f32[384,768]{1,0:T(8,128)S(1)} %get-tuple-element.27.sum_ref, bf16[2,384,768]{2,1,0:T(8,128)(2,1)} %collective-permute-done.3.cross_ref, bf16[384,768]{1,0:T(8,128)(2,1)S(1)} %get-tuple-element.28.back_ref), custom_call_target="tpu_custom_call" | custom-call | tf_op jit(solution)/shard_map/cond/branch_1_fun/pallas_call | solution.py:278
  73.8 4.5 %collective-permute-start.13 = (bf16[384,768]{1,0:T(8,128)(2,1)S(1)}, bf16[384,768]{1,0:T(8,128)(2,1)S(1)}, u32[]{:S(2)}, u32[]{:S(2)}) collective-permute-start(bf16[384,768]{1,0:T(8,128)(2,1)S(1)} %get-tuple-element.61), channel_id=1, source_target_pairs={{0,1},{1,0},{2,3},{3,2},{4,5},{5,4},{6,7},{7,6},{8,9},{9,8},{10,11... | collective-permute-start | bytes 1769480 | tf_op jit(solution)/shard_map/ppermute | solution.py:58
  78.3 2.8 %shard_map.62 = (s32[2]{0:T(128)S(1)}, f32[384,768]{1,0:T(8,128)}) custom-call(s32[2]{0:T(128)S(1)} %get-tuple-element.47.role, bf16[384,768]{1,0:T(8,128)(2,1)S(1)} %copy-done, f32[384,768]{1,0:T(8,128)S(1)} %get-tuple-element.51.text_sum, bf16[384,768]{1,0:T(8,128)(2,1)} %collective-permute-done.9.near_back, bf16[384,768]{1,0:T(8,128)(2,1)} %collective-permute-done.10.far_back), custom_call_target="tpu_custom_call" | custom-call | tf_op jit(solution)/shard_map/pallas_call | solution.py:214
  81.1 1.3 %shard_map.63.image_sum = f32[384,768]{1,0:T(8,128)S(1)} custom-call(s32[2]{0:T(128)S(1)} %get-tuple-element.47.role, f32[384,768]{1,0:T(8,128)S(1)} %get-tuple-element.55.sum_ref, bf16[2,384,768]{2,1,0:T(8,128)(2,1)} %get-tuple-element.59.cross_ref, bf16[384,768]{1,0:T(8,128)(2,1)S(1)} %collective-permute-done.12.back_ref), custom_call_target="tpu_custom_call" | custom-call | tf_op jit(solution)/shard_map/pallas_call | solution.py:278
  82.5 12.6 %collective-permute-done.13.from_partner = bf16[384,768]{1,0:T(8,128)(2,1)S(1)} collective-permute-done((bf16[384,768]{1,0:T(8,128)(2,1)S(1)}, bf16[384,768]{1,0:T(8,128)(2,1)S(1)}, u32[]{:S(2)}, u32[]{:S(2)}) %collective-permute-start.13) | collective-permute-done | bytes 589856 | tf_op jit(solution)/shard_map/ppermute | solution.py:58
  95.1 2.0 %shard_map.64 = f32[384,768]{1,0:T(8,128)} custom-call(s32[2]{0:T(128)S(1)} %get-tuple-element.54.role, bf16[384,768]{1,0:T(8,128)(2,1)S(1)} %copy-done.2, f32[384,768]{1,0:T(8,128)S(1)} %shard_map.63.image_sum, bf16[384,768]{1,0:T(8,128)(2,1)S(1)} %collective-permute-done.13.from_partner), custom_call_target="tpu_custom_call" | custom-call | tf_op jit(solution)/shard_map/pallas_call | solution.py:214
  (16 shorter events, 3.2 us)
Async XLA Ops:
  0.6 14.1 %collective-permute-start.5 = (bf16[384,768]{1,0:T(8,128)(2,1)}, bf16[384,768]{1,0:T(8,128)(2,1)S(1)}, u32[]{:S(2)}, u32[]{:S(2)}) collective-permute-start(bf16[384,768]{1,0:T(8,128)(2,1)} %images.1), channel_id=1, source_target_pairs={{0,1},{1,0},{2,3},{3,2},{4,5},{5,4},{6,7},{7,6},{8,9},{9,8},{10,11... | collective-permute-start | bytes 1769480 | tf_op jit(solution)/shard_map/ppermute | solution.py:58
  5.5 21.6 %collective-permute-start.8 = (bf16[384,768]{1,0:T(8,128)(2,1)}, bf16[384,768]{1,0:T(8,128)(2,1)S(1)}, u32[]{:S(2)}, u32[]{:S(2)}) collective-permute-start(bf16[384,768]{1,0:T(8,128)(2,1)} %texts.1), channel_id=1, source_target_pairs={{160,321},{161,320},{162,323},{163,322},{164,325},{165,324},{166,3... | collective-permute-start | bytes 1769480 | tf_op jit(solution)/shard_map/ppermute | solution.py:58
  6.2 23.6 %collective-permute-start.4 = (bf16[384,768]{1,0:T(8,128)(2,1)}, bf16[384,768]{1,0:T(8,128)(2,1)S(1)}, u32[]{:S(2)}, u32[]{:S(2)}) collective-permute-start(bf16[384,768]{1,0:T(8,128)(2,1)} %texts.1), channel_id=1, source_target_pairs={{0,64},{1,65},{2,66},{3,67},{4,68},{5,69},{6,70},{7,71},{8,72},{9,... | collective-permute-start | bytes 1769480 | tf_op jit(solution)/shard_map/ppermute | solution.py:58
  9.3 20.5 %collective-permute-start.6 = (bf16[384,768]{1,0:T(8,128)(2,1)}, bf16[384,768]{1,0:T(8,128)(2,1)S(1)}, u32[]{:S(2)}, u32[]{:S(2)}) collective-permute-start(bf16[384,768]{1,0:T(8,128)(2,1)} %images.1), channel_id=1, source_target_pairs={{0,64},{1,65},{2,66},{3,67},{4,68},{5,69},{6,70},{7,71},{8,72},{9,... | collective-permute-start | bytes 1769480 | tf_op jit(solution)/shard_map/ppermute | solution.py:58
  10.6 19.2 %collective-permute-start.7 = (bf16[384,768]{1,0:T(8,128)(2,1)}, bf16[384,768]{1,0:T(8,128)(2,1)S(1)}, u32[]{:S(2)}, u32[]{:S(2)}) collective-permute-start(bf16[384,768]{1,0:T(8,128)(2,1)} %images.1), channel_id=1, source_target_pairs={{0,65},{1,64},{2,67},{3,66},{4,69},{5,68},{6,71},{7,70},{8,73},{9,... | collective-permute-start | bytes 1769480 | tf_op jit(solution)/shard_map/ppermute | solution.py:58
  14.7 1.1 %copy-start.1 = (bf16[384,768]{1,0:T(8,128)(2,1)S(1)}, bf16[384,768]{1,0:T(8,128)(2,1)}, u32[]{:S(2)}) copy-start(bf16[384,768]{1,0:T(8,128)(2,1)} %images.1) | copy-start | bytes 1769476
  17.1 10.0 %collective-permute-start.1 = (bf16[2,384,768]{2,1,0:T(8,128)(2,1)}, bf16[2,384,768]{2,1,0:T(8,128)(2,1)}, u32[]{:S(2)}, u32[]{:S(2)}) collective-permute-start(bf16[2,384,768]{2,1,0:T(8,128)(2,1)} %param.1), channel_id=1, source_target_pairs={{0,32},{1,33},{2,34},{3,35},{4,36},{5,37},{6,38},{7,39},{8,40},{9,... | collective-permute-start | bytes 3538952 | tf_op jit(solution)/shard_map/cond/branch_1_fun/ppermute | solution.py:58
  27.1 35.3 %copy-start = (bf16[384,768]{1,0:T(8,128)(2,1)S(1)}, bf16[384,768]{1,0:T(8,128)(2,1)}, u32[]{:S(2)}) copy-start(bf16[384,768]{1,0:T(8,128)(2,1)} %texts.1) | copy-start | bytes 1769476
  37.2 30.4 %collective-permute-start.11 = (bf16[384,768]{1,0:T(8,128)(2,1)S(1)}, bf16[384,768]{1,0:T(8,128)(2,1)S(1)}, u32[]{:S(2)}, u32[]{:S(2)}) collective-permute-start(bf16[384,768]{1,0:T(8,128)(2,1)S(1)} %get-tuple-element.58), channel_id=1, source_target_pairs={{32,64},{33,65},{34,66},{35,67},{36,68},{37,69},{38,70},{39,71},{4... | collective-permute-start | bytes 1769480 | tf_op jit(solution)/shard_map/ppermute | solution.py:58
  47.2 31.1 %collective-permute-start.9 = (bf16[384,768]{1,0:T(8,128)(2,1)}, bf16[384,768]{1,0:T(8,128)(2,1)}, u32[]{:S(2)}, u32[]{:S(2)}) collective-permute-start(bf16[384,768]{1,0:T(8,128)(2,1)} %get-tuple-element.52), channel_id=1, source_target_pairs={{0,449},{1,448},{2,451},{3,450},{4,453},{5,452},{6,455},{7,454},{8... | collective-permute-start | bytes 1769480 | tf_op jit(solution)/shard_map/ppermute | solution.py:58
  50.6 27.7 %collective-permute-start.10 = (bf16[384,768]{1,0:T(8,128)(2,1)}, bf16[384,768]{1,0:T(8,128)(2,1)}, u32[]{:S(2)}, u32[]{:S(2)}) collective-permute-start(bf16[384,768]{1,0:T(8,128)(2,1)} %get-tuple-element.53), channel_id=1, source_target_pairs={{64,417},{65,416},{66,419},{67,418},{68,421},{69,420},{70,423},{71... | collective-permute-start | bytes 1769480 | tf_op jit(solution)/shard_map/ppermute | solution.py:58
  52.1 29.0 %collective-permute-start.12 = (bf16[384,768]{1,0:T(8,128)(2,1)}, bf16[384,768]{1,0:T(8,128)(2,1)S(1)}, u32[]{:S(2)}, u32[]{:S(2)}) collective-permute-start(bf16[384,768]{1,0:T(8,128)(2,1)} %get-tuple-element.60), channel_id=1, source_target_pairs={{32,64},{33,65},{34,66},{35,67},{36,68},{37,69},{38,70},{39,71},{4... | collective-permute-start | bytes 1769480 | tf_op jit(solution)/shard_map/ppermute | solution.py:58
  67.6 4.9 %collective-permute-start.3 = (bf16[2,384,768]{2,1,0:T(8,128)(2,1)S(1)}, bf16[2,384,768]{2,1,0:T(8,128)(2,1)}, u32[]{:S(2)}, u32[]{:S(2)}) collective-permute-start(bf16[2,384,768]{2,1,0:T(8,128)(2,1)S(1)} %get-tuple-element.25), channel_id=1, source_target_pairs={{0,32},{1,33},{2,34},{3,35},{4,36},{5,37},{6,38},{7,39},{8,40},{9,... | collective-permute-start | bytes 3538952 | tf_op jit(solution)/shard_map/cond/branch_1_fun/ppermute | solution.py:58
  73.8 21.3 %collective-permute-start.13 = (bf16[384,768]{1,0:T(8,128)(2,1)S(1)}, bf16[384,768]{1,0:T(8,128)(2,1)S(1)}, u32[]{:S(2)}, u32[]{:S(2)}) collective-permute-start(bf16[384,768]{1,0:T(8,128)(2,1)S(1)} %get-tuple-element.61), channel_id=1, source_target_pairs={{0,1},{1,0},{2,3},{3,2},{4,5},{5,4},{6,7},{7,6},{8,9},{9,8},{10,11... | collective-permute-start | bytes 1769480 | tf_op jit(solution)/shard_map/ppermute | solution.py:58
  81.1 14.0 %copy-start.2 = (bf16[384,768]{1,0:T(8,128)(2,1)S(1)}, bf16[384,768]{1,0:T(8,128)(2,1)}, u32[]{:S(2)}) copy-start(bf16[384,768]{1,0:T(8,128)(2,1)} %images.1) | copy-start | bytes 1769476

commit v5 on v4

--- a/solution.py
+++ b/solution.py
@@ -36,6 +36,17 @@
 
 def far_to(b, g, size):
     return ((b + 5) % size, g ^ 1) if b % 2 == 1 and b // 2 % CHIPS == CHIPS - 2 else None
+
+
+def back_to(b, g, size):
+    to = (b - 2) % size
+    if to // (2 * CHIPS) == b // (2 * CHIPS):
+        return to, g
+    return (to, g ^ 1) if b % 2 == 0 else (b + 2 * CHIPS - 2, g)
+
+
+def over_z(b, g, size):
+    return ((b + 2 * CHIPS) % size, g ^ 1) if b % 2 == 1 and b // 2 % CHIPS == CHIPS - 1 else None
 
 
 def other_core(b, g, size):
@@ -197,9 +208,11 @@
     return (total - unit * jnp.sum(unit * total, axis=-1, keepdims=True)) * inverse
 
 
-def text_final_kernel(role, texts, text_sum, near_back, far_back, role_out, out_ref):
+def text_final_kernel(role, texts, text_sum, near_back, last_back, far_back, role_out, out_ref):
     pass_on(role, role_out)
-    total = text_sum[...] + near_back[...].astype(jnp.float32) + far_back[...].astype(jnp.float32)
+    last = jnp.logical_and(role[0] == 1, role[1] == CHIPS - 1)
+    near = jnp.where(last, last_back[...].astype(jnp.float32), near_back[...].astype(jnp.float32))
+    total = text_sum[...] + near + far_back[...].astype(jnp.float32)
     out_ref[...] = project(texts[...], total)
 
 
@@ -255,7 +268,7 @@
         scalar_outs=1,
     )
     scalars = (role, logit_scale, logit_bias)
-    near_back = move(near_grad, near_to, True)
+    near_back = move(near_grad, back_to)
     far_back = move(far_grad, far_to, True)
     back_partner = move(back_partner, guest_to, True)
     back = move(back, guest_to, True)
@@ -290,11 +303,12 @@
 
     cross, for_partner = together(across, cross, role, partner_sum, back_partner)
     from_partner = move(for_partner, partner)
+    last_back = together(lambda values: move(values, over_z), near_back)
     image_sum = sum_with_cross(partner_kernel, 0, jnp.float32, role, mine_sum, cross, back)
     role, text_grad = call(
         text_final_kernel,
         [jax.ShapeDtypeStruct((2,), jnp.int32), full],
-        role, texts, text_sum, near_back, far_back,
+        role, texts, text_sum, near_back, last_back, far_back,
         scalars=1, scalar_outs=1,
     )
     image_grad = call(image_final_kernel, full, role, images, image_sum, from_partner, scalars=1)

time: 97.7 us -> 96.2 us (0.985)
  waiting for transfers between devices: 22.5 us -> 17.8 us
  Pallas kernels: 21.4 us -> 23 us
  starting transfers between devices: 50 us -> 51.4 us
    ppermute x12 -> x13, waiting for transfers between devices: 22.5 us -> 17.8 us  [move(): return lax.ppermute(values, AXES, sorted(pairs))]
    ppermute x12 -> x13, starting transfers between devices: 50 us -> 51.4 us  [move(): return lax.ppermute(values, AXES, sorted(pairs))]
  transfers between devices with their start and end apart: 12 -> 13, of which waited for: 5 -> 5; matrix products, arithmetic and copies ran while one was open for 0% -> 0% of each run, Pallas kernels for 12% -> 14%
where the time goes in v5:
time: 96.2 us; the launch traced here: 95.5 us
  starting transfers between devices  51.4 us (53%)
  Pallas kernels  23 us (24%)
  waiting for transfers between devices  17.8 us (19%)
  between operations  2.11 us (2%)
  local copies, waits for them, and re-layouts  1.07 us (1%)
    ppermute x13, starting transfers between devices, move(): return lax.ppermute(values, AXES, sorted(pairs))  51.4 us
    pallas_call x5, Pallas kernels, call(): pl.pallas_call(kernel, in_specs=[SMEM] * scalars + [WHOLE] * (len(operand...  19.5 us
    ppermute x13, waiting for transfers between devices, move(): return lax.ppermute(values, AXES, sorted(pairs))  17.8 us
    pallas_call x2, Pallas kernels, sum_with_cross(): pl.pallas_call(kernel, grid=(1,), in_specs=specs, out_specs=pl.BlockSpec(...  3.48 us
  transfers between devices with their start and end apart: 13, of which 5 were waited for; matrix products, arithmetic and copies ran while one was open for 0% of the time, Pallas kernels for 14%

profile of v5, /device:TPU:1, one launch (start us, length us, event | category | flops | bytes accessed | tf_op | source)
XLA Modules:
  0.0 95.5 jit_solution(6811658270291111053)
XLA Ops:
  0.6 4.8 %collective-permute-start.7 = (bf16[384,768]{1,0:T(8,128)(2,1)}, bf16[384,768]{1,0:T(8,128)(2,1)S(1)}, u32[]{:S(2)}, u32[]{:S(2)}) collective-permute-start(bf16[384,768]{1,0:T(8,128)(2,1)} %images.1), channel_id=1, source_target_pairs={{0,1},{1,0},{2,3},{3,2},{4,5},{5,4},{6,7},{7,6},{8,9},{9,8},{10,11... | collective-permute-start | bytes 1769480 | tf_op jit(solution)/shard_map/ppermute | solution.py:69
  6.2 3.1 %collective-permute-start.6 = (bf16[384,768]{1,0:T(8,128)(2,1)}, bf16[384,768]{1,0:T(8,128)(2,1)S(1)}, u32[]{:S(2)}, u32[]{:S(2)}) collective-permute-start(bf16[384,768]{1,0:T(8,128)(2,1)} %texts.1), channel_id=1, source_target_pairs={{0,64},{1,65},{2,66},{3,67},{4,68},{5,69},{6,70},{7,71},{8,72},{9,... | collective-permute-start | bytes 1769480 | tf_op jit(solution)/shard_map/ppermute | solution.py:69
  13.3 1.4 %collective-permute-done.7.partner_ref = bf16[384,768]{1,0:T(8,128)(2,1)S(1)} collective-permute-done((bf16[384,768]{1,0:T(8,128)(2,1)}, bf16[384,768]{1,0:T(8,128)(2,1)S(1)}, u32[]{:S(2)}, u32[]{:S(2)}) %collective-permute-start.7) | collective-permute-done | bytes 589856 | tf_op jit(solution)/shard_map/ppermute | solution.py:69
  15.8 1.4 %shard_map.59.mine_ref = bf16[2,384,768]{2,1,0:T(8,128)(2,1)} custom-call(bf16[384,768]{1,0:T(8,128)(2,1)S(1)} %copy-done.1, bf16[384,768]{1,0:T(8,128)(2,1)S(1)} %collective-permute-done.7.partner_ref), custom_call_target="tpu_custom_call" | custom-call | tf_op jit(solution)/shard_map/pallas_call | solution.py:227
  17.1 10.0 %conditional.3 = (bf16[2,384,768]{2,1,0:T(8,128)(2,1)}) conditional(s32[]{:T(128)} %bitcast.2, bf16[2,384,768]{2,1,0:T(8,128)(2,1)} %shard_map.59.mine_ref, bf16[2,384,768]{2,1,0:T(8,128)(2,1)} %shard_map.59.mine_ref), branch_computations={%region_0.1_spmd, %region_1.2_spmd} | conditional | bytes 4718640 | solution.py:250
  17.1 7.2 %collective-permute-start.1 = (bf16[2,384,768]{2,1,0:T(8,128)(2,1)}, bf16[2,384,768]{2,1,0:T(8,128)(2,1)}, u32[]{:S(2)}, u32[]{:S(2)}) collective-permute-start(bf16[2,384,768]{2,1,0:T(8,128)(2,1)} %param.1), channel_id=1, source_target_pairs={{0,32},{1,33},{2,34},{3,35},{4,36},{5,37},{6,38},{7,39},{8,40},{9,... | collective-permute-start | bytes 3538952 | tf_op jit(solution)/shard_map/cond/branch_1_fun/ppermute | solution.py:69
  24.3 2.8 %collective-permute-done.1 = bf16[2,384,768]{2,1,0:T(8,128)(2,1)} collective-permute-done((bf16[2,384,768]{2,1,0:T(8,128)(2,1)}, bf16[2,384,768]{2,1,0:T(8,128)(2,1)}, u32[]{:S(2)}, u32[]{:S(2)}) %collective-permute-start.1) | collective-permute-done | bytes 1179680 | tf_op jit(solution)/shard_map/cond/branch_1_fun/ppermute | solution.py:69
  27.1 2.7 %collective-permute-done.6.text_ref = bf16[384,768]{1,0:T(8,128)(2,1)S(1)} collective-permute-done((bf16[384,768]{1,0:T(8,128)(2,1)}, bf16[384,768]{1,0:T(8,128)(2,1)S(1)}, u32[]{:S(2)}, u32[]{:S(2)}) %collective-permute-start.6) | collective-permute-done | bytes 589856 | tf_op jit(solution)/shard_map/ppermute | solution.py:69
  29.8 7.4 %shard_map.60 = (s32[2]{0:T(128)S(1)}, bf16[384,768]{1,0:T(8,128)(2,1)}, bf16[384,768]{1,0:T(8,128)(2,1)S(1)}, bf16[384,768]{1,0:T(8,128)(2,1)S(1)}, bf16[384,76...) custom-call(s32[2]{0:T(128)S(1)} %pad_add_fusion.role, ...), custom_call_target="tpu_custom_call" | custom-call | tf_op jit(solution)/shard_map/pallas_call | solution.py:227
  37.2 10.0 %collective-permute-start.13 = (bf16[384,768]{1,0:T(8,128)(2,1)S(1)}, bf16[384,768]{1,0:T(8,128)(2,1)S(1)}, u32[]{:S(2)}, u32[]{:S(2)}) collective-permute-start(bf16[384,768]{1,0:T(8,128)(2,1)S(1)} %get-tuple-element.63), channel_id=1, source_target_pairs={{32,64},{33,65},{34,66},{35,67},{36,68},{37,69},{38,70},{39,71},{4... | collective-permute-start | bytes 1769480 | tf_op jit(solution)/shard_map/ppermute | solution.py:69
  47.2 1.9 %collective-permute-start.11 = (bf16[384,768]{1,0:T(8,128)(2,1)}, bf16[384,768]{1,0:T(8,128)(2,1)}, u32[]{:S(2)}, u32[]{:S(2)}) collective-permute-start(bf16[384,768]{1,0:T(8,128)(2,1)} %get-tuple-element.57), channel_id=1, source_target_pairs={{0,449},{1,448},{2,451},{3,450},{4,453},{5,452},{6,455},{7,454},{8... | collective-permute-start | bytes 1769480 | tf_op jit(solution)/shard_map/ppermute | solution.py:69
  49.2 1.5 %collective-permute-start.12 = (bf16[384,768]{1,0:T(8,128)(2,1)}, bf16[384,768]{1,0:T(8,128)(2,1)}, u32[]{:S(2)}, u32[]{:S(2)}) collective-permute-start(bf16[384,768]{1,0:T(8,128)(2,1)} %get-tuple-element.58), channel_id=1, source_target_pairs={{64,417},{65,416},{66,419},{67,418},{68,421},{69,420},{70,423},{71... | collective-permute-start | bytes 1769480 | tf_op jit(solution)/shard_map/ppermute | solution.py:69
  50.6 11.7 %collective-permute-start.14 = (bf16[384,768]{1,0:T(8,128)(2,1)}, bf16[384,768]{1,0:T(8,128)(2,1)S(1)}, u32[]{:S(2)}, u32[]{:S(2)}) collective-permute-start(bf16[384,768]{1,0:T(8,128)(2,1)} %get-tuple-element.65), channel_id=1, source_target_pairs={{32,64},{33,65},{34,66},{35,67},{36,68},{37,69},{38,70},{39,71},{4... | collective-permute-start | bytes 1769480 | tf_op jit(solution)/shard_map/ppermute | solution.py:69
  62.4 5.2 %shard_map.61 = (f32[384,768]{1,0:T(8,128)S(1)}, f32[384,768]{1,0:T(8,128)S(1)}, f32[384,768]{1,0:T(8,128)S(1)}, bf16[2,384,768]{2,1,0:T(8,128)(2,1)S(1)}) custom-call(s32[2]{0:T(128)S(1)} %get-tuple-element.52.role, f32[1]{0:T(128)S(6)} %copy.14.scale_ref, f32[1]{0:T(128)S(6)} %copy.15.bias_ref, bf16[384,768]{1,0:T(8,128)(2,1)S(1)} %copy-done, ...), custom_call_target="tpu_custom_call" | custom-call | tf_op jit(solution)/shard_map/pallas_call | solution.py:227
  67.5 7.0 %conditional.5 = (bf16[2,384,768]{2,1,0:T(8,128)(2,1)}, bf16[384,768]{1,0:T(8,128)(2,1)}) conditional(s32[]{:T(128)} %bitcast.2, (bf16[2,384,768]{2,1,0:T(8,128)(2,1)S(1)}, s32[2]{0:T(128)S(1)}, f32[384,768]{1,0:T(8,128)S(1)}, bf16[384,768]{1,0:T(8,128)(2,1)S(1)}) %tuple.28, (bf16[2,384,768]{2,1,0:T(8,128)(2,1)S(1)}, s32[2]{0:T(128)S(1)}, ...), branch_computations={%region_4.5_spmd, %region_5.6_spmd} | conditional | bytes 4718648 | solution.py:250
  67.6 1.9 %collective-permute-start.5 = (bf16[2,384,768]{2,1,0:T(8,128)(2,1)S(1)}, bf16[2,384,768]{2,1,0:T(8,128)(2,1)}, u32[]{:S(2)}, u32[]{:S(2)}) collective-permute-start(bf16[2,384,768]{2,1,0:T(8,128)(2,1)S(1)} %get-tuple-element.30), channel_id=1, source_target_pairs={{0,32},{1,33},{2,34},{3,35},{4,36},{5,37},{6,38},{7,39},{8,40},{9,... | collective-permute-start | bytes 3538952 | tf_op jit(solution)/shard_map/cond/branch_1_fun/ppermute | solution.py:69
  69.5 2.9 %collective-permute-done.5.cross_ref = bf16[2,384,768]{2,1,0:T(8,128)(2,1)} collective-permute-done((bf16[2,384,768]{2,1,0:T(8,128)(2,1)S(1)}, bf16[2,384,768]{2,1,0:T(8,128)(2,1)}, u32[]{:S(2)}, u32[]{:S(2)}) %collective-permute-start.5) | collective-permute-done | bytes 1179680 | tf_op jit(solution)/shard_map/cond/branch_1_fun/ppermute | solution.py:69
  72.4 2.2 %branch_1_fun.1 = bf16[384,768]{1,0:T(8,128)(2,1)} custom-call(s32[2]{0:T(128)S(1)} %get-tuple-element.31.role, f32[384,768]{1,0:T(8,128)S(1)} %get-tuple-element.32.sum_ref, bf16[2,384,768]{2,1,0:T(8,128)(2,1)} %collective-permute-done.5.cross_ref, bf16[384,768]{1,0:T(8,128)(2,1)S(1)} %get-tuple-element.33.back_ref), custom_call_target="tpu_custom_call" | custom-call | tf_op jit(solution)/shard_map/cond/branch_1_fun/pallas_call | solution.py:291
  74.6 4.5 %collective-permute-start.15 = (bf16[384,768]{1,0:T(8,128)(2,1)}, bf16[384,768]{1,0:T(8,128)(2,1)}, u32[]{:S(2)}, u32[]{:S(2)}) collective-permute-start(bf16[384,768]{1,0:T(8,128)(2,1)} %get-tuple-element.66), channel_id=1, source_target_pairs={{0,1},{1,0},{2,3},{3,2},{4,5},{5,4},{6,7},{7,6},{8,9},{9,8},{10,11... | collective-permute-start | bytes 1769480 | tf_op jit(solution)/shard_map/ppermute | solution.py:69
  79.1 1.5 %conditional.4 = (bf16[384,768]{1,0:T(8,128)(2,1)}) conditional(s32[]{:T(128)} %bitcast.2, bf16[384,768]{1,0:T(8,128)(2,1)} %collective-permute-done.11.near_back, bf16[384,768]{1,0:T(8,128)(2,1)} %collective-permute-done.11.near_back), branch_computations={%region_2.3_spmd, %region_3.4_spmd} | conditional | bytes 2359344 | solution.py:250
  79.1 1.5 %collective-permute-start.3 = (bf16[384,768]{1,0:T(8,128)(2,1)}, bf16[384,768]{1,0:T(8,128)(2,1)}, u32[]{:S(2)}, u32[]{:S(2)}) collective-permute-start(bf16[384,768]{1,0:T(8,128)(2,1)} %param.3), channel_id=1, source_target_pairs={{224,481},{225,480},{226,483},{227,482},{228,485},{229,484},{230,4... | collective-permute-start | bytes 1769480 | tf_op jit(solution)/shard_map/cond/branch_1_fun/ppermute | solution.py:69
  80.6 3.0 %shard_map.62 = (s32[2]{0:T(128)S(1)}, f32[384,768]{1,0:T(8,128)}) custom-call(s32[2]{0:T(128)S(1)} %get-tuple-element.52.role, bf16[384,768]{1,0:T(8,128)(2,1)S(1)} %copy-done, f32[384,768]{1,0:T(8,128)S(1)} %get-tuple-element.56.text_sum, bf16[384,768]{1,0:T(8,128)(2,1)} %collective-permute-done.11.near_back, ...), custom_call_target="tpu_custom_call" | custom-call | tf_op jit(solution)/shard_map/pallas_call | solution.py:227
  85.0 7.9 %collective-permute-done.15.from_partner = bf16[384,768]{1,0:T(8,128)(2,1)} collective-permute-done((bf16[384,768]{1,0:T(8,128)(2,1)}, bf16[384,768]{1,0:T(8,128)(2,1)}, u32[]{:S(2)}, u32[]{:S(2)}) %collective-permute-start.15) | collective-permute-done | bytes 589856 | tf_op jit(solution)/shard_map/ppermute | solution.py:69
  93.0 2.5 %shard_map.64 = f32[384,768]{1,0:T(8,128)} custom-call(s32[2]{0:T(128)S(1)} %get-tuple-element.59.role, bf16[384,768]{1,0:T(8,128)(2,1)S(1)} %copy-done.2, f32[384,768]{1,0:T(8,128)S(1)} %shard_map.63.image_sum, bf16[384,768]{1,0:T(8,128)(2,1)} %collective-permute-done.15.from_partner), custom_call_target="tpu_custom_call" | custom-call | tf_op jit(solution)/shard_map/pallas_call | solution.py:227
  (19 shorter events, 5.8 us)
Async XLA Ops:
  0.6 14.1 %collective-permute-start.7 = (bf16[384,768]{1,0:T(8,128)(2,1)}, bf16[384,768]{1,0:T(8,128)(2,1)S(1)}, u32[]{:S(2)}, u32[]{:S(2)}) collective-permute-start(bf16[384,768]{1,0:T(8,128)(2,1)} %images.1), channel_id=1, source_target_pairs={{0,1},{1,0},{2,3},{3,2},{4,5},{5,4},{6,7},{7,6},{8,9},{9,8},{10,11... | collective-permute-start | bytes 1769480 | tf_op jit(solution)/shard_map/ppermute | solution.py:69
  5.5 21.6 %collective-permute-start.10 = (bf16[384,768]{1,0:T(8,128)(2,1)}, bf16[384,768]{1,0:T(8,128)(2,1)S(1)}, u32[]{:S(2)}, u32[]{:S(2)}) collective-permute-start(bf16[384,768]{1,0:T(8,128)(2,1)} %texts.1), channel_id=1, source_target_pairs={{160,321},{161,320},{162,323},{163,322},{164,325},{165,324},{166,3... | collective-permute-start | bytes 1769480 | tf_op jit(solution)/shard_map/ppermute | solution.py:69
  6.2 23.6 %collective-permute-start.6 = (bf16[384,768]{1,0:T(8,128)(2,1)}, bf16[384,768]{1,0:T(8,128)(2,1)S(1)}, u32[]{:S(2)}, u32[]{:S(2)}) collective-permute-start(bf16[384,768]{1,0:T(8,128)(2,1)} %texts.1), channel_id=1, source_target_pairs={{0,64},{1,65},{2,66},{3,67},{4,68},{5,69},{6,70},{7,71},{8,72},{9,... | collective-permute-start | bytes 1769480 | tf_op jit(solution)/shard_map/ppermute | solution.py:69
  9.3 20.5 %collective-permute-start.8 = (bf16[384,768]{1,0:T(8,128)(2,1)}, bf16[384,768]{1,0:T(8,128)(2,1)S(1)}, u32[]{:S(2)}, u32[]{:S(2)}) collective-permute-start(bf16[384,768]{1,0:T(8,128)(2,1)} %images.1), channel_id=1, source_target_pairs={{0,64},{1,65},{2,66},{3,67},{4,68},{5,69},{6,70},{7,71},{8,72},{9,... | collective-permute-start | bytes 1769480 | tf_op jit(solution)/shard_map/ppermute | solution.py:69
  10.6 19.2 %collective-permute-start.9 = (bf16[384,768]{1,0:T(8,128)(2,1)}, bf16[384,768]{1,0:T(8,128)(2,1)S(1)}, u32[]{:S(2)}, u32[]{:S(2)}) collective-permute-start(bf16[384,768]{1,0:T(8,128)(2,1)} %images.1), channel_id=1, source_target_pairs={{0,65},{1,64},{2,67},{3,66},{4,69},{5,68},{6,71},{7,70},{8,73},{9,... | collective-permute-start | bytes 1769480 | tf_op jit(solution)/shard_map/ppermute | solution.py:69
  14.7 1.1 %copy-start.1 = (bf16[384,768]{1,0:T(8,128)(2,1)S(1)}, bf16[384,768]{1,0:T(8,128)(2,1)}, u32[]{:S(2)}) copy-start(bf16[384,768]{1,0:T(8,128)(2,1)} %images.1) | copy-start | bytes 1769476
  17.1 10.0 %collective-permute-start.1 = (bf16[2,384,768]{2,1,0:T(8,128)(2,1)}, bf16[2,384,768]{2,1,0:T(8,128)(2,1)}, u32[]{:S(2)}, u32[]{:S(2)}) collective-permute-start(bf16[2,384,768]{2,1,0:T(8,128)(2,1)} %param.1), channel_id=1, source_target_pairs={{0,32},{1,33},{2,34},{3,35},{4,36},{5,37},{6,38},{7,39},{8,40},{9,... | collective-permute-start | bytes 3538952 | tf_op jit(solution)/shard_map/cond/branch_1_fun/ppermute | solution.py:69
  27.1 35.2 %copy-start = (bf16[384,768]{1,0:T(8,128)(2,1)S(1)}, bf16[384,768]{1,0:T(8,128)(2,1)}, u32[]{:S(2)}) copy-start(bf16[384,768]{1,0:T(8,128)(2,1)} %texts.1) | copy-start | bytes 1769476
  37.2 30.4 %collective-permute-start.13 = (bf16[384,768]{1,0:T(8,128)(2,1)S(1)}, bf16[384,768]{1,0:T(8,128)(2,1)S(1)}, u32[]{:S(2)}, u32[]{:S(2)}) collective-permute-start(bf16[384,768]{1,0:T(8,128)(2,1)S(1)} %get-tuple-element.63), channel_id=1, source_target_pairs={{32,64},{33,65},{34,66},{35,67},{36,68},{37,69},{38,70},{39,71},{4... | collective-permute-start | bytes 1769480 | tf_op jit(solution)/shard_map/ppermute | solution.py:69
  47.2 31.9 %collective-permute-start.11 = (bf16[384,768]{1,0:T(8,128)(2,1)}, bf16[384,768]{1,0:T(8,128)(2,1)}, u32[]{:S(2)}, u32[]{:S(2)}) collective-permute-start(bf16[384,768]{1,0:T(8,128)(2,1)} %get-tuple-element.57), channel_id=1, source_target_pairs={{0,449},{1,448},{2,451},{3,450},{4,453},{5,452},{6,455},{7,454},{8... | collective-permute-start | bytes 1769480 | tf_op jit(solution)/shard_map/ppermute | solution.py:69
  49.2 31.5 %collective-permute-start.12 = (bf16[384,768]{1,0:T(8,128)(2,1)}, bf16[384,768]{1,0:T(8,128)(2,1)}, u32[]{:S(2)}, u32[]{:S(2)}) collective-permute-start(bf16[384,768]{1,0:T(8,128)(2,1)} %get-tuple-element.58), channel_id=1, source_target_pairs={{64,417},{65,416},{66,419},{67,418},{68,421},{69,420},{70,423},{71... | collective-permute-start | bytes 1769480 | tf_op jit(solution)/shard_map/ppermute | solution.py:69
  50.6 33.0 %collective-permute-start.14 = (bf16[384,768]{1,0:T(8,128)(2,1)}, bf16[384,768]{1,0:T(8,128)(2,1)S(1)}, u32[]{:S(2)}, u32[]{:S(2)}) collective-permute-start(bf16[384,768]{1,0:T(8,128)(2,1)} %get-tuple-element.65), channel_id=1, source_target_pairs={{32,64},{33,65},{34,66},{35,67},{36,68},{37,69},{38,70},{39,71},{4... | collective-permute-start | bytes 1769480 | tf_op jit(solution)/shard_map/ppermute | solution.py:69
  67.6 4.9 %collective-permute-start.5 = (bf16[2,384,768]{2,1,0:T(8,128)(2,1)S(1)}, bf16[2,384,768]{2,1,0:T(8,128)(2,1)}, u32[]{:S(2)}, u32[]{:S(2)}) collective-permute-start(bf16[2,384,768]{2,1,0:T(8,128)(2,1)S(1)} %get-tuple-element.30), channel_id=1, source_target_pairs={{0,32},{1,33},{2,34},{3,35},{4,36},{5,37},{6,38},{7,39},{8,40},{9,... | collective-permute-start | bytes 3538952 | tf_op jit(solution)/shard_map/cond/branch_1_fun/ppermute | solution.py:69
  74.6 18.4 %collective-permute-start.15 = (bf16[384,768]{1,0:T(8,128)(2,1)}, bf16[384,768]{1,0:T(8,128)(2,1)}, u32[]{:S(2)}, u32[]{:S(2)}) collective-permute-start(bf16[384,768]{1,0:T(8,128)(2,1)} %get-tuple-element.66), channel_id=1, source_target_pairs={{0,1},{1,0},{2,3},{3,2},{4,5},{5,4},{6,7},{7,6},{8,9},{9,8},{10,11... | collective-permute-start | bytes 1769480 | tf_op jit(solution)/shard_map/ppermute | solution.py:69
  79.1 1.5 %collective-permute-start.3 = (bf16[384,768]{1,0:T(8,128)(2,1)}, bf16[384,768]{1,0:T(8,128)(2,1)}, u32[]{:S(2)}, u32[]{:S(2)}) collective-permute-start(bf16[384,768]{1,0:T(8,128)(2,1)} %param.3), channel_id=1, source_target_pairs={{224,481},{225,480},{226,483},{227,482},{228,485},{229,484},{230,4... | collective-permute-start | bytes 1769480 | tf_op jit(solution)/shard_map/cond/branch_1_fun/ppermute | solution.py:69
  83.7 9.3 %copy-start.2 = (bf16[384,768]{1,0:T(8,128)(2,1)S(1)}, bf16[384,768]{1,0:T(8,128)(2,1)}, u32[]{:S(2)}) copy-start(bf16[384,768]{1,0:T(8,128)(2,1)} %images.1) | copy-start | bytes 1769476

commit v6 on v5

--- a/solution.py
+++ b/solution.py
@@ -159,35 +159,25 @@
     grad_ref[...] = total[...].astype(grad_ref.dtype)
 
 
-def own_kernel(
-    role, scale_ref, bias_ref, text_ref, mine_ref, theirs_ref, hat_ref,
-    mine_slopes_ref, theirs_slopes_ref,
-    text_sum_ref, mine_sum_ref, partner_sum_ref, cross_ref,
+def sent_kernel(
+    role, scale_ref, bias_ref, text_ref, mine_ref, theirs_ref, hat_ref, mine_slopes_ref, theirs_slopes_ref,
+    cross_ref, partner_sum_ref, slopes_ref,
 ):
     scale, bias = scale_ref[0], bias_ref[0]
     rows, width = text_ref.shape
-    near_hat = hat_ref[...]
     text_hat = hat(text_ref[...])
-    same = (
-        lax.broadcasted_iota(jnp.int32, (rows, 2 * rows), 0)
-        == lax.broadcasted_iota(jnp.int32, (rows, 2 * rows), 1)
-    ).astype(jnp.float32)
-    images = rows_of(mine_ref)
-    slopes = slopes_of(text_hat, images, scale, bias, same)
-    text_sum_ref[...] = dot(slopes, images, 1, 0)
-    for slot, out_ref in enumerate((mine_sum_ref, partner_sum_ref)):
-        at = slice(slot * rows, (slot + 1) * rows)
-        out_ref[...] = dot(slopes[:, at], text_hat, 0, 0) + dot(mine_slopes_ref[:, at], near_hat, 0, 0)
+    slopes = slopes_of(text_hat, mine_ref[1], scale, bias)
+    slopes_ref[:, :rows] = slopes
+    partner_sum_ref[...] = dot(slopes, text_hat, 0, 0) + dot(mine_slopes_ref[:, rows:], hat_ref[...], 0, 0)
 
     @pl.when(role[0] == 0)
     def _():
         text_hat = hat(text_ref[...])
-        images = rows_of(theirs_ref)
-        own = slopes_of(text_hat, images, scale, bias)
-        text_sum_ref[...] += dot(own, images, 1, 0)
+        slopes = slopes_of(text_hat, rows_of(theirs_ref), scale, bias)
+        slopes_ref[:, rows:] = slopes
         for slot in range(2):
             at = slice(slot * rows, (slot + 1) * rows)
-            total = dot(theirs_slopes_ref[:, at], hat_ref[...], 0, 0) + dot(own[:, at], text_hat, 0, 0)
+            total = dot(theirs_slopes_ref[:, at], hat_ref[...], 0, 0) + dot(slopes[:, at], text_hat, 0, 0)
             cross_ref[slot] = total.astype(cross_ref.dtype)
 
     @pl.when(role[0] == 1)
@@ -195,6 +185,31 @@
         for slot in range(2):
             at = slice(slot * rows, (slot + 1) * rows)
             cross_ref[slot] = dot(theirs_slopes_ref[:, at], hat_ref[...], 0, 0).astype(cross_ref.dtype)
+
+
+def kept_kernel(
+    role, scale_ref, bias_ref, text_ref, mine_ref, theirs_ref, hat_ref, slopes_ref, mine_slopes_ref, cross_ref, back_ref,
+    text_sum_ref, image_sum_ref,
+):
+    scale, bias = scale_ref[0], bias_ref[0]
+    rows, width = hat_ref.shape
+    text_hat = hat(text_ref[...])
+    same = (
+        lax.broadcasted_iota(jnp.int32, (rows, rows), 0) == lax.broadcasted_iota(jnp.int32, (rows, rows), 1)
+    ).astype(jnp.float32)
+    slopes = slopes_of(text_hat, mine_ref[0], scale, bias, same)
+    even = 1.0 - is_odd(role).astype(jnp.float32)
+    image_sum_ref[...] = (
+        dot(slopes, text_hat, 0, 0)
+        + dot(mine_slopes_ref[:, :rows], hat_ref[...], 0, 0)
+        + cross_ref[0].astype(jnp.float32)
+        + even * back_ref[...].astype(jnp.float32)
+    )
+    text_sum_ref[...] = dot(slopes, mine_ref[0], 1, 0) + dot(slopes_ref[:, :rows], mine_ref[1], 1, 0)
+
+    @pl.when(role[0] == 0)
+    def _():
+        text_sum_ref[...] += dot(slopes_ref[:, rows:], rows_of(theirs_ref), 1, 0)
 
 
 def partner_kernel(role, sum_ref, cross_ref, back_ref, out_ref):
@@ -272,11 +287,10 @@
     far_back = move(far_grad, far_to, True)
     back_partner = move(back_partner, guest_to, True)
     back = move(back, guest_to, True)
-    text_sum, mine_sum, partner_sum, cross = call(
-        own_kernel,
-        [full, full, full, half_pair],
+    cross, partner_sum, own_slopes = call(
+        sent_kernel,
+        [half_pair, full, bf16((rows, 3 * rows))],
         *scalars, texts, mine, theirs, near_hat, mine_slopes, theirs_slopes,
-        mib=24,
     )
 
     def sum_with_cross(kernel, slot, dtype, *operands):
@@ -303,8 +317,13 @@
 
     cross, for_partner = together(across, cross, role, partner_sum, back_partner)
     from_partner = move(for_partner, partner)
-    last_back = together(lambda values: move(values, over_z), near_back)
-    image_sum = sum_with_cross(partner_kernel, 0, jnp.float32, role, mine_sum, cross, back)
+    def over(near_back, *kept):
+        text_sum, image_sum = call(kept_kernel, [full, full], *kept, mib=20)
+        return move(near_back, over_z), text_sum, image_sum
+
+    last_back, text_sum, image_sum = together(
+        over, near_back, *scalars, texts, mine, theirs, near_hat, own_slopes, mine_slopes, cross, back
+    )
     role, text_grad = call(
         text_final_kernel,
         [jax.ShapeDtypeStruct((2,), jnp.int32), full],

time: 96.2 us -> 94.6 us (0.983)
  waiting for transfers between devices: 17.8 us -> 14.3 us
  Pallas kernels: 23 us -> 24.4 us
  local copies, waits for them, and re-layouts: 1.07 us -> 2.1 us
    ppermute x13, waiting for transfers between devices: 17.8 us -> 14.3 us  [move(): return lax.ppermute(values, AXES, sorted(pairs))]
    pallas_call x5 -> x6, Pallas kernels: 19.5 us -> 22.3 us  [call(): pl.pallas_call(kernel, in_specs=[SMEM] * scalars + [WHOLE] * (len(operand...]
    pallas_call x2 -> x1, Pallas kernels: 3.48 us -> 2.1 us  [sum_with_cross(): pl.pallas_call(kernel, grid=(1,), in_specs=specs, out_specs=pl.BlockSpec(...]
    unnamed x6 -> x16, local copies, waits for them, and re-layouts: 1.07 us -> 2.1 us
  transfers between devices with their start and end apart: 13 -> 13, of which waited for: 5 -> 5; matrix products, arithmetic and copies ran while one was open for 0% -> 0% of each run, Pallas kernels for 14% -> 16%
where the time goes in v6:
time: 94.6 us; the launch traced here: 94 us
  starting transfers between devices  50.6 us (53%)
  Pallas kernels  24.4 us (26%)
  waiting for transfers between devices  14.3 us (15%)
  between operations  2.17 us (2%)
  local copies, waits for them, and re-layouts  2.1 us (2%)
    ppermute x13, starting transfers between devices, move(): return lax.ppermute(values, AXES, sorted(pairs))  50.6 us
    pallas_call x6, Pallas kernels, call(): pl.pallas_call(kernel, in_specs=[SMEM] * scalars + [WHOLE] * (len(operand...  22.3 us
    ppermute x13, waiting for transfers between devices, move(): return lax.ppermute(values, AXES, sorted(pairs))  14.3 us
    unnamed x16, local copies, waits for them, and re-layouts  2.1 us
    pallas_call x1, Pallas kernels, sum_with_cross(): pl.pallas_call(kernel, grid=(1,), in_specs=specs, out_specs=pl.BlockSpec(...  2.1 us
  transfers between devices with their start and end apart: 13, of which 5 were waited for; matrix products, arithmetic and copies ran while one was open for 0% of the time, Pallas kernels for 16%

profile of v6, /device:TPU:1, one launch (start us, length us, event | category | flops | bytes accessed | tf_op | source)
XLA Modules:
  0.0 94.0 jit_solution(17498024565392559186)
XLA Ops:
  0.6 4.8 %collective-permute-start.7 = (bf16[384,768]{1,0:T(8,128)(2,1)}, bf16[384,768]{1,0:T(8,128)(2,1)S(1)}, u32[]{:S(2)}, u32[]{:S(2)}) collective-permute-start(bf16[384,768]{1,0:T(8,128)(2,1)} %images.1), channel_id=1, source_target_pairs={{0,1},{1,0},{2,3},{3,2},{4,5},{5,4},{6,7},{7,6},{8,9},{9,8},{10,11... | collective-permute-start | bytes 1769480 | tf_op jit(solution)/shard_map/ppermute | solution.py:69
  5.5 1.3 %collective-permute-start.8 = (bf16[384,768]{1,0:T(8,128)(2,1)}, bf16[384,768]{1,0:T(8,128)(2,1)S(1)}, u32[]{:S(2)}, u32[]{:S(2)}) collective-permute-start(bf16[384,768]{1,0:T(8,128)(2,1)} %images.1), channel_id=1, source_target_pairs={{0,64},{1,65},{2,66},{3,67},{4,68},{5,69},{6,70},{7,71},{8,72},{9,... | collective-permute-start | bytes 1769480 | tf_op jit(solution)/shard_map/ppermute | solution.py:69
  8.8 3.1 %collective-permute-start.6 = (bf16[384,768]{1,0:T(8,128)(2,1)}, bf16[384,768]{1,0:T(8,128)(2,1)S(1)}, u32[]{:S(2)}, u32[]{:S(2)}) collective-permute-start(bf16[384,768]{1,0:T(8,128)(2,1)} %texts.1), channel_id=1, source_target_pairs={{0,64},{1,65},{2,66},{3,67},{4,68},{5,69},{6,70},{7,71},{8,72},{9,... | collective-permute-start | bytes 1769480 | tf_op jit(solution)/shard_map/ppermute | solution.py:69
  13.3 1.4 %collective-permute-done.7.partner_ref = bf16[384,768]{1,0:T(8,128)(2,1)S(1)} collective-permute-done((bf16[384,768]{1,0:T(8,128)(2,1)}, bf16[384,768]{1,0:T(8,128)(2,1)S(1)}, u32[]{:S(2)}, u32[]{:S(2)}) %collective-permute-start.7) | collective-permute-done | bytes 589856 | tf_op jit(solution)/shard_map/ppermute | solution.py:69
  17.1 9.7 %conditional.3 = (bf16[2,384,768]{2,1,0:T(8,128)(2,1)}) conditional(s32[]{:T(128)} %bitcast.2, bf16[2,384,768]{2,1,0:T(8,128)(2,1)S(1)} %shard_map.59.mine_ref, bf16[2,384,768]{2,1,0:T(8,128)(2,1)S(1)} %shard_map.59.mine_ref), branch_computations={%region_0.1_spmd, %region_1.2_spmd} | conditional | bytes 4718640 | solution.py:265
  17.1 7.2 %collective-permute-start.1 = (bf16[2,384,768]{2,1,0:T(8,128)(2,1)S(1)}, bf16[2,384,768]{2,1,0:T(8,128)(2,1)}, u32[]{:S(2)}, u32[]{:S(2)}) collective-permute-start(bf16[2,384,768]{2,1,0:T(8,128)(2,1)S(1)} %param.1), channel_id=1, source_target_pairs={{0,32},{1,33},{2,34},{3,35},{4,36},{5,37},{6,38},{7,39},{8,40},{9,... | collective-permute-start | bytes 3538952 | tf_op jit(solution)/shard_map/cond/branch_1_fun/ppermute | solution.py:69
  24.3 2.6 %collective-permute-done.1 = bf16[2,384,768]{2,1,0:T(8,128)(2,1)} collective-permute-done((bf16[2,384,768]{2,1,0:T(8,128)(2,1)S(1)}, bf16[2,384,768]{2,1,0:T(8,128)(2,1)}, u32[]{:S(2)}, u32[]{:S(2)}) %collective-permute-start.1) | collective-permute-done | bytes 1179680 | tf_op jit(solution)/shard_map/cond/branch_1_fun/ppermute | solution.py:69
  26.9 4.8 %collective-permute-done.6.text_ref = bf16[384,768]{1,0:T(8,128)(2,1)S(1)} collective-permute-done((bf16[384,768]{1,0:T(8,128)(2,1)}, bf16[384,768]{1,0:T(8,128)(2,1)S(1)}, u32[]{:S(2)}, u32[]{:S(2)}) %collective-permute-start.6) | collective-permute-done | bytes 589856 | tf_op jit(solution)/shard_map/ppermute | solution.py:69
  31.7 7.0 %shard_map.60 = (s32[2]{0:T(128)S(1)}, bf16[384,768]{1,0:T(8,128)(2,1)}, bf16[384,768]{1,0:T(8,128)(2,1)S(1)}, bf16[384,768]{1,0:T(8,128)(2,1)S(1)}, bf16[384,76...) custom-call(s32[2]{0:T(128)S(1)} %pad_add_fusion.role, ...), custom_call_target="tpu_custom_call" | custom-call | tf_op jit(solution)/shard_map/pallas_call | solution.py:242
  38.7 9.8 %collective-permute-start.12 = (bf16[384,768]{1,0:T(8,128)(2,1)S(1)}, bf16[384,768]{1,0:T(8,128)(2,1)S(1)}, u32[]{:S(2)}, u32[]{:S(2)}) collective-permute-start(bf16[384,768]{1,0:T(8,128)(2,1)S(1)} %get-tuple-element.133), channel_id=1, source_target_pairs={{32,64},{33,65},{34,66},{35,67},{36,68},{37,69},{38,70},{39,71},{4... | collective-permute-start | bytes 1769480 | tf_op jit(solution)/shard_map/ppermute | solution.py:69
  48.5 2.9 %collective-permute-start.11 = (bf16[384,768]{1,0:T(8,128)(2,1)}, bf16[384,768]{1,0:T(8,128)(2,1)}, u32[]{:S(2)}, u32[]{:S(2)}) collective-permute-start(bf16[384,768]{1,0:T(8,128)(2,1)} %get-tuple-element.126), channel_id=1, source_target_pairs={{0,449},{1,448},{2,451},{3,450},{4,453},{5,452},{6,455},{7,454},{8... | collective-permute-start | bytes 1769480 | tf_op jit(solution)/shard_map/ppermute | solution.py:69
  51.4 2.1 %collective-permute-start.13 = (bf16[384,768]{1,0:T(8,128)(2,1)S(1)}, bf16[384,768]{1,0:T(8,128)(2,1)}, u32[]{:S(2)}, u32[]{:S(2)}) collective-permute-start(bf16[384,768]{1,0:T(8,128)(2,1)S(1)} %get-tuple-element.135), channel_id=1, source_target_pairs={{32,64},{33,65},{34,66},{35,67},{36,68},{37,69},{38,70},{39,71},{4... | collective-permute-start | bytes 1769480 | tf_op jit(solution)/shard_map/ppermute | solution.py:69
  54.3 4.2 %shard_map.61 = (bf16[2,384,768]{2,1,0:T(8,128)(2,1)S(1)}, f32[384,768]{1,0:T(8,128)S(1)}, bf16[384,1152]{1,0:T(8,128)(2,1)}) custom-call(s32[2]{0:T(128)S(1)} %get-tuple-element.125.role, f32[1]{0:T(128)S(6)} %copy.18.scale_ref, f32[1]{0:T(128)S(6)} %copy.19.bias_ref, bf16[384,768]{1,0:T(8,128)(2,1)S(1)} %copy-done.5, bf16[2,384,768]{2,1,0:T(8,128)(2,1)S(1)} %copy-done.3, ...), custom_call_target="tpu_custom_call" | custom-call | tf_op jit(solution)/shard_map/pallas_call | solution.py:242
  58.5 12.8 %conditional.4 = (bf16[2,384,768]{2,1,0:T(8,128)(2,1)}, bf16[384,768]{1,0:T(8,128)(2,1)}) conditional(s32[]{:T(128)} %bitcast.2, (bf16[2,384,768]{2,1,0:T(8,128)(2,1)S(1)}, s32[2]{0:T(128)S(1)}, f32[384,768]{1,0:T(8,128)S(1)}, bf16[384,768]{1,0:T(8,128)(2,1)S(1)}) %tuple.30, (bf16[2,384,768]{2,1,0:T(8,128)(2,1)S(1)}, s32[2]{0:T(128)S(1)}, ...), branch_computations={%region_2.3_spmd, %region_3.4_spmd} | conditional | bytes 4718648 | solution.py:265
  58.5 8.1 %collective-permute-start.3 = (bf16[2,384,768]{2,1,0:T(8,128)(2,1)S(1)}, bf16[2,384,768]{2,1,0:T(8,128)(2,1)}, u32[]{:S(2)}, u32[]{:S(2)}) collective-permute-start(bf16[2,384,768]{2,1,0:T(8,128)(2,1)S(1)} %get-tuple-element.73), channel_id=1, source_target_pairs={{0,32},{1,33},{2,34},{3,35},{4,36},{5,37},{6,38},{7,39},{8,40},{9,... | collective-permute-start | bytes 3538952 | tf_op jit(solution)/shard_map/cond/branch_1_fun/ppermute | solution.py:69
  66.6 2.6 %collective-permute-done.3.cross_ref = bf16[2,384,768]{2,1,0:T(8,128)(2,1)} collective-permute-done((bf16[2,384,768]{2,1,0:T(8,128)(2,1)S(1)}, bf16[2,384,768]{2,1,0:T(8,128)(2,1)}, u32[]{:S(2)}, u32[]{:S(2)}) %collective-permute-start.3) | collective-permute-done | bytes 1179680 | tf_op jit(solution)/shard_map/cond/branch_1_fun/ppermute | solution.py:69
  69.2 2.1 %branch_1_fun.2 = bf16[384,768]{1,0:T(8,128)(2,1)} custom-call(s32[2]{0:T(128)S(1)} %get-tuple-element.74.role, f32[384,768]{1,0:T(8,128)S(1)} %get-tuple-element.75.sum_ref, bf16[2,384,768]{2,1,0:T(8,128)(2,1)} %collective-permute-done.3.cross_ref, bf16[384,768]{1,0:T(8,128)(2,1)S(1)} %get-tuple-element.76.back_ref), custom_call_target="tpu_custom_call" | custom-call | tf_op jit(solution)/shard_map/cond/branch_1_fun/pallas_call | solution.py:305
  71.3 7.0 %collective-permute-start.15 = (bf16[384,768]{1,0:T(8,128)(2,1)}, bf16[384,768]{1,0:T(8,128)(2,1)S(1)}, u32[]{:S(2)}, u32[]{:S(2)}) collective-permute-start(bf16[384,768]{1,0:T(8,128)(2,1)} %get-tuple-element.141), channel_id=1, source_target_pairs={{0,1},{1,0},{2,3},{3,2},{4,5},{5,4},{6,7},{7,6},{8,9},{9,8},{10,11... | collective-permute-start | bytes 1769480 | tf_op jit(solution)/shard_map/ppermute | solution.py:69
  78.4 7.4 %conditional.5 = (bf16[384,768]{1,0:T(8,128)(2,1)}, f32[384,768]{1,0:T(8,128)S(1)}, f32[384,768]{1,0:T(8,128)S(1)}) conditional(s32[]{:T(128)} %bitcast.2, (bf16[384,768]{1,0:T(8,128)(2,1)}, s32[2]{0:T(128)S(1)}, f32[1]{0:T(128)}, f32[1]{0:T(128)}, bf16[384,768]{1,0:T(8,128)(2,1)}, /*index=5*/bf16[2,384,768]{2,1,0:T(8,128)(2,1)S(1)}, ...), branch_computations={%region_4.5_spmd, %region_5.6_spmd} | conditional | bytes 2359360 | solution.py:265
  78.6 1.5 %collective-permute-start.5 = (bf16[384,768]{1,0:T(8,128)(2,1)}, bf16[384,768]{1,0:T(8,128)(2,1)}, u32[]{:S(2)}, u32[]{:S(2)}) collective-permute-start(bf16[384,768]{1,0:T(8,128)(2,1)} %get-tuple-element.91), channel_id=1, source_target_pairs={{224,481},{225,480},{226,483},{227,482},{228,485},{229,484},{230,4... | collective-permute-start | bytes 1769480 | tf_op jit(solution)/shard_map/cond/branch_1_fun/ppermute | solution.py:69
  80.1 5.7 %branch_1_fun.3 = (f32[384,768]{1,0:T(8,128)S(1)}, f32[384,768]{1,0:T(8,128)S(1)}) custom-call(s32[2]{0:T(128)S(1)} %get-tuple-element.92.role, f32[1]{0:T(128)} %get-tuple-element.93.scale_ref, f32[1]{0:T(128)} %get-tuple-element.94.bias_ref, bf16[384,768]{1,0:T(8,128)(2,1)} %get-tuple-element.95.text_ref, ...), custom_call_target="tpu_custom_call" | custom-call | tf_op jit(solution)/shard_map/cond/branch_1_fun/pallas_call | solution.py:242
  85.8 3.1 %shard_map.62 = (s32[2]{0:T(128)S(1)}, f32[384,768]{1,0:T(8,128)}) custom-call(s32[2]{0:T(128)S(1)} %get-tuple-element.125.role, bf16[384,768]{1,0:T(8,128)(2,1)} %texts.1, f32[384,768]{1,0:T(8,128)S(1)} %get-tuple-element.136.text_sum, bf16[384,768]{1,0:T(8,128)(2,1)} %collective-permute-done.11.near_back, bf16[384,768]{1,0:T(8,128)(2,1)} %get-tuple-element.137.last_back, ...), custom_call_target="tpu_custom_call" | custom-call | tf_op jit(solution)/shard_map/pallas_call | solution.py:242
  88.9 3.0 %collective-permute-done.15.from_partner = bf16[384,768]{1,0:T(8,128)(2,1)S(1)} collective-permute-done((bf16[384,768]{1,0:T(8,128)(2,1)}, bf16[384,768]{1,0:T(8,128)(2,1)S(1)}, u32[]{:S(2)}, u32[]{:S(2)}) %collective-permute-start.15) | collective-permute-done | bytes 589856 | tf_op jit(solution)/shard_map/ppermute | solution.py:69
  92.0 2.0 %shard_map.63 = f32[384,768]{1,0:T(8,128)} custom-call(s32[2]{0:T(128)S(1)} %get-tuple-element.139.role, bf16[384,768]{1,0:T(8,128)(2,1)S(1)} %copy-done.1, f32[384,768]{1,0:T(8,128)S(1)} %get-tuple-element.140.image_sum, bf16[384,768]{1,0:T(8,128)(2,1)S(1)} %collective-permute-done.15.from_partner), custom_call_target="tpu_custom_call" | custom-call | tf_op jit(solution)/shard_map/pallas_call | solution.py:242
  (29 shorter events, 5.2 us)
Async XLA Ops:
  0.6 14.1 %collective-permute-start.7 = (bf16[384,768]{1,0:T(8,128)(2,1)}, bf16[384,768]{1,0:T(8,128)(2,1)S(1)}, u32[]{:S(2)}, u32[]{:S(2)}) collective-permute-start(bf16[384,768]{1,0:T(8,128)(2,1)} %images.1), channel_id=1, source_target_pairs={{0,1},{1,0},{2,3},{3,2},{4,5},{5,4},{6,7},{7,6},{8,9},{9,8},{10,11... | collective-permute-start | bytes 1769480 | tf_op jit(solution)/shard_map/ppermute | solution.py:69
  5.5 21.4 %collective-permute-start.8 = (bf16[384,768]{1,0:T(8,128)(2,1)}, bf16[384,768]{1,0:T(8,128)(2,1)S(1)}, u32[]{:S(2)}, u32[]{:S(2)}) collective-permute-start(bf16[384,768]{1,0:T(8,128)(2,1)} %images.1), channel_id=1, source_target_pairs={{0,64},{1,65},{2,66},{3,67},{4,68},{5,69},{6,70},{7,71},{8,72},{9,... | collective-permute-start | bytes 1769480 | tf_op jit(solution)/shard_map/ppermute | solution.py:69
  6.8 20.1 %collective-permute-start.9 = (bf16[384,768]{1,0:T(8,128)(2,1)}, bf16[384,768]{1,0:T(8,128)(2,1)S(1)}, u32[]{:S(2)}, u32[]{:S(2)}) collective-permute-start(bf16[384,768]{1,0:T(8,128)(2,1)} %images.1), channel_id=1, source_target_pairs={{0,65},{1,64},{2,67},{3,66},{4,69},{5,68},{6,71},{7,70},{8,73},{9,... | collective-permute-start | bytes 1769480 | tf_op jit(solution)/shard_map/ppermute | solution.py:69
  8.1 18.8 %collective-permute-start.10 = (bf16[384,768]{1,0:T(8,128)(2,1)}, bf16[384,768]{1,0:T(8,128)(2,1)S(1)}, u32[]{:S(2)}, u32[]{:S(2)}) collective-permute-start(bf16[384,768]{1,0:T(8,128)(2,1)} %texts.1), channel_id=1, source_target_pairs={{160,321},{161,320},{162,323},{163,322},{164,325},{165,324},{166,3... | collective-permute-start | bytes 1769480 | tf_op jit(solution)/shard_map/ppermute | solution.py:69
  8.8 22.9 %collective-permute-start.6 = (bf16[384,768]{1,0:T(8,128)(2,1)}, bf16[384,768]{1,0:T(8,128)(2,1)S(1)}, u32[]{:S(2)}, u32[]{:S(2)}) collective-permute-start(bf16[384,768]{1,0:T(8,128)(2,1)} %texts.1), channel_id=1, source_target_pairs={{0,64},{1,65},{2,66},{3,67},{4,68},{5,69},{6,70},{7,71},{8,72},{9,... | collective-permute-start | bytes 1769480 | tf_op jit(solution)/shard_map/ppermute | solution.py:69
  14.7 1.1 %copy-start = (bf16[384,768]{1,0:T(8,128)(2,1)S(1)}, bf16[384,768]{1,0:T(8,128)(2,1)}, u32[]{:S(2)}) copy-start(bf16[384,768]{1,0:T(8,128)(2,1)} %images.1) | copy-start | bytes 1769476
  16.1 1.0 %copy-start.2 = (bf16[2,384,768]{2,1,0:T(8,128)(2,1)}, bf16[2,384,768]{2,1,0:T(8,128)(2,1)S(1)}, u32[]{:S(2)}) copy-start(bf16[2,384,768]{2,1,0:T(8,128)(2,1)S(1)} %shard_map.59.mine_ref) | copy-start | bytes 3538948
  17.1 9.7 %collective-permute-start.1 = (bf16[2,384,768]{2,1,0:T(8,128)(2,1)S(1)}, bf16[2,384,768]{2,1,0:T(8,128)(2,1)}, u32[]{:S(2)}, u32[]{:S(2)}) collective-permute-start(bf16[2,384,768]{2,1,0:T(8,128)(2,1)S(1)} %param.1), channel_id=1, source_target_pairs={{0,32},{1,33},{2,34},{3,35},{4,36},{5,37},{6,38},{7,39},{8,40},{9,... | collective-permute-start | bytes 3538952 | tf_op jit(solution)/shard_map/cond/branch_1_fun/ppermute | solution.py:69
  26.9 27.4 %copy-start.3 = (bf16[2,384,768]{2,1,0:T(8,128)(2,1)S(1)}, bf16[2,384,768]{2,1,0:T(8,128)(2,1)}, u32[]{:S(2)}) copy-start(bf16[2,384,768]{2,1,0:T(8,128)(2,1)} %copy-done.2) | copy-start | bytes 3538948
  26.9 27.4 %copy-start.5 = (bf16[384,768]{1,0:T(8,128)(2,1)S(1)}, bf16[384,768]{1,0:T(8,128)(2,1)}, u32[]{:S(2)}) copy-start(bf16[384,768]{1,0:T(8,128)(2,1)} %texts.1) | copy-start | bytes 1769476
  38.7 19.8 %copy-start.6 = (bf16[384,768]{1,0:T(8,128)(2,1)}, bf16[384,768]{1,0:T(8,128)(2,1)S(1)}, u32[]{:S(2)}) copy-start(bf16[384,768]{1,0:T(8,128)(2,1)S(1)} %get-tuple-element.127.hat_ref) | copy-start | bytes 1769476
  38.7 19.8 %copy-start.7 = (bf16[384,768]{1,0:T(8,128)(2,1)}, bf16[384,768]{1,0:T(8,128)(2,1)S(1)}, u32[]{:S(2)}) copy-start(bf16[384,768]{1,0:T(8,128)(2,1)S(1)} %get-tuple-element.128.mine_slopes_ref) | copy-start | bytes 1769476
  38.7 19.8 %collective-permute-start.12 = (bf16[384,768]{1,0:T(8,128)(2,1)S(1)}, bf16[384,768]{1,0:T(8,128)(2,1)S(1)}, u32[]{:S(2)}, u32[]{:S(2)}) collective-permute-start(bf16[384,768]{1,0:T(8,128)(2,1)S(1)} %get-tuple-element.133), channel_id=1, source_target_pairs={{32,64},{33,65},{34,66},{35,67},{36,68},{37,69},{38,70},{39,71},{4... | collective-permute-start | bytes 1769480 | tf_op jit(solution)/shard_map/ppermute | solution.py:69
  48.5 29.8 %collective-permute-start.11 = (bf16[384,768]{1,0:T(8,128)(2,1)}, bf16[384,768]{1,0:T(8,128)(2,1)}, u32[]{:S(2)}, u32[]{:S(2)}) collective-permute-start(bf16[384,768]{1,0:T(8,128)(2,1)} %get-tuple-element.126), channel_id=1, source_target_pairs={{0,449},{1,448},{2,451},{3,450},{4,453},{5,452},{6,455},{7,454},{8... | collective-permute-start | bytes 1769480 | tf_op jit(solution)/shard_map/ppermute | solution.py:69
  51.4 27.0 %collective-permute-start.13 = (bf16[384,768]{1,0:T(8,128)(2,1)S(1)}, bf16[384,768]{1,0:T(8,128)(2,1)}, u32[]{:S(2)}, u32[]{:S(2)}) collective-permute-start(bf16[384,768]{1,0:T(8,128)(2,1)S(1)} %get-tuple-element.135), channel_id=1, source_target_pairs={{32,64},{33,65},{34,66},{35,67},{36,68},{37,69},{38,70},{39,71},{4... | collective-permute-start | bytes 1769480 | tf_op jit(solution)/shard_map/ppermute | solution.py:69
  53.6 32.3 %collective-permute-start.14 = (bf16[384,768]{1,0:T(8,128)(2,1)S(1)}, bf16[384,768]{1,0:T(8,128)(2,1)S(1)}, u32[]{:S(2)}, u32[]{:S(2)}) collective-permute-start(bf16[384,768]{1,0:T(8,128)(2,1)S(1)} %get-tuple-element.138), channel_id=1, source_target_pairs={{64,417},{65,416},{66,419},{67,418},{68,421},{69,420},{70,423},{71... | collective-permute-start | bytes 1769480 | tf_op jit(solution)/shard_map/ppermute | solution.py:69
  58.5 19.9 %copy-start.4 = (bf16[2,384,768]{2,1,0:T(8,128)(2,1)S(1)}, bf16[2,384,768]{2,1,0:T(8,128)(2,1)}, u32[]{:S(2)}) copy-start(bf16[2,384,768]{2,1,0:T(8,128)(2,1)} %copy-done.2) | copy-start | bytes 3538948
  58.5 10.7 %collective-permute-start.3 = (bf16[2,384,768]{2,1,0:T(8,128)(2,1)S(1)}, bf16[2,384,768]{2,1,0:T(8,128)(2,1)}, u32[]{:S(2)}, u32[]{:S(2)}) collective-permute-start(bf16[2,384,768]{2,1,0:T(8,128)(2,1)S(1)} %get-tuple-element.73), channel_id=1, source_target_pairs={{0,32},{1,33},{2,34},{3,35},{4,36},{5,37},{6,38},{7,39},{8,40},{9,... | collective-permute-start | bytes 3538952 | tf_op jit(solution)/shard_map/cond/branch_1_fun/ppermute | solution.py:69
  71.3 20.7 %collective-permute-start.15 = (bf16[384,768]{1,0:T(8,128)(2,1)}, bf16[384,768]{1,0:T(8,128)(2,1)S(1)}, u32[]{:S(2)}, u32[]{:S(2)}) collective-permute-start(bf16[384,768]{1,0:T(8,128)(2,1)} %get-tuple-element.141), channel_id=1, source_target_pairs={{0,1},{1,0},{2,3},{3,2},{4,5},{5,4},{6,7},{7,6},{8,9},{9,8},{10,11... | collective-permute-start | bytes 1769480 | tf_op jit(solution)/shard_map/ppermute | solution.py:69
  78.6 7.2 %collective-permute-start.5 = (bf16[384,768]{1,0:T(8,128)(2,1)}, bf16[384,768]{1,0:T(8,128)(2,1)}, u32[]{:S(2)}, u32[]{:S(2)}) collective-permute-start(bf16[384,768]{1,0:T(8,128)(2,1)} %get-tuple-element.91), channel_id=1, source_target_pairs={{224,481},{225,480},{226,483},{227,482},{228,485},{229,484},{230,4... | collective-permute-start | bytes 1769480 | tf_op jit(solution)/shard_map/cond/branch_1_fun/ppermute | solution.py:69
  85.8 6.1 %copy-start.1 = (bf16[384,768]{1,0:T(8,128)(2,1)S(1)}, bf16[384,768]{1,0:T(8,128)(2,1)}, u32[]{:S(2)}) copy-start(bf16[384,768]{1,0:T(8,128)(2,1)} %images.1) | copy-start | bytes 1769476

commit v7 on v6

--- a/solution.py
+++ b/solution.py
@@ -115,21 +115,25 @@
     role_out[1] = role[1]
 
 
+def near_hat_kernel(role, text_ref, role_out, hat_ref):
+    pass_on(role, role_out)
+    hat_ref[...] = hat(text_ref[...])
+
+
 def hats_kernel(image_ref, partner_ref, hats_ref):
     hats_ref[0] = hat(image_ref[...])
     hats_ref[1] = hat(partner_ref[...])
 
 
 def near_kernel(
-    role, scale_ref, bias_ref, text_ref, mine_ref, theirs_ref, guest_ref, guest_partner_ref, far_ref,
-    role_out, grad_ref, hat_ref, mine_slopes_ref, theirs_slopes_ref, back_ref, back_partner_ref, far_grad_ref,
+    role, scale_ref, bias_ref, hat_ref, mine_ref, theirs_ref, guest_ref, guest_partner_ref, far_ref,
+    role_out, grad_ref, mine_slopes_ref, theirs_slopes_ref, back_ref, back_partner_ref, far_grad_ref,
     total, guests_ref,
 ):
     pass_on(role, role_out)
     scale, bias = scale_ref[0], bias_ref[0]
     rows, width = hat_ref.shape
-    near_hat = hat(text_ref[...])
-    hat_ref[...] = near_hat
+    near_hat = hat_ref[...]
     mine, theirs = rows_of(mine_ref), rows_of(theirs_ref)
     mine_slopes = slopes_of(near_hat, mine, scale, bias)
     mine_slopes_ref[...] = mine_slopes
@@ -273,11 +277,13 @@
     theirs = together(lambda values: move(values, other_core), mine)
     role_type = jax.ShapeDtypeStruct((2,), jnp.int32)
     scalars = (role, logit_scale, logit_bias)
+    role, near_hat = call(near_hat_kernel, [role_type, half], role, near, scalars=1, scalar_outs=1)
+    scalars = (role, logit_scale, logit_bias)
     slopes_pair = bf16((rows, 2 * rows))
-    role, near_grad, near_hat, mine_slopes, theirs_slopes, back, back_partner, far_grad = call(
+    role, near_grad, mine_slopes, theirs_slopes, back, back_partner, far_grad = call(
         near_kernel,
-        [role_type, half, half, slopes_pair, slopes_pair, half, half, half],
-        *scalars, near, mine, theirs, guest, guest_partner, far,
+        [role_type, half, slopes_pair, slopes_pair, half, half, half],
+        *scalars, near_hat, mine, theirs, guest, guest_partner, far,
         scratch=[pltpu.VMEM((rows, width), jnp.float32), pltpu.VMEM((2, rows, width), jnp.bfloat16)],
         mib=24,
         scalar_outs=1,

time: 94.6 us -> 93.8 us (level)
  the two profiles are of different devices: /device:TPU:1 before, /device:TPU:58 now
where the time goes in v7:
time: 93.8 us; the launch traced here: 93.2 us
  starting transfers between devices  40.2 us (43%)
  Pallas kernels  27.4 us (29%)
  waiting for transfers between devices  21 us (22%)
  between operations  2.17 us (2%)
  local copies, waits for them, and re-layouts  2.1 us (2%)
    ppermute x13, starting transfers between devices, move(): return lax.ppermute(values, AXES, sorted(pairs))  40.2 us
    pallas_call x7, Pallas kernels, call(): pl.pallas_call(kernel, in_specs=[SMEM] * scalars + [WHOLE] * (len(operand...  25.3 us
    ppermute x13, waiting for transfers between devices, move(): return lax.ppermute(values, AXES, sorted(pairs))  21 us
    pallas_call x1, Pallas kernels, sum_with_cross(): pl.pallas_call(kernel, grid=(1,), in_specs=specs, out_specs=pl.BlockSpec(...  2.12 us
    unnamed x14, local copies, waits for them, and re-layouts  2.1 us
  transfers between devices with their start and end apart: 13, of which 6 were waited for; matrix products, arithmetic and copies ran while one was open for 0% of the time, Pallas kernels for 20%

profile of v7, /device:TPU:58, one launch (start us, length us, event | category | flops | bytes accessed | tf_op | source)
XLA Modules:
  0.0 93.2 jit_solution(16792725189463838603)
XLA Ops:
  0.6 4.3 %collective-permute-start.7 = (bf16[384,768]{1,0:T(8,128)(2,1)}, bf16[384,768]{1,0:T(8,128)(2,1)S(1)}, u32[]{:S(2)}, u32[]{:S(2)}) collective-permute-start(bf16[384,768]{1,0:T(8,128)(2,1)} %images.1), channel_id=1, source_target_pairs={{0,1},{1,0},{2,3},{3,2},{4,5},{5,4},{6,7},{7,6},{8,9},{9,8},{10,11... | collective-permute-start | bytes 1769480 | tf_op jit(solution)/shard_map/ppermute | solution.py:69
  4.9 3.4 %collective-permute-start.6 = (bf16[384,768]{1,0:T(8,128)(2,1)}, bf16[384,768]{1,0:T(8,128)(2,1)S(1)}, u32[]{:S(2)}, u32[]{:S(2)}) collective-permute-start(bf16[384,768]{1,0:T(8,128)(2,1)} %texts.1), channel_id=1, source_target_pairs={{0,64},{1,65},{2,66},{3,67},{4,68},{5,69},{6,70},{7,71},{8,72},{9,... | collective-permute-start | bytes 1769480 | tf_op jit(solution)/shard_map/ppermute | solution.py:69
  8.3 1.9 %collective-permute-start.8 = (bf16[384,768]{1,0:T(8,128)(2,1)}, bf16[384,768]{1,0:T(8,128)(2,1)S(1)}, u32[]{:S(2)}, u32[]{:S(2)}) collective-permute-start(bf16[384,768]{1,0:T(8,128)(2,1)} %images.1), channel_id=1, source_target_pairs={{0,64},{1,65},{2,66},{3,67},{4,68},{5,69},{6,70},{7,71},{8,72},{9,... | collective-permute-start | bytes 1769480 | tf_op jit(solution)/shard_map/ppermute | solution.py:69
  10.3 1.9 %collective-permute-start.9 = (bf16[384,768]{1,0:T(8,128)(2,1)}, bf16[384,768]{1,0:T(8,128)(2,1)S(1)}, u32[]{:S(2)}, u32[]{:S(2)}) collective-permute-start(bf16[384,768]{1,0:T(8,128)(2,1)} %images.1), channel_id=1, source_target_pairs={{0,65},{1,64},{2,67},{3,66},{4,69},{5,68},{6,71},{7,70},{8,73},{9,... | collective-permute-start | bytes 1769480 | tf_op jit(solution)/shard_map/ppermute | solution.py:69
  14.9 3.5 %collective-permute-done.7.partner_ref = bf16[384,768]{1,0:T(8,128)(2,1)S(1)} collective-permute-done((bf16[384,768]{1,0:T(8,128)(2,1)}, bf16[384,768]{1,0:T(8,128)(2,1)S(1)}, u32[]{:S(2)}, u32[]{:S(2)}) %collective-permute-start.7) | collective-permute-done | bytes 589856 | tf_op jit(solution)/shard_map/ppermute | solution.py:69
  20.9 4.9 %conditional.3 = (bf16[2,384,768]{2,1,0:T(8,128)(2,1)}) conditional(s32[]{:T(128)} %bitcast.2, bf16[2,384,768]{2,1,0:T(8,128)(2,1)S(1)} %shard_map.60.mine_ref, bf16[2,384,768]{2,1,0:T(8,128)(2,1)S(1)} %shard_map.60.mine_ref), branch_computations={%region_0.1_spmd, %region_1.2_spmd} | conditional | bytes 4718640 | solution.py:269
  22.8 2.9 %collective-permute-done.1 = bf16[2,384,768]{2,1,0:T(8,128)(2,1)} collective-permute-done((bf16[2,384,768]{2,1,0:T(8,128)(2,1)S(1)}, bf16[2,384,768]{2,1,0:T(8,128)(2,1)}, u32[]{:S(2)}, u32[]{:S(2)}) %collective-permute-start.1) | collective-permute-done | bytes 1179680 | tf_op jit(solution)/shard_map/cond/branch_1_fun/ppermute | solution.py:69
  25.8 2.4 %collective-permute-done.6.text_ref = bf16[384,768]{1,0:T(8,128)(2,1)S(1)} collective-permute-done((bf16[384,768]{1,0:T(8,128)(2,1)}, bf16[384,768]{1,0:T(8,128)(2,1)S(1)}, u32[]{:S(2)}, u32[]{:S(2)}) %collective-permute-start.6) | collective-permute-done | bytes 589856 | tf_op jit(solution)/shard_map/ppermute | solution.py:69
  29.3 5.2 %collective-permute-done.8.guest_ref = bf16[384,768]{1,0:T(8,128)(2,1)S(1)} collective-permute-done((bf16[384,768]{1,0:T(8,128)(2,1)}, bf16[384,768]{1,0:T(8,128)(2,1)S(1)}, u32[]{:S(2)}, u32[]{:S(2)}) %collective-permute-start.8) | collective-permute-done | bytes 589856 | tf_op jit(solution)/shard_map/ppermute | solution.py:69
  34.5 7.2 %shard_map.61 = (s32[2]{0:T(128)S(1)}, bf16[384,768]{1,0:T(8,128)(2,1)}, bf16[384,768]{1,0:T(8,128)(2,1)S(1)}, bf16[384,768]{1,0:T(8,128)(2,1)S(1)}, bf16[384,76...) custom-call(s32[2]{0:T(128)S(1)} %get-tuple-element.126.role, f32[1]{0:T(128)S(6)} %copy.18.scale_ref, ...), custom_call_target="tpu_custom_call" | custom-call | tf_op jit(solution)/shard_map/pallas_call | solution.py:246
  43.7 1.9 %collective-permute-start.11 = (bf16[384,768]{1,0:T(8,128)(2,1)}, bf16[384,768]{1,0:T(8,128)(2,1)}, u32[]{:S(2)}, u32[]{:S(2)}) collective-permute-start(bf16[384,768]{1,0:T(8,128)(2,1)} %get-tuple-element.129), channel_id=1, source_target_pairs={{0,449},{1,448},{2,451},{3,450},{4,453},{5,452},{6,455},{7,454},{8... | collective-permute-start | bytes 1769480 | tf_op jit(solution)/shard_map/ppermute | solution.py:69
  45.6 11.4 %collective-permute-start.13 = (bf16[384,768]{1,0:T(8,128)(2,1)S(1)}, bf16[384,768]{1,0:T(8,128)(2,1)}, u32[]{:S(2)}, u32[]{:S(2)}) collective-permute-start(bf16[384,768]{1,0:T(8,128)(2,1)S(1)} %get-tuple-element.137), channel_id=1, source_target_pairs={{32,64},{33,65},{34,66},{35,67},{36,68},{37,69},{38,70},{39,71},{4... | collective-permute-start | bytes 1769480 | tf_op jit(solution)/shard_map/ppermute | solution.py:69
  57.0 4.2 %collective-permute-start.14 = (bf16[384,768]{1,0:T(8,128)(2,1)S(1)}, bf16[384,768]{1,0:T(8,128)(2,1)S(1)}, u32[]{:S(2)}, u32[]{:S(2)}) collective-permute-start(bf16[384,768]{1,0:T(8,128)(2,1)S(1)} %get-tuple-element.140), channel_id=1, source_target_pairs={{64,417},{65,416},{66,419},{67,418},{68,421},{69,420},{70,423},{71... | collective-permute-start | bytes 1769480 | tf_op jit(solution)/shard_map/ppermute | solution.py:69
  61.2 5.3 %shard_map.62 = (bf16[2,384,768]{2,1,0:T(8,128)(2,1)S(1)}, f32[384,768]{1,0:T(8,128)S(1)}, bf16[384,1152]{1,0:T(8,128)(2,1)}) custom-call(s32[2]{0:T(128)S(1)} %get-tuple-element.128.role, f32[1]{0:T(128)S(6)} %copy.18.scale_ref, f32[1]{0:T(128)S(6)} %copy.19.bias_ref, bf16[384,768]{1,0:T(8,128)(2,1)S(1)} %copy-done.4, bf16[2,384,768]{2,1,0:T(8,128)(2,1)S(1)} %copy-done.3, ...), custom_call_target="tpu_custom_call" | custom-call | tf_op jit(solution)/shard_map/pallas_call | solution.py:246
  66.6 7.1 %conditional.4 = (bf16[2,384,768]{2,1,0:T(8,128)(2,1)}, bf16[384,768]{1,0:T(8,128)(2,1)}) conditional(s32[]{:T(128)} %bitcast.2, (bf16[2,384,768]{2,1,0:T(8,128)(2,1)S(1)}, s32[2]{0:T(128)S(1)}, f32[384,768]{1,0:T(8,128)S(1)}, bf16[384,768]{1,0:T(8,128)(2,1)S(1)}) %tuple.30, (bf16[2,384,768]{2,1,0:T(8,128)(2,1)S(1)}, s32[2]{0:T(128)S(1)}, ...), branch_computations={%region_2.3_spmd, %region_3.4_spmd} | conditional | bytes 4718648 | solution.py:269
  66.6 2.1 %collective-permute-start.3 = (bf16[2,384,768]{2,1,0:T(8,128)(2,1)S(1)}, bf16[2,384,768]{2,1,0:T(8,128)(2,1)}, u32[]{:S(2)}, u32[]{:S(2)}) collective-permute-start(bf16[2,384,768]{2,1,0:T(8,128)(2,1)S(1)} %get-tuple-element.73), channel_id=1, source_target_pairs={{0,32},{1,33},{2,34},{3,35},{4,36},{5,37},{6,38},{7,39},{8,40},{9,... | collective-permute-start | bytes 3538952 | tf_op jit(solution)/shard_map/cond/branch_1_fun/ppermute | solution.py:69
  68.6 2.9 %collective-permute-done.3.cross_ref = bf16[2,384,768]{2,1,0:T(8,128)(2,1)} collective-permute-done((bf16[2,384,768]{2,1,0:T(8,128)(2,1)S(1)}, bf16[2,384,768]{2,1,0:T(8,128)(2,1)}, u32[]{:S(2)}, u32[]{:S(2)}) %collective-permute-start.3) | collective-permute-done | bytes 1179680 | tf_op jit(solution)/shard_map/cond/branch_1_fun/ppermute | solution.py:69
  71.6 2.1 %branch_1_fun.2 = bf16[384,768]{1,0:T(8,128)(2,1)} custom-call(s32[2]{0:T(128)S(1)} %get-tuple-element.74.role, f32[384,768]{1,0:T(8,128)S(1)} %get-tuple-element.75.sum_ref, bf16[2,384,768]{2,1,0:T(8,128)(2,1)} %collective-permute-done.3.cross_ref, bf16[384,768]{1,0:T(8,128)(2,1)S(1)} %get-tuple-element.76.back_ref), custom_call_target="tpu_custom_call" | custom-call | tf_op jit(solution)/shard_map/cond/branch_1_fun/pallas_call | solution.py:311
  73.7 2.4 %collective-permute-start.15 = (bf16[384,768]{1,0:T(8,128)(2,1)}, bf16[384,768]{1,0:T(8,128)(2,1)S(1)}, u32[]{:S(2)}, u32[]{:S(2)}) collective-permute-start(bf16[384,768]{1,0:T(8,128)(2,1)} %get-tuple-element.143), channel_id=1, source_target_pairs={{0,1},{1,0},{2,3},{3,2},{4,5},{5,4},{6,7},{7,6},{8,9},{9,8},{10,11... | collective-permute-start | bytes 1769480 | tf_op jit(solution)/shard_map/ppermute | solution.py:69
  76.2 8.1 %conditional.5 = (bf16[384,768]{1,0:T(8,128)(2,1)}, f32[384,768]{1,0:T(8,128)S(1)}, f32[384,768]{1,0:T(8,128)S(1)}) conditional(s32[]{:T(128)} %bitcast.2, (bf16[384,768]{1,0:T(8,128)(2,1)}, s32[2]{0:T(128)S(1)}, f32[1]{0:T(128)}, f32[1]{0:T(128)}, bf16[384,768]{1,0:T(8,128)(2,1)S(1)}, /*index=5*/bf16[2,384,768]{2,1,0:T(8,128)(2,1)}, ...), branch_computations={%region_4.5_spmd, %region_5.6_spmd} | conditional | bytes 2359360 | solution.py:269
  77.9 6.3 %branch_1_fun.3 = (f32[384,768]{1,0:T(8,128)S(1)}, f32[384,768]{1,0:T(8,128)S(1)}) custom-call(s32[2]{0:T(128)S(1)} %get-tuple-element.92.role, f32[1]{0:T(128)} %get-tuple-element.93.scale_ref, f32[1]{0:T(128)} %get-tuple-element.94.bias_ref, bf16[384,768]{1,0:T(8,128)(2,1)S(1)} %get-tuple-element.95.text_ref, ...), custom_call_target="tpu_custom_call" | custom-call | tf_op jit(solution)/shard_map/cond/branch_1_fun/pallas_call | solution.py:246
  84.3 2.9 %shard_map.63 = (s32[2]{0:T(128)S(1)}, f32[384,768]{1,0:T(8,128)}) custom-call(s32[2]{0:T(128)S(1)} %get-tuple-element.128.role, bf16[384,768]{1,0:T(8,128)(2,1)S(1)} %copy-done.5, f32[384,768]{1,0:T(8,128)S(1)} %get-tuple-element.138.text_sum, bf16[384,768]{1,0:T(8,128)(2,1)} %collective-permute-done.11.near_back, ...), custom_call_target="tpu_custom_call" | custom-call | tf_op jit(solution)/shard_map/pallas_call | solution.py:246
  87.2 4.0 %collective-permute-done.15.from_partner = bf16[384,768]{1,0:T(8,128)(2,1)S(1)} collective-permute-done((bf16[384,768]{1,0:T(8,128)(2,1)}, bf16[384,768]{1,0:T(8,128)(2,1)S(1)}, u32[]{:S(2)}, u32[]{:S(2)}) %collective-permute-start.15) | collective-permute-done | bytes 589856 | tf_op jit(solution)/shard_map/ppermute | solution.py:69
  91.2 2.0 %shard_map.64 = f32[384,768]{1,0:T(8,128)} custom-call(s32[2]{0:T(128)S(1)} %get-tuple-element.141.role, bf16[384,768]{1,0:T(8,128)(2,1)S(1)} %copy-done.1, f32[384,768]{1,0:T(8,128)S(1)} %get-tuple-element.142.image_sum, bf16[384,768]{1,0:T(8,128)(2,1)S(1)} %collective-permute-done.15.from_partner), custom_call_target="tpu_custom_call" | custom-call | tf_op jit(solution)/shard_map/pallas_call | solution.py:246
  (28 shorter events, 10.3 us)
Async XLA Ops:
  0.6 17.8 %collective-permute-start.7 = (bf16[384,768]{1,0:T(8,128)(2,1)}, bf16[384,768]{1,0:T(8,128)(2,1)S(1)}, u32[]{:S(2)}, u32[]{:S(2)}) collective-permute-start(bf16[384,768]{1,0:T(8,128)(2,1)} %images.1), channel_id=1, source_target_pairs={{0,1},{1,0},{2,3},{3,2},{4,5},{5,4},{6,7},{7,6},{8,9},{9,8},{10,11... | collective-permute-start | bytes 1769480 | tf_op jit(solution)/shard_map/ppermute | solution.py:69
  4.9 23.2 %collective-permute-start.6 = (bf16[384,768]{1,0:T(8,128)(2,1)}, bf16[384,768]{1,0:T(8,128)(2,1)S(1)}, u32[]{:S(2)}, u32[]{:S(2)}) collective-permute-start(bf16[384,768]{1,0:T(8,128)(2,1)} %texts.1), channel_id=1, source_target_pairs={{0,64},{1,65},{2,66},{3,67},{4,68},{5,69},{6,70},{7,71},{8,72},{9,... | collective-permute-start | bytes 1769480 | tf_op jit(solution)/shard_map/ppermute | solution.py:69
  8.3 26.1 %collective-permute-start.8 = (bf16[384,768]{1,0:T(8,128)(2,1)}, bf16[384,768]{1,0:T(8,128)(2,1)S(1)}, u32[]{:S(2)}, u32[]{:S(2)}) collective-permute-start(bf16[384,768]{1,0:T(8,128)(2,1)} %images.1), channel_id=1, source_target_pairs={{0,64},{1,65},{2,66},{3,67},{4,68},{5,69},{6,70},{7,71},{8,72},{9,... | collective-permute-start | bytes 1769480 | tf_op jit(solution)/shard_map/ppermute | solution.py:69
  10.3 24.2 %collective-permute-start.9 = (bf16[384,768]{1,0:T(8,128)(2,1)}, bf16[384,768]{1,0:T(8,128)(2,1)S(1)}, u32[]{:S(2)}, u32[]{:S(2)}) collective-permute-start(bf16[384,768]{1,0:T(8,128)(2,1)} %images.1), channel_id=1, source_target_pairs={{0,65},{1,64},{2,67},{3,66},{4,69},{5,68},{6,71},{7,70},{8,73},{9,... | collective-permute-start | bytes 1769480 | tf_op jit(solution)/shard_map/ppermute | solution.py:69
  12.2 22.3 %collective-permute-start.10 = (bf16[384,768]{1,0:T(8,128)(2,1)}, bf16[384,768]{1,0:T(8,128)(2,1)S(1)}, u32[]{:S(2)}, u32[]{:S(2)}) collective-permute-start(bf16[384,768]{1,0:T(8,128)(2,1)} %texts.1), channel_id=1, source_target_pairs={{160,321},{161,320},{162,323},{163,322},{164,325},{165,324},{166,3... | collective-permute-start | bytes 1769480 | tf_op jit(solution)/shard_map/ppermute | solution.py:69
  18.4 1.1 %copy-start = (bf16[384,768]{1,0:T(8,128)(2,1)S(1)}, bf16[384,768]{1,0:T(8,128)(2,1)}, u32[]{:S(2)}) copy-start(bf16[384,768]{1,0:T(8,128)(2,1)} %images.1) | copy-start | bytes 1769476
  19.9 1.0 %copy-start.2 = (bf16[2,384,768]{2,1,0:T(8,128)(2,1)}, bf16[2,384,768]{2,1,0:T(8,128)(2,1)S(1)}, u32[]{:S(2)}) copy-start(bf16[2,384,768]{2,1,0:T(8,128)(2,1)S(1)} %shard_map.60.mine_ref) | copy-start | bytes 3538948
  20.9 4.9 %collective-permute-start.1 = (bf16[2,384,768]{2,1,0:T(8,128)(2,1)S(1)}, bf16[2,384,768]{2,1,0:T(8,128)(2,1)}, u32[]{:S(2)}, u32[]{:S(2)}) collective-permute-start(bf16[2,384,768]{2,1,0:T(8,128)(2,1)S(1)} %param.1), channel_id=1, source_target_pairs={{0,32},{1,33},{2,34},{3,35},{4,36},{5,37},{6,38},{7,39},{8,40},{9,... | collective-permute-start | bytes 3538952 | tf_op jit(solution)/shard_map/cond/branch_1_fun/ppermute | solution.py:69
  34.5 26.7 %copy-start.3 = (bf16[2,384,768]{2,1,0:T(8,128)(2,1)S(1)}, bf16[2,384,768]{2,1,0:T(8,128)(2,1)}, u32[]{:S(2)}) copy-start(bf16[2,384,768]{2,1,0:T(8,128)(2,1)} %copy-done.2) | copy-start | bytes 3538948
  34.5 26.7 %copy-start.4 = (bf16[384,768]{1,0:T(8,128)(2,1)S(1)}, bf16[384,768]{1,0:T(8,128)(2,1)}, u32[]{:S(2)}) copy-start(bf16[384,768]{1,0:T(8,128)(2,1)} %texts.1) | copy-start | bytes 1769476
  41.7 24.8 %copy-start.6 = (bf16[384,768]{1,0:T(8,128)(2,1)}, bf16[384,768]{1,0:T(8,128)(2,1)S(1)}, u32[]{:S(2)}) copy-start(bf16[384,768]{1,0:T(8,128)(2,1)S(1)} %get-tuple-element.130.mine_slopes_ref) | copy-start | bytes 1769476
  41.7 24.8 %collective-permute-start.12 = (bf16[384,768]{1,0:T(8,128)(2,1)S(1)}, bf16[384,768]{1,0:T(8,128)(2,1)S(1)}, u32[]{:S(2)}, u32[]{:S(2)}) collective-permute-start(bf16[384,768]{1,0:T(8,128)(2,1)S(1)} %get-tuple-element.135), channel_id=1, source_target_pairs={{32,64},{33,65},{34,66},{35,67},{36,68},{37,69},{38,70},{39,71},{4... | collective-permute-start | bytes 1769480 | tf_op jit(solution)/shard_map/ppermute | solution.py:69
  43.7 32.5 %collective-permute-start.11 = (bf16[384,768]{1,0:T(8,128)(2,1)}, bf16[384,768]{1,0:T(8,128)(2,1)}, u32[]{:S(2)}, u32[]{:S(2)}) collective-permute-start(bf16[384,768]{1,0:T(8,128)(2,1)} %get-tuple-element.129), channel_id=1, source_target_pairs={{0,449},{1,448},{2,451},{3,450},{4,453},{5,452},{6,455},{7,454},{8... | collective-permute-start | bytes 1769480 | tf_op jit(solution)/shard_map/ppermute | solution.py:69
  45.6 30.6 %collective-permute-start.13 = (bf16[384,768]{1,0:T(8,128)(2,1)S(1)}, bf16[384,768]{1,0:T(8,128)(2,1)}, u32[]{:S(2)}, u32[]{:S(2)}) collective-permute-start(bf16[384,768]{1,0:T(8,128)(2,1)S(1)} %get-tuple-element.137), channel_id=1, source_target_pairs={{32,64},{33,65},{34,66},{35,67},{36,68},{37,69},{38,70},{39,71},{4... | collective-permute-start | bytes 1769480 | tf_op jit(solution)/shard_map/ppermute | solution.py:69
  57.0 27.3 %collective-permute-start.14 = (bf16[384,768]{1,0:T(8,128)(2,1)S(1)}, bf16[384,768]{1,0:T(8,128)(2,1)S(1)}, u32[]{:S(2)}, u32[]{:S(2)}) collective-permute-start(bf16[384,768]{1,0:T(8,128)(2,1)S(1)} %get-tuple-element.140), channel_id=1, source_target_pairs={{64,417},{65,416},{66,419},{67,418},{68,421},{69,420},{70,423},{71... | collective-permute-start | bytes 1769480 | tf_op jit(solution)/shard_map/ppermute | solution.py:69
  66.6 9.6 %copy-start.5 = (bf16[384,768]{1,0:T(8,128)(2,1)S(1)}, bf16[384,768]{1,0:T(8,128)(2,1)}, u32[]{:S(2)}) copy-start(bf16[384,768]{1,0:T(8,128)(2,1)} %texts.1) | copy-start | bytes 1769476
  66.6 5.0 %collective-permute-start.3 = (bf16[2,384,768]{2,1,0:T(8,128)(2,1)S(1)}, bf16[2,384,768]{2,1,0:T(8,128)(2,1)}, u32[]{:S(2)}, u32[]{:S(2)}) collective-permute-start(bf16[2,384,768]{2,1,0:T(8,128)(2,1)S(1)} %get-tuple-element.73), channel_id=1, source_target_pairs={{0,32},{1,33},{2,34},{3,35},{4,36},{5,37},{6,38},{7,39},{8,40},{9,... | collective-permute-start | bytes 3538952 | tf_op jit(solution)/shard_map/cond/branch_1_fun/ppermute | solution.py:69
  73.7 17.5 %collective-permute-start.15 = (bf16[384,768]{1,0:T(8,128)(2,1)}, bf16[384,768]{1,0:T(8,128)(2,1)S(1)}, u32[]{:S(2)}, u32[]{:S(2)}) collective-permute-start(bf16[384,768]{1,0:T(8,128)(2,1)} %get-tuple-element.143), channel_id=1, source_target_pairs={{0,1},{1,0},{2,3},{3,2},{4,5},{5,4},{6,7},{7,6},{8,9},{9,8},{10,11... | collective-permute-start | bytes 1769480 | tf_op jit(solution)/shard_map/ppermute | solution.py:69
  76.4 7.8 %collective-permute-start.5 = (bf16[384,768]{1,0:T(8,128)(2,1)}, bf16[384,768]{1,0:T(8,128)(2,1)}, u32[]{:S(2)}, u32[]{:S(2)}) collective-permute-start(bf16[384,768]{1,0:T(8,128)(2,1)} %get-tuple-element.91), channel_id=1, source_target_pairs={{224,481},{225,480},{226,483},{227,482},{228,485},{229,484},{230,4... | collective-permute-start | bytes 1769480 | tf_op jit(solution)/shard_map/cond/branch_1_fun/ppermute | solution.py:69
  84.3 6.9 %copy-start.1 = (bf16[384,768]{1,0:T(8,128)(2,1)S(1)}, bf16[384,768]{1,0:T(8,128)(2,1)}, u32[]{:S(2)}) copy-start(bf16[384,768]{1,0:T(8,128)(2,1)} %images.1) | copy-start | bytes 1769476

commit v8 on v7

--- a/solution.py
+++ b/solution.py
@@ -172,7 +172,8 @@
     text_hat = hat(text_ref[...])
     slopes = slopes_of(text_hat, mine_ref[1], scale, bias)
     slopes_ref[:, :rows] = slopes
-    partner_sum_ref[...] = dot(slopes, text_hat, 0, 0) + dot(mine_slopes_ref[:, rows:], hat_ref[...], 0, 0)
+    total = dot(slopes, text_hat, 0, 0) + dot(mine_slopes_ref[:, rows:], hat_ref[...], 0, 0)
+    partner_sum_ref[...] = total.astype(partner_sum_ref.dtype)
 
     @pl.when(role[0] == 0)
     def _():
@@ -218,7 +219,7 @@
 
 def partner_kernel(role, sum_ref, cross_ref, back_ref, out_ref):
     even = 1.0 - is_odd(role).astype(jnp.float32)
-    total = sum_ref[...] + cross_ref[0].astype(jnp.float32) + even * back_ref[...].astype(jnp.float32)
+    total = sum_ref[...].astype(jnp.float32) + cross_ref[0].astype(jnp.float32) + even * back_ref[...].astype(jnp.float32)
     out_ref[...] = total.astype(out_ref.dtype)
 
 
@@ -295,7 +296,7 @@
     back = move(back, guest_to, True)
     cross, partner_sum, own_slopes = call(
         sent_kernel,
-        [half_pair, full, bf16((rows, 3 * rows))],
+        [half_pair, half, bf16((rows, 3 * rows))],
         *scalars, texts, mine, theirs, near_hat, mine_slopes, theirs_slopes,
     )
 

time: 93.8 us -> 93.8 us (level)
  no operation moved by 1% of the time
where the time goes in v8:
time: 93.8 us; the launch traced here: 93.2 us
  starting transfers between devices  40.2 us (43%)
  Pallas kernels  27.5 us (29%)
  waiting for transfers between devices  21 us (22%)
  between operations  2.17 us (2%)
  local copies, waits for them, and re-layouts  2.1 us (2%)
    ppermute x13, starting transfers between devices, move(): return lax.ppermute(values, AXES, sorted(pairs))  40.2 us
    pallas_call x7, Pallas kernels, call(): pl.pallas_call(kernel, in_specs=[SMEM] * scalars + [WHOLE] * (len(operand...  25.3 us
    ppermute x13, waiting for transfers between devices, move(): return lax.ppermute(values, AXES, sorted(pairs))  21 us
    pallas_call x1, Pallas kernels, sum_with_cross(): pl.pallas_call(kernel, grid=(1,), in_specs=specs, out_specs=pl.BlockSpec(...  2.15 us
    unnamed x14, local copies, waits for them, and re-layouts  2.1 us
  transfers between devices with their start and end apart: 13, of which 6 were waited for; matrix products, arithmetic and copies ran while one was open for 0% of the time, Pallas kernels for 20%

profile of v8, /device:TPU:58, one launch (start us, length us, event | category | flops | bytes accessed | tf_op | source)
XLA Modules:
  0.0 93.2 jit_solution(7812595635186172354)
XLA Ops:
  0.6 4.3 %collective-permute-start.7 = (bf16[384,768]{1,0:T(8,128)(2,1)}, bf16[384,768]{1,0:T(8,128)(2,1)S(1)}, u32[]{:S(2)}, u32[]{:S(2)}) collective-permute-start(bf16[384,768]{1,0:T(8,128)(2,1)} %images.1), channel_id=1, source_target_pairs={{0,1},{1,0},{2,3},{3,2},{4,5},{5,4},{6,7},{7,6},{8,9},{9,8},{10,11... | collective-permute-start | bytes 1769480 | tf_op jit(solution)/shard_map/ppermute | solution.py:69
  4.9 3.4 %collective-permute-start.6 = (bf16[384,768]{1,0:T(8,128)(2,1)}, bf16[384,768]{1,0:T(8,128)(2,1)S(1)}, u32[]{:S(2)}, u32[]{:S(2)}) collective-permute-start(bf16[384,768]{1,0:T(8,128)(2,1)} %texts.1), channel_id=1, source_target_pairs={{0,64},{1,65},{2,66},{3,67},{4,68},{5,69},{6,70},{7,71},{8,72},{9,... | collective-permute-start | bytes 1769480 | tf_op jit(solution)/shard_map/ppermute | solution.py:69
  8.3 1.9 %collective-permute-start.8 = (bf16[384,768]{1,0:T(8,128)(2,1)}, bf16[384,768]{1,0:T(8,128)(2,1)S(1)}, u32[]{:S(2)}, u32[]{:S(2)}) collective-permute-start(bf16[384,768]{1,0:T(8,128)(2,1)} %images.1), channel_id=1, source_target_pairs={{0,64},{1,65},{2,66},{3,67},{4,68},{5,69},{6,70},{7,71},{8,72},{9,... | collective-permute-start | bytes 1769480 | tf_op jit(solution)/shard_map/ppermute | solution.py:69
  10.3 1.9 %collective-permute-start.9 = (bf16[384,768]{1,0:T(8,128)(2,1)}, bf16[384,768]{1,0:T(8,128)(2,1)S(1)}, u32[]{:S(2)}, u32[]{:S(2)}) collective-permute-start(bf16[384,768]{1,0:T(8,128)(2,1)} %images.1), channel_id=1, source_target_pairs={{0,65},{1,64},{2,67},{3,66},{4,69},{5,68},{6,71},{7,70},{8,73},{9,... | collective-permute-start | bytes 1769480 | tf_op jit(solution)/shard_map/ppermute | solution.py:69
  14.9 3.5 %collective-permute-done.7.partner_ref = bf16[384,768]{1,0:T(8,128)(2,1)S(1)} collective-permute-done((bf16[384,768]{1,0:T(8,128)(2,1)}, bf16[384,768]{1,0:T(8,128)(2,1)S(1)}, u32[]{:S(2)}, u32[]{:S(2)}) %collective-permute-start.7) | collective-permute-done | bytes 589856 | tf_op jit(solution)/shard_map/ppermute | solution.py:69
  20.9 4.9 %conditional.3 = (bf16[2,384,768]{2,1,0:T(8,128)(2,1)}) conditional(s32[]{:T(128)} %bitcast.2, bf16[2,384,768]{2,1,0:T(8,128)(2,1)S(1)} %shard_map.60.mine_ref, bf16[2,384,768]{2,1,0:T(8,128)(2,1)S(1)} %shard_map.60.mine_ref), branch_computations={%region_0.1_spmd, %region_1.2_spmd} | conditional | bytes 4718640 | solution.py:270
  22.8 2.9 %collective-permute-done.1 = bf16[2,384,768]{2,1,0:T(8,128)(2,1)} collective-permute-done((bf16[2,384,768]{2,1,0:T(8,128)(2,1)S(1)}, bf16[2,384,768]{2,1,0:T(8,128)(2,1)}, u32[]{:S(2)}, u32[]{:S(2)}) %collective-permute-start.1) | collective-permute-done | bytes 1179680 | tf_op jit(solution)/shard_map/cond/branch_1_fun/ppermute | solution.py:69
  25.8 2.4 %collective-permute-done.6.text_ref = bf16[384,768]{1,0:T(8,128)(2,1)S(1)} collective-permute-done((bf16[384,768]{1,0:T(8,128)(2,1)}, bf16[384,768]{1,0:T(8,128)(2,1)S(1)}, u32[]{:S(2)}, u32[]{:S(2)}) %collective-permute-start.6) | collective-permute-done | bytes 589856 | tf_op jit(solution)/shard_map/ppermute | solution.py:69
  29.3 5.2 %collective-permute-done.8.guest_ref = bf16[384,768]{1,0:T(8,128)(2,1)S(1)} collective-permute-done((bf16[384,768]{1,0:T(8,128)(2,1)}, bf16[384,768]{1,0:T(8,128)(2,1)S(1)}, u32[]{:S(2)}, u32[]{:S(2)}) %collective-permute-start.8) | collective-permute-done | bytes 589856 | tf_op jit(solution)/shard_map/ppermute | solution.py:69
  34.5 7.2 %shard_map.61 = (s32[2]{0:T(128)S(1)}, bf16[384,768]{1,0:T(8,128)(2,1)}, bf16[384,768]{1,0:T(8,128)(2,1)S(1)}, bf16[384,768]{1,0:T(8,128)(2,1)S(1)}, bf16[384,76...) custom-call(s32[2]{0:T(128)S(1)} %get-tuple-element.126.role, f32[1]{0:T(128)S(6)} %copy.18.scale_ref, ...), custom_call_target="tpu_custom_call" | custom-call | tf_op jit(solution)/shard_map/pallas_call | solution.py:247
  43.7 1.9 %collective-permute-start.11 = (bf16[384,768]{1,0:T(8,128)(2,1)}, bf16[384,768]{1,0:T(8,128)(2,1)}, u32[]{:S(2)}, u32[]{:S(2)}) collective-permute-start(bf16[384,768]{1,0:T(8,128)(2,1)} %get-tuple-element.129), channel_id=1, source_target_pairs={{0,449},{1,448},{2,451},{3,450},{4,453},{5,452},{6,455},{7,454},{8... | collective-permute-start | bytes 1769480 | tf_op jit(solution)/shard_map/ppermute | solution.py:69
  45.6 11.4 %collective-permute-start.13 = (bf16[384,768]{1,0:T(8,128)(2,1)S(1)}, bf16[384,768]{1,0:T(8,128)(2,1)}, u32[]{:S(2)}, u32[]{:S(2)}) collective-permute-start(bf16[384,768]{1,0:T(8,128)(2,1)S(1)} %get-tuple-element.137), channel_id=1, source_target_pairs={{32,64},{33,65},{34,66},{35,67},{36,68},{37,69},{38,70},{39,71},{4... | collective-permute-start | bytes 1769480 | tf_op jit(solution)/shard_map/ppermute | solution.py:69
  57.0 4.2 %collective-permute-start.14 = (bf16[384,768]{1,0:T(8,128)(2,1)S(1)}, bf16[384,768]{1,0:T(8,128)(2,1)S(1)}, u32[]{:S(2)}, u32[]{:S(2)}) collective-permute-start(bf16[384,768]{1,0:T(8,128)(2,1)S(1)} %get-tuple-element.140), channel_id=1, source_target_pairs={{64,417},{65,416},{66,419},{67,418},{68,421},{69,420},{70,423},{71... | collective-permute-start | bytes 1769480 | tf_op jit(solution)/shard_map/ppermute | solution.py:69
  61.2 5.3 %shard_map.62 = (bf16[2,384,768]{2,1,0:T(8,128)(2,1)S(1)}, bf16[384,768]{1,0:T(8,128)(2,1)S(1)}, bf16[384,1152]{1,0:T(8,128)(2,1)}) custom-call(s32[2]{0:T(128)S(1)} %get-tuple-element.128.role, f32[1]{0:T(128)S(6)} %copy.18.scale_ref, f32[1]{0:T(128)S(6)} %copy.19.bias_ref, bf16[384,768]{1,0:T(8,128)(2,1)S(1)} %copy-done.4, ...), custom_call_target="tpu_custom_call" | custom-call | tf_op jit(solution)/shard_map/pallas_call | solution.py:247
  66.6 7.2 %conditional.4 = (bf16[2,384,768]{2,1,0:T(8,128)(2,1)}, bf16[384,768]{1,0:T(8,128)(2,1)}) conditional(s32[]{:T(128)} %bitcast.2, (bf16[2,384,768]{2,1,0:T(8,128)(2,1)S(1)}, s32[2]{0:T(128)S(1)}, bf16[384,768]{1,0:T(8,128)(2,1)S(1)}, bf16[384,768]{1,0:T(8,128)(2,1)S(1)}) %tuple.30, (bf16[2,384,768]{2,1,0:T(8,128)(2,1)S(1)}, s32[2]{0:T(128)S(1)}, ...), branch_computations={%region_2.3_spmd, %region_3.4_spmd} | conditional | bytes 4718648 | solution.py:270
  66.6 2.1 %collective-permute-start.3 = (bf16[2,384,768]{2,1,0:T(8,128)(2,1)S(1)}, bf16[2,384,768]{2,1,0:T(8,128)(2,1)}, u32[]{:S(2)}, u32[]{:S(2)}) collective-permute-start(bf16[2,384,768]{2,1,0:T(8,128)(2,1)S(1)} %get-tuple-element.73), channel_id=1, source_target_pairs={{0,32},{1,33},{2,34},{3,35},{4,36},{5,37},{6,38},{7,39},{8,40},{9,... | collective-permute-start | bytes 3538952 | tf_op jit(solution)/shard_map/cond/branch_1_fun/ppermute | solution.py:69
  68.6 2.9 %collective-permute-done.3.cross_ref = bf16[2,384,768]{2,1,0:T(8,128)(2,1)} collective-permute-done((bf16[2,384,768]{2,1,0:T(8,128)(2,1)S(1)}, bf16[2,384,768]{2,1,0:T(8,128)(2,1)}, u32[]{:S(2)}, u32[]{:S(2)}) %collective-permute-start.3) | collective-permute-done | bytes 1179680 | tf_op jit(solution)/shard_map/cond/branch_1_fun/ppermute | solution.py:69
  71.6 2.2 %branch_1_fun.2 = bf16[384,768]{1,0:T(8,128)(2,1)} custom-call(s32[2]{0:T(128)S(1)} %get-tuple-element.74.role, bf16[384,768]{1,0:T(8,128)(2,1)S(1)} %get-tuple-element.75.sum_ref, bf16[2,384,768]{2,1,0:T(8,128)(2,1)} %collective-permute-done.3.cross_ref, bf16[384,768]{1,0:T(8,128)(2,1)S(1)} %get-tuple-element.76.back_ref), custom_call_target="tpu_custom_call" | custom-call | tf_op jit(solution)/shard_map/cond/branch_1_fun/pallas_call | solution.py:312
  73.7 2.4 %collective-permute-start.15 = (bf16[384,768]{1,0:T(8,128)(2,1)}, bf16[384,768]{1,0:T(8,128)(2,1)S(1)}, u32[]{:S(2)}, u32[]{:S(2)}) collective-permute-start(bf16[384,768]{1,0:T(8,128)(2,1)} %get-tuple-element.143), channel_id=1, source_target_pairs={{0,1},{1,0},{2,3},{3,2},{4,5},{5,4},{6,7},{7,6},{8,9},{9,8},{10,11... | collective-permute-start | bytes 1769480 | tf_op jit(solution)/shard_map/ppermute | solution.py:69
  76.2 8.0 %conditional.5 = (bf16[384,768]{1,0:T(8,128)(2,1)}, f32[384,768]{1,0:T(8,128)S(1)}, f32[384,768]{1,0:T(8,128)S(1)}) conditional(s32[]{:T(128)} %bitcast.2, (bf16[384,768]{1,0:T(8,128)(2,1)}, s32[2]{0:T(128)S(1)}, f32[1]{0:T(128)}, f32[1]{0:T(128)}, bf16[384,768]{1,0:T(8,128)(2,1)S(1)}, /*index=5*/bf16[2,384,768]{2,1,0:T(8,128)(2,1)}, ...), branch_computations={%region_4.5_spmd, %region_5.6_spmd} | conditional | bytes 2359360 | solution.py:270
  77.9 6.3 %branch_1_fun.3 = (f32[384,768]{1,0:T(8,128)S(1)}, f32[384,768]{1,0:T(8,128)S(1)}) custom-call(s32[2]{0:T(128)S(1)} %get-tuple-element.92.role, f32[1]{0:T(128)} %get-tuple-element.93.scale_ref, f32[1]{0:T(128)} %get-tuple-element.94.bias_ref, bf16[384,768]{1,0:T(8,128)(2,1)S(1)} %get-tuple-element.95.text_ref, ...), custom_call_target="tpu_custom_call" | custom-call | tf_op jit(solution)/shard_map/cond/branch_1_fun/pallas_call | solution.py:247
  84.3 2.9 %shard_map.63 = (s32[2]{0:T(128)S(1)}, f32[384,768]{1,0:T(8,128)}) custom-call(s32[2]{0:T(128)S(1)} %get-tuple-element.128.role, bf16[384,768]{1,0:T(8,128)(2,1)S(1)} %copy-done.5, f32[384,768]{1,0:T(8,128)S(1)} %get-tuple-element.138.text_sum, bf16[384,768]{1,0:T(8,128)(2,1)} %collective-permute-done.11.near_back, ...), custom_call_target="tpu_custom_call" | custom-call | tf_op jit(solution)/shard_map/pallas_call | solution.py:247
  87.2 4.0 %collective-permute-done.15.from_partner = bf16[384,768]{1,0:T(8,128)(2,1)S(1)} collective-permute-done((bf16[384,768]{1,0:T(8,128)(2,1)}, bf16[384,768]{1,0:T(8,128)(2,1)S(1)}, u32[]{:S(2)}, u32[]{:S(2)}) %collective-permute-start.15) | collective-permute-done | bytes 589856 | tf_op jit(solution)/shard_map/ppermute | solution.py:69
  91.2 2.0 %shard_map.64 = f32[384,768]{1,0:T(8,128)} custom-call(s32[2]{0:T(128)S(1)} %get-tuple-element.141.role, bf16[384,768]{1,0:T(8,128)(2,1)S(1)} %copy-done.1, f32[384,768]{1,0:T(8,128)S(1)} %get-tuple-element.142.image_sum, bf16[384,768]{1,0:T(8,128)(2,1)S(1)} %collective-permute-done.15.from_partner), custom_call_target="tpu_custom_call" | custom-call | tf_op jit(solution)/shard_map/pallas_call | solution.py:247
  (28 shorter events, 10.3 us)
Async XLA Ops:
  0.6 17.8 %collective-permute-start.7 = (bf16[384,768]{1,0:T(8,128)(2,1)}, bf16[384,768]{1,0:T(8,128)(2,1)S(1)}, u32[]{:S(2)}, u32[]{:S(2)}) collective-permute-start(bf16[384,768]{1,0:T(8,128)(2,1)} %images.1), channel_id=1, source_target_pairs={{0,1},{1,0},{2,3},{3,2},{4,5},{5,4},{6,7},{7,6},{8,9},{9,8},{10,11... | collective-permute-start | bytes 1769480 | tf_op jit(solution)/shard_map/ppermute | solution.py:69
  4.9 23.2 %collective-permute-start.6 = (bf16[384,768]{1,0:T(8,128)(2,1)}, bf16[384,768]{1,0:T(8,128)(2,1)S(1)}, u32[]{:S(2)}, u32[]{:S(2)}) collective-permute-start(bf16[384,768]{1,0:T(8,128)(2,1)} %texts.1), channel_id=1, source_target_pairs={{0,64},{1,65},{2,66},{3,67},{4,68},{5,69},{6,70},{7,71},{8,72},{9,... | collective-permute-start | bytes 1769480 | tf_op jit(solution)/shard_map/ppermute | solution.py:69
  8.3 26.1 %collective-permute-start.8 = (bf16[384,768]{1,0:T(8,128)(2,1)}, bf16[384,768]{1,0:T(8,128)(2,1)S(1)}, u32[]{:S(2)}, u32[]{:S(2)}) collective-permute-start(bf16[384,768]{1,0:T(8,128)(2,1)} %images.1), channel_id=1, source_target_pairs={{0,64},{1,65},{2,66},{3,67},{4,68},{5,69},{6,70},{7,71},{8,72},{9,... | collective-permute-start | bytes 1769480 | tf_op jit(solution)/shard_map/ppermute | solution.py:69
  10.3 24.2 %collective-permute-start.9 = (bf16[384,768]{1,0:T(8,128)(2,1)}, bf16[384,768]{1,0:T(8,128)(2,1)S(1)}, u32[]{:S(2)}, u32[]{:S(2)}) collective-permute-start(bf16[384,768]{1,0:T(8,128)(2,1)} %images.1), channel_id=1, source_target_pairs={{0,65},{1,64},{2,67},{3,66},{4,69},{5,68},{6,71},{7,70},{8,73},{9,... | collective-permute-start | bytes 1769480 | tf_op jit(solution)/shard_map/ppermute | solution.py:69
  12.2 22.3 %collective-permute-start.10 = (bf16[384,768]{1,0:T(8,128)(2,1)}, bf16[384,768]{1,0:T(8,128)(2,1)S(1)}, u32[]{:S(2)}, u32[]{:S(2)}) collective-permute-start(bf16[384,768]{1,0:T(8,128)(2,1)} %texts.1), channel_id=1, source_target_pairs={{160,321},{161,320},{162,323},{163,322},{164,325},{165,324},{166,3... | collective-permute-start | bytes 1769480 | tf_op jit(solution)/shard_map/ppermute | solution.py:69
  18.4 1.1 %copy-start = (bf16[384,768]{1,0:T(8,128)(2,1)S(1)}, bf16[384,768]{1,0:T(8,128)(2,1)}, u32[]{:S(2)}) copy-start(bf16[384,768]{1,0:T(8,128)(2,1)} %images.1) | copy-start | bytes 1769476
  19.9 1.0 %copy-start.2 = (bf16[2,384,768]{2,1,0:T(8,128)(2,1)}, bf16[2,384,768]{2,1,0:T(8,128)(2,1)S(1)}, u32[]{:S(2)}) copy-start(bf16[2,384,768]{2,1,0:T(8,128)(2,1)S(1)} %shard_map.60.mine_ref) | copy-start | bytes 3538948
  20.9 4.9 %collective-permute-start.1 = (bf16[2,384,768]{2,1,0:T(8,128)(2,1)S(1)}, bf16[2,384,768]{2,1,0:T(8,128)(2,1)}, u32[]{:S(2)}, u32[]{:S(2)}) collective-permute-start(bf16[2,384,768]{2,1,0:T(8,128)(2,1)S(1)} %param.1), channel_id=1, source_target_pairs={{0,32},{1,33},{2,34},{3,35},{4,36},{5,37},{6,38},{7,39},{8,40},{9,... | collective-permute-start | bytes 3538952 | tf_op jit(solution)/shard_map/cond/branch_1_fun/ppermute | solution.py:69
  34.5 26.7 %copy-start.3 = (bf16[2,384,768]{2,1,0:T(8,128)(2,1)S(1)}, bf16[2,384,768]{2,1,0:T(8,128)(2,1)}, u32[]{:S(2)}) copy-start(bf16[2,384,768]{2,1,0:T(8,128)(2,1)} %copy-done.2) | copy-start | bytes 3538948
  34.5 26.7 %copy-start.4 = (bf16[384,768]{1,0:T(8,128)(2,1)S(1)}, bf16[384,768]{1,0:T(8,128)(2,1)}, u32[]{:S(2)}) copy-start(bf16[384,768]{1,0:T(8,128)(2,1)} %texts.1) | copy-start | bytes 1769476
  41.7 24.8 %copy-start.6 = (bf16[384,768]{1,0:T(8,128)(2,1)}, bf16[384,768]{1,0:T(8,128)(2,1)S(1)}, u32[]{:S(2)}) copy-start(bf16[384,768]{1,0:T(8,128)(2,1)S(1)} %get-tuple-element.130.mine_slopes_ref) | copy-start | bytes 1769476
  41.7 24.8 %collective-permute-start.12 = (bf16[384,768]{1,0:T(8,128)(2,1)S(1)}, bf16[384,768]{1,0:T(8,128)(2,1)S(1)}, u32[]{:S(2)}, u32[]{:S(2)}) collective-permute-start(bf16[384,768]{1,0:T(8,128)(2,1)S(1)} %get-tuple-element.135), channel_id=1, source_target_pairs={{32,64},{33,65},{34,66},{35,67},{36,68},{37,69},{38,70},{39,71},{4... | collective-permute-start | bytes 1769480 | tf_op jit(solution)/shard_map/ppermute | solution.py:69
  43.7 32.5 %collective-permute-start.11 = (bf16[384,768]{1,0:T(8,128)(2,1)}, bf16[384,768]{1,0:T(8,128)(2,1)}, u32[]{:S(2)}, u32[]{:S(2)}) collective-permute-start(bf16[384,768]{1,0:T(8,128)(2,1)} %get-tuple-element.129), channel_id=1, source_target_pairs={{0,449},{1,448},{2,451},{3,450},{4,453},{5,452},{6,455},{7,454},{8... | collective-permute-start | bytes 1769480 | tf_op jit(solution)/shard_map/ppermute | solution.py:69
  45.6 30.6 %collective-permute-start.13 = (bf16[384,768]{1,0:T(8,128)(2,1)S(1)}, bf16[384,768]{1,0:T(8,128)(2,1)}, u32[]{:S(2)}, u32[]{:S(2)}) collective-permute-start(bf16[384,768]{1,0:T(8,128)(2,1)S(1)} %get-tuple-element.137), channel_id=1, source_target_pairs={{32,64},{33,65},{34,66},{35,67},{36,68},{37,69},{38,70},{39,71},{4... | collective-permute-start | bytes 1769480 | tf_op jit(solution)/shard_map/ppermute | solution.py:69
  57.0 27.3 %collective-permute-start.14 = (bf16[384,768]{1,0:T(8,128)(2,1)S(1)}, bf16[384,768]{1,0:T(8,128)(2,1)S(1)}, u32[]{:S(2)}, u32[]{:S(2)}) collective-permute-start(bf16[384,768]{1,0:T(8,128)(2,1)S(1)} %get-tuple-element.140), channel_id=1, source_target_pairs={{64,417},{65,416},{66,419},{67,418},{68,421},{69,420},{70,423},{71... | collective-permute-start | bytes 1769480 | tf_op jit(solution)/shard_map/ppermute | solution.py:69
  66.6 9.7 %copy-start.5 = (bf16[384,768]{1,0:T(8,128)(2,1)S(1)}, bf16[384,768]{1,0:T(8,128)(2,1)}, u32[]{:S(2)}) copy-start(bf16[384,768]{1,0:T(8,128)(2,1)} %texts.1) | copy-start | bytes 1769476
  66.6 5.0 %collective-permute-start.3 = (bf16[2,384,768]{2,1,0:T(8,128)(2,1)S(1)}, bf16[2,384,768]{2,1,0:T(8,128)(2,1)}, u32[]{:S(2)}, u32[]{:S(2)}) collective-permute-start(bf16[2,384,768]{2,1,0:T(8,128)(2,1)S(1)} %get-tuple-element.73), channel_id=1, source_target_pairs={{0,32},{1,33},{2,34},{3,35},{4,36},{5,37},{6,38},{7,39},{8,40},{9,... | collective-permute-start | bytes 3538952 | tf_op jit(solution)/shard_map/cond/branch_1_fun/ppermute | solution.py:69
  73.7 17.5 %collective-permute-start.15 = (bf16[384,768]{1,0:T(8,128)(2,1)}, bf16[384,768]{1,0:T(8,128)(2,1)S(1)}, u32[]{:S(2)}, u32[]{:S(2)}) collective-permute-start(bf16[384,768]{1,0:T(8,128)(2,1)} %get-tuple-element.143), channel_id=1, source_target_pairs={{0,1},{1,0},{2,3},{3,2},{4,5},{5,4},{6,7},{7,6},{8,9},{9,8},{10,11... | collective-permute-start | bytes 1769480 | tf_op jit(solution)/shard_map/ppermute | solution.py:69
  76.4 7.8 %collective-permute-start.5 = (bf16[384,768]{1,0:T(8,128)(2,1)}, bf16[384,768]{1,0:T(8,128)(2,1)}, u32[]{:S(2)}, u32[]{:S(2)}) collective-permute-start(bf16[384,768]{1,0:T(8,128)(2,1)} %get-tuple-element.91), channel_id=1, source_target_pairs={{224,481},{225,480},{226,483},{227,482},{228,485},{229,484},{230,4... | collective-permute-start | bytes 1769480 | tf_op jit(solution)/shard_map/cond/branch_1_fun/ppermute | solution.py:69
  84.3 6.9 %copy-start.1 = (bf16[384,768]{1,0:T(8,128)(2,1)S(1)}, bf16[384,768]{1,0:T(8,128)(2,1)}, u32[]{:S(2)}) copy-start(bf16[384,768]{1,0:T(8,128)(2,1)} %images.1) | copy-start | bytes 1769476
